TPU v7x, 32 devices: a whole 2x2x4 slice. The times are simulated.
32 devices in a mesh: groups: 2 (over x), row: 8 (over z, y), col: 2 (over core).
Axes of the slice: x: 2, y: 2, z: 4, core: 2. Of those that a mesh axis runs over, the one named last changes fastest.
Arguments:
- hamiltonian: float32 [192, 7, 128, 128], P(('groups', 'row'), None, 'col'), parts along dimension 0, may hold values from -2.5 to 2.5, as said below
- bounds: float32 [4], P('groups'), parts along dimension 0, may hold values from 5 to 6
- block_reach: int32 [192], P(('groups', 'row')), parts along dimension 0, may hold values from 2 to 6, as said below
- branch_flags: int32 [2], P('groups'), parts along dimension 0, may hold values from 0 to 1
Outputs:
- density: float32 [192, 7, 128, 128], P(('groups', 'row'), None, 'col'), parts along dimension 0
- occupancy: float32 [2], P('groups'), parts along dimension 0
There are 2 independent parts, one for each index of `groups`. A program takes and returns all parts, laid end to end along the dimension named above; each array names one. Nothing has to cross between parts.
Inputs may be any that keep to these rules, and one draw needn't show every extreme that they name: The diagonal blocks hamiltonian[i, 0] are symmetric; the spectrum of the full symmetric matrix lies between -bounds[0] and bounds[1]. `block_reach`: in every draw some block rows reach 6.
All inputs are finite; a program needn't handle non-finite values.
Results may differ from a plain program's by a relative error of at most 0.005.
Values may be sent and summed in bfloat16 or wider, within the bound.
No kernel may reach another device: no remote copies, remote signals or barrier semaphores. Data moves between devices by JAX's collectives and lax.ppermute only.
A program may use at most 64 MiB of HBM per device.

v0:
```python
import jax
import jax.numpy as jnp
from jax import lax
from jax.sharding import PartitionSpec as P


def with_halo(cells, sides, width):
    for axis, dim in sides:
        count = lax.axis_size(axis)
        ends = count - 1
        head = lax.slice_in_dim(cells, 0, width, axis=dim)
        tail = lax.slice_in_dim(cells, cells.shape[dim] - width, cells.shape[dim], axis=dim)
        cells = jnp.concatenate(
            [
                lax.ppermute(tail, axis, [(i, (i + 1) % count) for i in range(ends)]),
                cells,
                lax.ppermute(head, axis, [((i + 1) % count, i) for i in range(ends)]),
            ],
            axis=dim,
        )
    return cells


def band_square(current, extended, column, band_width):
    row_count = current.shape[0]
    half_rows = current.shape[2]
    skewed = jnp.stack(
        [
            extended[band_width - m : band_width - m + row_count + band_width, m]
            for m in range(band_width + 1)
        ],
        axis=1,
    )
    lower_part = jnp.stack(
        [
            jnp.swapaxes(
                lax.dynamic_slice_in_dim(
                    extended[band_width - k : band_width - k + row_count, k],
                    column * half_rows,
                    half_rows,
                    2,
                ),
                1,
                2,
            )
            for k in range(1, band_width + 1)
        ],
        axis=1,
    )
    left_blocks = jnp.concatenate([current[:, ::-1], lower_part], axis=1)
    products = []
    for d in range(band_width + 1):
        total = jnp.einsum(
            "rmpq,rmqs->rps",
            left_blocks[:, band_width - d : 2 * band_width - d + 1],
            skewed[d : d + row_count],
            preferred_element_type=jnp.float32,
        )
        if d < band_width:
            total = total + jnp.einsum(
                "repq,resq->rps",
                current[:, d + 1 :],
                extended[band_width + d : band_width + d + row_count, 1 : band_width - d + 1],
                preferred_element_type=jnp.float32,
            )
        products.append(total)
    return jnp.stack(products, axis=1)


def per_device(hamiltonian, bounds, block_reach, branch_flags):
    row_count = hamiltonian.shape[0]
    band_width = hamiltonian.shape[1] - 1
    half_rows = hamiltonian.shape[2]
    block_size = hamiltonian.shape[3]
    column = lax.axis_index("col")
    first_row = lax.axis_index("row") * row_count
    total_rows = lax.axis_size("row") * row_count
    row_ids = first_row + jnp.arange(row_count, dtype=jnp.int32)
    offsets = jnp.arange(band_width + 1, dtype=jnp.int32)
    kept_mask = (offsets[None, :] <= block_reach[:, None]) & (
        row_ids[:, None] + offsets[None, :] < total_rows
    )
    diag_mask = (
        jnp.arange(block_size, dtype=jnp.int32)[None, :]
        == column * half_rows + jnp.arange(half_rows, dtype=jnp.int32)[:, None]
    )
    unit_diag = jnp.where((offsets[:, None, None] == 0) & diag_mask[None], 1.0, 0.0).astype(
        jnp.float32
    )
    spectrum_low = -bounds[0]
    spectrum_high = bounds[1]
    start_band = (spectrum_high * unit_diag[None] - hamiltonian) / (spectrum_high - spectrum_low)
    current = jnp.where(kept_mask[:, :, None, None], start_band, 0.0).astype(jnp.bfloat16)
    scale_orbitals = 1.0 / (total_rows * block_size)
    assembled = lax.all_gather(current, "col", axis=2, tiled=True)
    extended = with_halo(assembled, (("row", 0),), band_width)
    square = jnp.where(
        kept_mask[:, :, None, None], band_square(current, extended, column, band_width), 0.0
    )
    previous = current.astype(jnp.float32)
    updated = jnp.where(branch_flags[0] == 1, square, 2.0 * previous - square)
    partial_trace = jnp.sum(jnp.where(diag_mask[None], updated[:, 0], 0.0))
    occupied = [lax.psum(partial_trace, ("row", "col")) * scale_orbitals]
    return (updated, jnp.stack(occupied))


def solution(mesh):
    placed = (
        P(("groups", "row"), None, "col", None),
        P("groups"),
        P(("groups", "row")),
        P("groups"),
    )
    return jax.shard_map(
        per_device,
        mesh=mesh,
        in_specs=placed,
        out_specs=(P(("groups", "row"), None, "col", None), P("groups")),
        check_vma=False,
    )
```

profile of v0, /device:TPU:0, one launch (start us, length us, event | category | flops | bytes accessed | tf_op | source)
XLA Modules:
  0.0 168.7 jit_solution(15513123114985950500)
XLA Ops:
  7.3 1.3 fusion.157
  9.9 0.7 select_multiply_fusion
  10.7 0.7 fusion.151
  11.4 3.3 %select_convert_fusion = bf16[12,7,64,128]{3,2,1,0:T(8,128)(2,1)} fusion(f32[12,7,64,128]{3,2,1,0:T(8,128)} %param.4, f32[]{:T(128)S(6)} %sub.16, f32[7,64,128]{2,1,0:T(8,128)S(1)} %select_multiply_fusion, pred[12,7]{1,0:T(8,128)(4,1)S(1)} %fusion.151), kind=kLoop, calls=%fused_computation.15 | loop fusion | flops 2752512 | bytes 4358232 | tf_op jit(solution)/shard_map/convert_element_type | solution.py:93
  14.7 14.4 %all-gather.2.cloned.1.call-done = bf16[12,7,128,128]{3,2,1,0:T(8,128)(2,1)} async-done(((bf16[12,7,64,128]{3,2,1,0:T(8,128)(2,1)}), bf16[12,7,128,128]{3,2,1,0:T(8,128)(2,1)}) %all-gather.2.cloned.1.call-update) | async-done | bytes 2752528 | tf_op jit(solution)/shard_map/all_gather | solution.py:95
  29.1 3.1 %fusion.156 = (bf16[6,7,128,128]{3,2,1,0:T(8,128)(2,1)S(1)}, bf16[6,7,128,128]{3,2,1,0:T(8,128)(2,1)}) fusion(bf16[12,7,128,128]{3,2,1,0:T(8,128)(2,1)} %all-gather.2.cloned.1.call-done), kind=kLoop, calls=%fused_computation.126 | loop fusion | bytes 5505024 | tf_op jit(solution)/shard_map/slice | solution.py:11
  32.2 4.7 %collective-permute-start = (bf16[6,7,128,128]{3,2,1,0:T(8,128)(2,1)}, bf16[6,7,128,128]{3,2,1,0:T(8,128)(2,1)}, u32[]{:S(2)}, u32[]{:S(2)}) collective-permute-start(bf16[6,7,128,128]{3,2,1,0:T(8,128)(2,1)} %get-tuple-element.12), channel_id=1, source_target_pairs={{0,2},{2,4},{4,6},{6,8},{8,10},{10,12},{12,14},{1,3},{3,5},{5,7},{... | collective-permute-start | bytes 4128776 | tf_op jit(solution)/shard_map/ppermute | solution.py:15
  37.0 1.3 collective-permute-start.1
  38.3 1.2 rev.3
  40.1 3.1 %constant_dynamic-update-slice_fusion.18 = (bf16[12,11,64,128]{3,2,1,0:T(8,128)(2,1)}, bf16[12,13,64,128]{3,2,1,0:T(8,128)(2,1)}, bf16[12,12,64,128]{3,2,1,0:T(8,128)(2,1)}) fusion(bf16[12,7,64,128]{3,2,1,0:T(8,128)(2,1)S(1)} %copy-done), kind=kLoop, calls=%fused_computation.108 | loop fusion | bytes 5505024
  43.2 1.7 %fusion.35 = f32[12,64,128]{2,1,0:T(8,128)} fusion(bf16[12,7,64,128]{3,2,1,0:T(8,128)(2,1)S(1)} %copy-done, bf16[12,7,128,128]{3,2,1,0:T(8,128)(2,1)S(1)} %copy-done.2), kind=kOutput, calls=%fused_computation.37 | convolution fusion | flops 150994944 | bytes 4128768 | tf_op jit(solution)/shard_map/repq,resq->rps/dot_general | solution.py:60
  44.9 50.6 %collective-permute-done = bf16[6,7,128,128]{3,2,1,0:T(8,128)(2,1)} collective-permute-done((bf16[6,7,128,128]{3,2,1,0:T(8,128)(2,1)}, bf16[6,7,128,128]{3,2,1,0:T(8,128)(2,1)}, u32[]{:S(2)}, u32[]{:S(2)}) %collective-permute-start) | collective-permute-done | bytes 1376288 | tf_op jit(solution)/shard_map/ppermute | solution.py:15
  95.6 2.0 %constant_dynamic-update-slice_fusion.10 = (bf16[24,7,128,128]{3,2,1,0:T(8,128)(2,1)S(1)}, bf16[18,7,128,128]{3,2,1,0:T(8,128)(2,1)S(1)}) fusion(bf16[6,7,128,128]{3,2,1,0:T(8,128)(2,1)} %collective-permute-done), kind=kLoop, calls=%fused_computation.100 | loop fusion | bytes 4128768
  97.6 1.9 %constant_dynamic-update-slice_fusion.9 = (bf16[24,7,128,128]{3,2,1,0:T(8,128)(2,1)S(1)}, bf16[18,7,128,128]{3,2,1,0:T(8,128)(2,1)S(1)}, bf16[18,7,128,128]{3,2,1,0:T(8,128)(2,1)S(1)}) fusion(bf16[24,7,128,128]{3,2,1,0:T(8,128)(2,1)S(1)} %get-tuple-element.18, bf16[12,7,128,128]{3,2,1,0:T(8,128)(2,1)S(1)} %copy-done.2, ...), kind=kLoop, calls=%fused_computation.99 | loop fusion | bytes 11010048
  99.5 2.5 %constant_dynamic-update-slice_fusion.8 = (bf16[24,7,128,128]{3,2,1,0:T(8,128)(2,1)S(1)}, bf16[18,7,128,128]{3,2,1,0:T(8,128)(2,1)S(1)}) fusion(bf16[24,7,128,128]{3,2,1,0:T(8,128)(2,1)S(1)} %get-tuple-element.8, bf16[6,7,128,128]{3,2,1,0:T(8,128)(2,1)} %collective-permute-done.1, bf16[18,7,128,128]{3,2,1,0:T(8,128)(2,1)S(1)} %get-tuple-element.9), kind=kLoop, calls=%fused_computation.98 | loop fusion | bytes 4128768 | tf_op jit(solution)/shard_map/concatenate | solution.py:13
  102.1 1.6 fusion.44
  103.7 1.4 fusion.65
  105.1 1.4 convolution_bitcast_fusion.1
  106.5 1.1 convolution_bitcast_fusion
  107.7 1.1 fusion.150
  109.9 1.6 copy-done.10
  113.2 0.9 constant_dynamic-update-slice_fusion.17
  114.2 1.0 constant_dynamic-update-slice_fusion.16
  115.1 1.0 constant_dynamic-update-slice_fusion.15
  116.1 0.9 bitcast_dynamic-update-slice_fusion.3
  117.1 0.8 bitcast_dynamic-update-slice_fusion.1
  117.9 0.7 bitcast_dynamic-update-slice_fusion
  118.6 2.2 %fusion.143 = f32[12,7,64,128]{3,2,1,0:T(8,128)S(1)} fusion(f32[12,64,128]{2,1,0:T(8,128)S(1)} %copy-done.14, bf16[12,13,64,128]{3,2,1,0:T(8,128)(2,1)} %bitcast_dynamic-update-slice_fusion, bf16[18,7,128,128]{3,2,1,0:T(8,128)(2,1)S(1)} %copy-done.11), kind=kOutput, calls=%fused_computation.67 | convolution fusion | flops 176259072 | bytes 6094848 | tf_op jit(solution)/shard_map/rmpq,rmqs->rps/dot_general | solution.py:53
  121.6 0.9 copy-done.5
  127.3 1.1 copy-done.1
  129.1 0.9 fusion.149
  129.9 30.1 %psum.7 = f32[]{:T(128)} all-reduce(f32[]{:T(128)} %fusion.149), channel_id=1, replica_groups=mesh['groups'=2,'row'=8,'col'=2] {'row','col'}, use_global_device_ids=true, to_apply=%region_1.2 | all-reduce | flops 1 | bytes 8 | tf_op jit(solution)/shard_map/psum | solution.py:103
  (58 shorter events, 9.1 us)
Async XLA Ops:
  7.2 22.0 %all-gather.2.cloned.1.call-start = ((), (), s32[]{:S(2)}) async-start(), calls=%async_computation | async-start | bytes 4128768 | tf_op jit(solution)/shard_map/all_gather | solution.py:95
  14.7 23.5 %copy-start = (bf16[12,7,64,128]{3,2,1,0:T(8,128)(2,1)S(1)}, bf16[12,7,64,128]{3,2,1,0:T(8,128)(2,1)}, u32[]{:S(2)}) copy-start(bf16[12,7,64,128]{3,2,1,0:T(8,128)(2,1)} %select_convert_fusion) | copy-start | bytes 4128772
  32.2 63.3 %collective-permute-start = (bf16[6,7,128,128]{3,2,1,0:T(8,128)(2,1)}, bf16[6,7,128,128]{3,2,1,0:T(8,128)(2,1)}, u32[]{:S(2)}, u32[]{:S(2)}) collective-permute-start(bf16[6,7,128,128]{3,2,1,0:T(8,128)(2,1)} %get-tuple-element.12), channel_id=1, source_target_pairs={{0,2},{2,4},{4,6},{6,8},{8,10},{10,12},{12,14},{1,3},{3,5},{5,7},{... | collective-permute-start | bytes 4128776 | tf_op jit(solution)/shard_map/ppermute | solution.py:15
  37.0 62.6 %collective-permute-start.1 = (bf16[6,7,128,128]{3,2,1,0:T(8,128)(2,1)S(1)}, bf16[6,7,128,128]{3,2,1,0:T(8,128)(2,1)}, u32[]{:S(2)}, u32[]{:S(2)}) collective-permute-start(bf16[6,7,128,128]{3,2,1,0:T(8,128)(2,1)S(1)} %get-tuple-element.11), channel_id=1, source_target_pairs={{2,0},{4,2},{6,4},{8,6},{10,8},{12,10},{14,12},{3,1},{5,3},{7,5},{... | collective-permute-start | bytes 4128776 | tf_op jit(solution)/shard_map/ppermute | solution.py:17
  40.1 3.1 %copy-start.2 = (bf16[12,7,128,128]{3,2,1,0:T(8,128)(2,1)S(1)}, bf16[12,7,128,128]{3,2,1,0:T(8,128)(2,1)}, u32[]{:S(2)}) copy-start(bf16[12,7,128,128]{3,2,1,0:T(8,128)(2,1)} %all-gather.2.cloned.1.call-done) | copy-start | bytes 8257540
  109.6 1.9 %copy-start.10 = (bf16[18,7,128,128]{3,2,1,0:T(8,128)(2,1)}, bf16[18,7,128,128]{3,2,1,0:T(8,128)(2,1)S(1)}, u32[]{:S(2)}) copy-start(bf16[18,7,128,128]{3,2,1,0:T(8,128)(2,1)S(1)} %slice_dynamic-update-slice_fusion) | copy-start | bytes 12386308
  112.8 5.8 %copy-start.14 = (f32[12,64,128]{2,1,0:T(8,128)S(1)}, f32[12,64,128]{2,1,0:T(8,128)}, u32[]{:S(2)}) copy-start(f32[12,64,128]{2,1,0:T(8,128)} %fusion.35) | copy-start | bytes 1179652
  113.2 5.4 %copy-start.11 = (bf16[18,7,128,128]{3,2,1,0:T(8,128)(2,1)S(1)}, bf16[18,7,128,128]{3,2,1,0:T(8,128)(2,1)}, u32[]{:S(2)}) copy-start(bf16[18,7,128,128]{3,2,1,0:T(8,128)(2,1)} %copy-done.10) | copy-start | bytes 12386308
  118.6 2.2 %copy-start.6 = (bf16[12,12,64,128]{3,2,1,0:T(8,128)(2,1)S(1)}, bf16[12,12,64,128]{3,2,1,0:T(8,128)(2,1)}, u32[]{:S(2)}) copy-start(bf16[12,12,64,128]{3,2,1,0:T(8,128)(2,1)} %get-tuple-element.32) | copy-start | bytes 7077892
  118.6 2.2 %copy-start.13 = (f32[12,64,128]{2,1,0:T(8,128)S(1)}, f32[12,64,128]{2,1,0:T(8,128)}, u32[]{:S(2)}) copy-start(f32[12,64,128]{2,1,0:T(8,128)} %fusion.44) | copy-start | bytes 1179652
  120.8 1.6 copy-start.5
  120.8 1.6 copy-start.12
  122.5 1.3 copy-start.4
  122.5 1.4 copy-start.9
  123.9 1.0 copy-start.8
  124.9 1.0 copy-start.7
  126.6 1.8 %copy-start.1 = (f32[12,7,64,128]{3,2,1,0:T(8,128)S(1)}, f32[12,7,64,128]{3,2,1,0:T(8,128)}, u32[]{:S(2)}) copy-start(f32[12,7,64,128]{3,2,1,0:T(8,128)} %param.4) | copy-start | bytes 8257540
  129.0 31.6 %copy-start.3 = (f32[12,7,64,128]{3,2,1,0:T(8,128)}, f32[12,7,64,128]{3,2,1,0:T(8,128)S(1)}, u32[]{:S(2)}) copy-start(f32[12,7,64,128]{3,2,1,0:T(8,128)S(1)} %subtract_select_fusion) | copy-start | bytes 8257540
Sparse Core Ops, SparseCore 0:
  14.8 14.2 all-gather.1
where the time goes:
time: 169 us
  waiting for transfers between devices  65 us (38%)
  blocking collectives  30.1 us (18%)
  local copies, waits for them, and re-layouts  28.2 us (17%)
  between operations  18.1 us (11%)
  matrix products  14.8 us (9%)
  other arithmetic  6.36 us (4%)
  starting transfers between devices  6.04 us (4%)
    ppermute x1, waiting for transfers between devices, with_halo(): lax.ppermute(tail, axis, [(i, (i + 1) % count) for i in range(ends)])  50.6 us
    psum x1, blocking collectives, per_device(): occupied = [lax.psum(partial_trace, ('row', 'col')) * scale_orbitals]  30.1 us
    unnamed x42, local copies, waits for them, and re-layouts  15.3 us
    all_gather x1, waiting for transfers between devices, per_device(): assembled = lax.all_gather(current, 'col', axis=2, tiled=True)  14.4 us
    dot_general x6, matrix products, band_square(): jnp.einsum('repq,resq->rps', current[:, d + 1:], extended[band_width + d:...  8.43 us
    dot_general x7, matrix products, band_square(): jnp.einsum('rmpq,rmqs->rps', left_blocks[:, band_width - d:2 * band_width...  6.35 us
    ppermute x1, starting transfers between devices, with_halo(): lax.ppermute(tail, axis, [(i, (i + 1) % count) for i in range(ends)])  4.72 us
  transfers between devices with their start and end apart: 3, of which 2 were waited for; matrix products, arithmetic and copies ran while one was open for 6% of the time, Pallas kernels for 0%

commit v1 on v0

v1 whole, which is shorter than its diff:
```python
import functools

import jax
import jax.numpy as jnp
from jax import lax
from jax.experimental import pallas as pl
from jax.experimental.pallas import tpu as pltpu
from jax.sharding import PartitionSpec as P

SMEM = pl.BlockSpec(memory_space=pltpu.SMEM)
VMEM = pl.BlockSpec(memory_space=pltpu.VMEM)
ANY = pl.BlockSpec(memory_space=pl.ANY)
F32 = jnp.float32
BF16 = jnp.bfloat16
MIB = 1 << 20


def tail_blocks(rows, width):
    return [(rows - m, d) for m in range(1, width + 1) for d in range(m, width + 1)]


def head_blocks(width):
    return [(m, d) for m in range(width) for d in range(width - m)]


def runs(blocks):
    out = []
    for place, (row, d) in enumerate(blocks):
        if out and out[-1][0] == row:
            out[-1][2] += 1
        else:
            out.append([row, d, 1, place])
    return out


def is_kept(reach_ref, row, d, first_row, total_rows):
    return (d <= reach_ref[row]) & (first_row + row + d < total_rows)


def start_block(h, d, kept, bounds_ref, on_diag):
    high = bounds_ref[1]
    scale = jnp.where(kept, 1.0, 0.0) / (high + bounds_ref[0])
    if d == 0:
        return ((jnp.where(on_diag, high, 0.0) - h) * scale).astype(BF16)
    return (h * -scale).astype(BF16)


def diag_mask(half, size):
    rows = lax.broadcasted_iota(jnp.int32, (half, size), 0) + lax.axis_index("col") * half
    return lax.broadcasted_iota(jnp.int32, (half, size), 1) == rows


def pack_kernel(dims, reach_ref, bounds_ref, h_ref, tail_ref, head_ref, buf, sems):
    rows, width, half, size = dims
    first_row = lax.axis_index("row") * rows
    total_rows = lax.axis_size("row") * rows
    on_diag = diag_mask(half, size)
    jobs = [(out, run) for out, blocks in ((tail_ref, tail_blocks(rows, width)), (head_ref, head_blocks(width)))
            for run in runs(blocks)]
    copies = []
    at = 0
    for n, (out, (row, d, count, place)) in enumerate(jobs):
        copy = pltpu.make_async_copy(h_ref.at[row, pl.ds(d, count)], buf.at[pl.ds(at, count)], sems.at[n])
        copy.start()
        copies.append((copy, at))
        at += count
    for (out, (row, d, count, place)), (copy, at) in zip(jobs, copies):
        copy.wait()
        for e in range(count):
            kept = is_kept(reach_ref, row, d + e, first_row, total_rows)
            out[place + e] = start_block(buf[at + e], d + e, kept, bounds_ref, on_diag)


def start_kernel(dims, reach_ref, bounds_ref, flag_ref, h_ref, after_ref, x_ref, part_ref):
    rows, width, half, size = dims
    first_row = lax.axis_index("row") * rows
    total_rows = lax.axis_size("row") * rows
    on_diag = diag_mask(half, size)
    count = h_ref.shape[0]
    step = pl.program_id(0)

    def fold(block):
        return jnp.sum(block.reshape(half // 8, 8, size), axis=0)

    diag = jnp.zeros((8, size), F32)
    once = jnp.zeros((8, size), F32)
    twice = jnp.zeros((8, size), F32)
    for e in range(count):
        row = step * count + e
        for d in range(width + 1):
            kept = is_kept(reach_ref, row, d, first_row, total_rows)
            x = start_block(h_ref[e, d], d, kept, bounds_ref, on_diag)
            x_ref[e, d] = x
            wide = x.astype(F32)
            if d == 0:
                diag = diag + fold(jnp.where(on_diag, wide, 0.0))
                once = once + fold(wide * wide)
            else:
                twice = twice + fold(wide * wide)
    norm = once + 2.0 * twice
    part = jnp.where(flag_ref[0] == 1, norm, 2.0 * diag - norm)

    @pl.when(step == 0)
    def _():
        part_ref[...] = part

    @pl.when(step > 0)
    def _():
        part_ref[...] += part


def strips(rows, width):
    out = []
    for j in range(0, rows + width, 2):
        cols = list(range(j, min(j + 2, rows + width)))
        i_lo, i_hi = max(0, j - width), min(rows - 1, cols[-1])
        k_lo = max(0, j - width)
        k_hi = min(rows + width - 1 if j < rows else rows - 1, cols[-1] + width, i_hi + width)
        out.append((cols, i_lo, i_hi, k_lo, k_hi))
    return out


def inner_kernel(dims, reach_ref, flag_ref, mine_ref, other_ref, out_ref, full, left):
    rows, width, half, size = dims
    column = lax.axis_index("col")
    first_row = lax.axis_index("row") * rows
    total_rows = lax.axis_size("row") * rows
    mine = pl.multiple_of(column * half, half)
    other = pl.multiple_of((1 - column) * half, half)
    zero_full = jnp.zeros((size, size), BF16)
    zero_left = jnp.zeros((half, size), BF16)

    def block(n):
        return pl.ds(n * size, size)

    for k in range(rows):
        for d in range(width + 1):
            full[pl.ds(k * size + mine, half), block(k + d)] = mine_ref[k, d]
            full[pl.ds(k * size + other, half), block(k + d)] = other_ref[k, d]
    have_full = {(k, k + d) for k in range(rows) for d in range(width + 1)}
    for j in range(rows):
        for d in range(1, width + 1):
            full[block(j + d), block(j)] = full[block(j), block(j + d)].T
            have_full.add((j + d, j))
    need_full, need_left = set(), set()
    for cols, i_lo, i_hi, k_lo, k_hi in strips(rows, width):
        need_full |= {(k, j) for k in range(k_lo, k_hi + 1) for j in cols}
        need_left |= {(i, k) for i in range(i_lo, i_hi + 1) for k in range(k_lo, k_hi + 1)}
    for k, j in sorted(need_full - have_full):
        full[block(k), block(j)] = zero_full
    for i, k in sorted(need_left):
        if k < i - width or k > i + width:
            piece = zero_left
        elif k >= i:
            piece = mine_ref[i, k - i]
        else:
            piece = full[pl.ds(i * size + mine, half), block(k)]
        left[pl.ds(i * half, half), block(k)] = piece

    sign = jnp.where(flag_ref[0] == 1, 1.0, -1.0)
    twice = jnp.where(flag_ref[0] == 1, 0.0, 2.0)
    for cols, i_lo, i_hi, k_lo, k_hi in strips(rows, width):
        depth = pl.ds(k_lo * size, (k_hi - k_lo + 1) * size)
        square = jnp.dot(
            left[pl.ds(i_lo * half, (i_hi - i_lo + 1) * half), depth],
            full[depth, pl.ds(cols[0] * size, len(cols) * size)],
            preferred_element_type=F32,
        )
        for n, j in enumerate(cols):
            for i in range(max(i_lo, j - width), min(i_hi, j) + 1):
                d = j - i
                kept = is_kept(reach_ref, i, d, first_row, total_rows)
                part = square[(i - i_lo) * half : (i - i_lo + 1) * half, n * size : (n + 1) * size]
                out_ref[i, d] = part * jnp.where(kept, sign, 0.0) + twice * mine_ref[i, d].astype(F32)


def halo_kernel(
    dims, reach_ref, flag_ref, above_mine, above_other, below_mine, below_other, own_tail, base_ref, out_ref,
    above, above_t, above_left, below, tail_left, held, in_sems, out_sems,
):
    rows, width, half, size = dims
    column = lax.axis_index("col")
    first_row = lax.axis_index("row") * rows
    total_rows = lax.axis_size("row") * rows
    mine = pl.multiple_of(column * half, half)
    other = pl.multiple_of((1 - column) * half, half)
    tails, heads = tail_blocks(rows, width), head_blocks(width)

    copies = []
    jobs = [(run, run[3]) for run in runs(heads)] + [(run, len(heads) + run[3]) for run in runs(tails)]
    for n, ((row, d, count, _), at) in enumerate(jobs):
        copy = pltpu.make_async_copy(base_ref.at[row, pl.ds(d, count)], held.at[pl.ds(at, count)], in_sems.at[n])
        copy.start()
        copies.append(copy)

    def block(n):
        return pl.ds(n * size, size)

    zero_full = jnp.zeros((size, size), BF16)
    zero_left = jnp.zeros((half, size), BF16)
    have = set()
    for n, (row, d) in enumerate(tails):
        k, j = row - rows + width, row + d - rows
        above[pl.ds(k * size + mine, half), block(j)] = above_mine[n]
        above[pl.ds(k * size + other, half), block(j)] = above_other[n]
        tail_left[pl.ds(k * half, half), block(j)] = own_tail[n]
        have.add((k, j))
    for k in range(width):
        for j in range(width):
            if (k, j) not in have:
                above[block(k), block(j)] = zero_full
                above_left[pl.ds(j * half, half), block(k)] = zero_left
                tail_left[pl.ds(k * half, half), block(j)] = zero_left
    for k, j in sorted(have):
        above_t[block(j), block(k)] = above[block(k), block(j)].T
        above_left[pl.ds(j * half, half), block(k)] = above_t[pl.ds(j * size + mine, half), block(k)]
    for n, (k, d) in enumerate(heads):
        below[pl.ds(k * size + mine, half), block(k + d)] = below_mine[n]
        below[pl.ds(k * size + other, half), block(k + d)] = below_other[n]
    for k, d in heads:
        if d:
            below[block(k + d), block(k)] = below[block(k), block(k + d)].T
    first = jnp.dot(above_left[...], above[...], preferred_element_type=F32)
    second = jnp.dot(tail_left[...], below[...], preferred_element_type=F32)

    sign = jnp.where(flag_ref[0] == 1, 1.0, -1.0)
    backs = []
    for n, ((row, d, count, _), at) in enumerate(jobs):
        copies[n].wait()
        for e in range(count):
            if n < len(runs(heads)):
                i, j, square = row, row + d + e, first
            else:
                i, j, square = row - rows + width, row + d + e - rows, second
            kept = is_kept(reach_ref, row, d + e, first_row, total_rows)
            part = square[i * half : (i + 1) * half, j * size : (j + 1) * size]
            held[at + e] = held[at + e] + part * jnp.where(kept, sign, 0.0)
        copy = pltpu.make_async_copy(held.at[pl.ds(at, count)], out_ref.at[row, pl.ds(d, count)], out_sems.at[n])
        copy.start()
        backs.append(copy)
    for copy in backs:
        copy.wait()


def per_device(hamiltonian, bounds, block_reach, branch_flags):
    rows, offsets, half, size = hamiltonian.shape
    width = offsets - 1
    dims = (rows, width, half, size)
    halo = len(head_blocks(width))
    count = lax.axis_size("row")
    down = [(i, i + 1) for i in range(count - 1)]
    up = [(i + 1, i) for i in range(count - 1)]
    swap = [(0, 1), (1, 0)]
    packed = jax.ShapeDtypeStruct((halo, half, size), BF16)
    runs_count = 2 * width

    tail, head = pl.pallas_call(
        functools.partial(pack_kernel, dims),
        out_shape=(packed, packed),
        in_specs=[SMEM, SMEM, ANY],
        out_specs=(VMEM, VMEM),
        scratch_shapes=[pltpu.VMEM((2 * halo, half, size), F32), pltpu.SemaphoreType.DMA((runs_count,))],
        compiler_params=pltpu.CompilerParams(vmem_limit_bytes=8 * MIB),
        name="pack",
    )(block_reach, bounds, hamiltonian)
    above_mine = lax.ppermute(tail, "row", down)
    below_mine = lax.ppermute(head, "row", up)

    per_step = 3 if rows % 3 == 0 else 1
    current, part = pl.pallas_call(
        functools.partial(start_kernel, dims),
        grid=(rows // per_step,),
        out_shape=(jax.ShapeDtypeStruct(hamiltonian.shape, BF16), jax.ShapeDtypeStruct((8, size), F32)),
        in_specs=[SMEM, SMEM, SMEM, pl.BlockSpec((per_step, offsets, half, size), lambda s: (s, 0, 0, 0)), ANY],
        out_specs=(
            pl.BlockSpec((per_step, offsets, half, size), lambda s: (s, 0, 0, 0)),
            pl.BlockSpec((8, size), lambda s: (0, 0)),
        ),
        compiler_params=pltpu.CompilerParams(vmem_limit_bytes=16 * MIB),
        cost_estimate=pl.CostEstimate(flops=4 * hamiltonian.size, bytes_accessed=6 * hamiltonian.size, transcendentals=0),
        name="start",
    )(block_reach, bounds, branch_flags, hamiltonian, tail)
    swapped = lax.ppermute(current, "col", swap)
    trace = lax.psum(part, ("row", "col"))

    products = rows * sum(2 * width + 1 - d for d in range(width + 1))
    base = pl.pallas_call(
        functools.partial(inner_kernel, dims),
        out_shape=jax.ShapeDtypeStruct(hamiltonian.shape, F32),
        in_specs=[SMEM, SMEM, VMEM, VMEM],
        out_specs=VMEM,
        scratch_shapes=[
            pltpu.VMEM(((rows + width) * size, (rows + width) * size), BF16),
            pltpu.VMEM((rows * half, (rows + width) * size), BF16),
        ],
        compiler_params=pltpu.CompilerParams(vmem_limit_bytes=40 * MIB),
        cost_estimate=pl.CostEstimate(
            flops=2 * products * half * size * size, bytes_accessed=8 * hamiltonian.size, transcendentals=0
        ),
        name="inner",
    )(block_reach, branch_flags, current, swapped)

    above_other = lax.ppermute(above_mine, "col", swap)
    below_other = lax.ppermute(below_mine, "col", swap)
    density = pl.pallas_call(
        functools.partial(halo_kernel, dims),
        out_shape=jax.ShapeDtypeStruct(hamiltonian.shape, F32),
        in_specs=[SMEM, SMEM, VMEM, VMEM, VMEM, VMEM, VMEM, ANY],
        out_specs=ANY,
        input_output_aliases={7: 0},
        scratch_shapes=[
            pltpu.VMEM((width * size, width * size), BF16),
            pltpu.VMEM((width * size, width * size), BF16),
            pltpu.VMEM((width * half, width * size), BF16),
            pltpu.VMEM((width * size, width * size), BF16),
            pltpu.VMEM((width * half, width * size), BF16),
            pltpu.VMEM((2 * halo, half, size), F32),
            pltpu.SemaphoreType.DMA((runs_count,)),
            pltpu.SemaphoreType.DMA((runs_count,)),
        ],
        compiler_params=pltpu.CompilerParams(vmem_limit_bytes=24 * MIB),
        name="halo",
    )(block_reach, branch_flags, above_mine, above_other, below_mine, below_other, tail, base)
    occupancy = jnp.sum(trace) / (count * rows * size)
    return density, occupancy.reshape(1)


def solution(mesh):
    placed = (
        P(("groups", "row"), None, "col", None),
        P("groups"),
        P(("groups", "row")),
        P("groups"),
    )
    return jax.shard_map(
        per_device,
        mesh=mesh,
        in_specs=placed,
        out_specs=(P(("groups", "row"), None, "col", None), P("groups")),
        check_vma=False,
    )
```

time: 169 us -> 75.9 us (0.45)
  waiting for transfers between devices: 65 us -> 14.3 us
  local copies, waits for them, and re-layouts: 28.2 us -> 3.09 us
  Pallas kernels: 0 us -> 15.3 us
  between operations: 18.1 us -> 3.18 us
  matrix products: 14.8 us -> 0 us
  other arithmetic: 6.36 us -> 0.6 us
  blocking collectives: 30.1 us -> 32.2 us
    ppermute x2 -> x5, waiting for transfers between devices: 50.6 us -> 14.3 us  [the longest x1 7.55 us: per_device(): above_mine = lax.ppermute(tail, 'row', down)]
    pallas_call x0 -> x4, Pallas kernels: none -> 15.3 us  [the longest x1 6.78 us: per_device(): pl.pallas_call(functools.partial(inner_kernel, dims), out_shape=jax.Shape...]
    dot_general x13 -> x0, matrix products: 14.8 us -> none  [the longest x6 8.43 us: band_square(): jnp.einsum('repq,resq->rps', current[:, d + 1:], extended[band_width + d:...]
    all_gather x1 -> x0, waiting for transfers between devices: 14.4 us -> none  [per_device(): assembled = lax.all_gather(current, 'col', axis=2, tiled=True)]
    unnamed x42 -> x12, local copies, waits for them, and re-layouts: 15.3 us -> 3.09 us
    concatenate x4 -> x0, local copies, waits for them, and re-layouts: 4.98 us -> none  [the longest x3 2.5 us: band_square(): left_blocks = jnp.concatenate([current[:, ::-1], lower_part], axis=1)]
    slice x3 -> x0, local copies, waits for them, and re-layouts: 4.67 us -> none  [the longest x1 3.11 us: with_halo(): head = lax.slice_in_dim(cells, 0, width, axis=dim)]
    convert_element_type x1 -> x0, other arithmetic: 3.27 us -> none  [per_device(): jnp.where(kept_mask[:, :, None, None], start_band, 0.0).astype(jnp.bfloat16)]
  transfers between devices with their start and end apart: 3 -> 5, of which waited for: 2 -> 2; matrix products, arithmetic and copies ran while one was open for 6% -> 1% of each run, Pallas kernels for 0% -> 9%
where the time goes in v1:
time: 75.9 us; the launch traced here: 75.6 us
  blocking collectives  32.2 us (42%)
  Pallas kernels  15.3 us (20%)
  waiting for transfers between devices  14.3 us (19%)
  starting transfers between devices  6.94 us (9%)
  between operations  3.18 us (4%)
  local copies, waits for them, and re-layouts  3.09 us (4%)
    psum x1, blocking collectives, per_device(): trace = lax.psum(part, ('row', 'col'))  32.2 us
    ppermute x1, waiting for transfers between devices, per_device(): above_mine = lax.ppermute(tail, 'row', down)  7.55 us
    pallas_call x1, Pallas kernels, per_device(): pl.pallas_call(functools.partial(inner_kernel, dims), out_shape=jax.Shape...  6.78 us
    ppermute x1, waiting for transfers between devices, per_device(): below_mine = lax.ppermute(head, 'row', up)  6.75 us
    ppermute x1, starting transfers between devices, per_device(): above_mine = lax.ppermute(tail, 'row', down)  5.09 us
    pallas_call x1, Pallas kernels, per_device(): pl.pallas_call(functools.partial(halo_kernel, dims), out_shape=jax.ShapeD...  4.16 us
    unnamed x12, local copies, waits for them, and re-layouts  3.09 us
    pallas_call x1, Pallas kernels, per_device(): pl.pallas_call(functools.partial(pack_kernel, dims), out_shape=(packed, p...  3.09 us
  transfers between devices with their start and end apart: 5, of which 2 were waited for; matrix products, arithmetic and copies ran while one was open for 1% of the time, Pallas kernels for 9%

profile of v1, /device:TPU:0, one launch (start us, length us, event | category | flops | bytes accessed | tf_op | source)
XLA Modules:
  0.0 75.6 jit_solution(9194383748096048889)
XLA Ops:
  0.6 0.0 copy-start.3
  0.6 0.0 copy-start.5
  1.3 0.0 copy-start
  1.3 1.8 %copy-done = f32[12,7,64,128]{3,2,1,0:T(8,128)S(1)} copy-done((f32[12,7,64,128]{3,2,1,0:T(8,128)S(1)}, f32[12,7,64,128]{3,2,1,0:T(8,128)}, u32[]{:S(2)}) %copy-start) | copy-done | bytes 2752536
  3.1 0.0 copy-start.2
  3.1 0.7 copy-done.2
  3.7 0.0 copy-start.4
  3.8 0.7 copy-done.4
  4.4 0.0 copy-start.1
  4.4 3.1 %pack.1 = (bf16[21,64,128]{2,1,0:T(8,128)(2,1)S(1)}, bf16[21,64,128]{2,1,0:T(8,128)(2,1)S(1)}) custom-call(s32[12]{0:T(128)S(1)} %copy-done.2, f32[2]{0:T(128)S(1)} %copy-done.4, f32[12,7,64,128]{3,2,1,0:T(8,128)S(1)} %copy-done), custom_call_target="tpu_custom_call" | custom-call | tf_op jit(solution)/shard_map/pack/pallas_call | solution.py:257
  7.5 0.0 copy-done.3
  7.5 0.0 copy-done.5
  7.5 0.0 copy-done.1
  7.5 1.3 %start.1 = (bf16[12,7,64,128]{3,2,1,0:T(8,128)(2,1)S(1)}, f32[8,128]{1,0:T(8,128)S(1)}) custom-call(s32[12]{0:T(128)S(1)} %copy-done.3, f32[2]{0:T(128)S(1)} %copy-done.5, s32[1]{0:T(128)S(6)} %copy.8.flag_ref, f32[12,7,64,128]{3,2,1,0:T(8,128)S(1)} %copy-done.1, bf16[21,64,128]{2,1,0:T(8,128)(2,1)S(1)} %get-tuple-element.6.after_ref.own_tail), custom_call_target="tpu_custom_call" | custom-call | flops 2752512 | bytes 4128768 | tf_op jit(solution)/shard_map/start/pallas_call | solution.py:270
  8.9 0.5 collective-permute-start.4
  9.4 1.3 %collective-permute-start.2 = (bf16[21,64,128]{2,1,0:T(8,128)(2,1)S(1)}, bf16[21,64,128]{2,1,0:T(8,128)(2,1)S(1)}, u32[]{:S(2)}, u32[]{:S(2)}) collective-permute-start(bf16[21,64,128]{2,1,0:T(8,128)(2,1)S(1)} %get-tuple-element.7), channel_id=1, source_target_pairs={{2,0},{4,2},{6,4},{8,6},{10,8},{12,10},{14,12},{3,1},{5,3},{7,5},{... | collective-permute-start | bytes 1032200 | tf_op jit(solution)/shard_map/ppermute | solution.py:267
  10.7 5.1 %collective-permute-start = (bf16[21,64,128]{2,1,0:T(8,128)(2,1)S(1)}, bf16[21,64,128]{2,1,0:T(8,128)(2,1)S(1)}, u32[]{:S(2)}, u32[]{:S(2)}) collective-permute-start(bf16[21,64,128]{2,1,0:T(8,128)(2,1)S(1)} %get-tuple-element.6.after_ref.own_tail), channel_id=1, source_target_pairs={{0,2},{2,4},{4,6},{6,8},{8,10},{10,12},{12,14},{1,3},{3,5},{5,7},{... | collective-permute-start | bytes 1032200 | tf_op jit(solution)/shard_map/ppermute | solution.py:266
  15.8 6.7 %collective-permute-done.2.below_mine = bf16[21,64,128]{2,1,0:T(8,128)(2,1)S(1)} collective-permute-done((bf16[21,64,128]{2,1,0:T(8,128)(2,1)S(1)}, bf16[21,64,128]{2,1,0:T(8,128)(2,1)S(1)}, u32[]{:S(2)}, u32[]{:S(2)}) %collective-permute-start.2) | collective-permute-done | bytes 344096 | tf_op jit(solution)/shard_map/ppermute | solution.py:267
  22.5 0.0 collective-permute-start.3
  22.5 7.5 %collective-permute-done.above_mine = bf16[21,64,128]{2,1,0:T(8,128)(2,1)S(1)} collective-permute-done((bf16[21,64,128]{2,1,0:T(8,128)(2,1)S(1)}, bf16[21,64,128]{2,1,0:T(8,128)(2,1)S(1)}, u32[]{:S(2)}, u32[]{:S(2)}) %collective-permute-start) | collective-permute-done | bytes 344096 | tf_op jit(solution)/shard_map/ppermute | solution.py:266
  30.1 0.0 collective-permute-start.1
  30.1 32.2 %psum.7 = f32[8,128]{1,0:T(8,128)S(1)} all-reduce(f32[8,128]{1,0:T(8,128)S(1)} %get-tuple-element.9), channel_id=1, replica_groups=mesh['groups'=2,'row'=8,'col'=2] {'row','col'}, use_global_device_ids=true, to_apply=%region_0.0 | all-reduce | flops 1024 | bytes 8192 | tf_op jit(solution)/shard_map/psum | solution.py:284
  62.3 0.6 reduce_sum.9
  63.5 0.0 collective-permute-done.4.other_ref
  63.5 6.8 %inner.1.base_ref = f32[12,7,64,128]{3,2,1,0:T(8,128)} custom-call(s32[12]{0:T(128)S(1)} %copy-done.3, s32[1]{0:T(128)S(6)} %copy.8.flag_ref, bf16[12,7,64,128]{3,2,1,0:T(8,128)(2,1)S(1)} %get-tuple-element.8.mine_ref, bf16[12,7,64,128]{3,2,1,0:T(8,128)(2,1)} %collective-permute-done.4.other_ref), custom_call_target="tpu_custom_call" | custom-call | flops 1761607680 | bytes 5505024 | tf_op jit(solution)/shard_map/inner/pallas_call | solution.py:287
  70.3 0.0 collective-permute-done.3.below_other
  70.3 0.0 collective-permute-done.1.above_other
  70.3 4.2 %halo.1 = f32[12,7,64,128]{3,2,1,0:T(8,128)} custom-call(s32[12]{0:T(128)S(1)} %copy-done.3, s32[1]{0:T(128)S(6)} %copy.8.flag_ref, bf16[21,64,128]{2,1,0:T(8,128)(2,1)S(1)} %collective-permute-done.above_mine, bf16[21,64,128]{2,1,0:T(8,128)(2,1)S(1)} %collective-permute-done.1.above_other, ...), custom_call_target="tpu_custom_call", output_to_operand_aliasing={{}: (7, {})} | custom-call | tf_op jit(solution)/shard_map/halo/pallas_call | solution.py:305
Async XLA Ops:
  0.6 6.9 %copy-start.3 = (s32[12]{0:T(128)S(1)}, s32[12]{0:T(128)}, u32[]{:S(2)}) copy-start(s32[12]{0:T(128)} %reach_ref.7) | copy-start | bytes 148
  0.6 6.9 %copy-start.5 = (f32[2]{0:T(128)S(1)}, f32[2]{0:T(128)}, u32[]{:S(2)}) copy-start(f32[2]{0:T(128)} %bounds_ref.3) | copy-start | bytes 28
  1.3 1.8 %copy-start = (f32[12,7,64,128]{3,2,1,0:T(8,128)S(1)}, f32[12,7,64,128]{3,2,1,0:T(8,128)}, u32[]{:S(2)}) copy-start(f32[12,7,64,128]{3,2,1,0:T(8,128)} %h_ref.3) | copy-start | bytes 8257540
  3.1 0.7 copy-start.2
  3.7 0.7 copy-start.4
  4.4 3.1 %copy-start.1 = (f32[12,7,64,128]{3,2,1,0:T(8,128)S(1)}, f32[12,7,64,128]{3,2,1,0:T(8,128)}, u32[]{:S(2)}) copy-start(f32[12,7,64,128]{3,2,1,0:T(8,128)} %h_ref.3) | copy-start | bytes 8257540
  8.9 54.7 %collective-permute-start.4 = (bf16[12,7,64,128]{3,2,1,0:T(8,128)(2,1)S(1)}, bf16[12,7,64,128]{3,2,1,0:T(8,128)(2,1)}, u32[]{:S(2)}, u32[]{:S(2)}) collective-permute-start(bf16[12,7,64,128]{3,2,1,0:T(8,128)(2,1)S(1)} %get-tuple-element.8.mine_ref), channel_id=1, source_target_pairs={{0,1},{1,0},{2,3},{3,2},{4,5},{5,4},{6,7},{7,6},{8,9},{9,8},{10,11... | collective-permute-start | bytes 4128776 | tf_op jit(solution)/shard_map/ppermute | solution.py:283
  9.4 13.1 %collective-permute-start.2 = (bf16[21,64,128]{2,1,0:T(8,128)(2,1)S(1)}, bf16[21,64,128]{2,1,0:T(8,128)(2,1)S(1)}, u32[]{:S(2)}, u32[]{:S(2)}) collective-permute-start(bf16[21,64,128]{2,1,0:T(8,128)(2,1)S(1)} %get-tuple-element.7), channel_id=1, source_target_pairs={{2,0},{4,2},{6,4},{8,6},{10,8},{12,10},{14,12},{3,1},{5,3},{7,5},{... | collective-permute-start | bytes 1032200 | tf_op jit(solution)/shard_map/ppermute | solution.py:267
  10.7 19.4 %collective-permute-start = (bf16[21,64,128]{2,1,0:T(8,128)(2,1)S(1)}, bf16[21,64,128]{2,1,0:T(8,128)(2,1)S(1)}, u32[]{:S(2)}, u32[]{:S(2)}) collective-permute-start(bf16[21,64,128]{2,1,0:T(8,128)(2,1)S(1)} %get-tuple-element.6.after_ref.own_tail), channel_id=1, source_target_pairs={{0,2},{2,4},{4,6},{6,8},{8,10},{10,12},{12,14},{1,3},{3,5},{5,7},{... | collective-permute-start | bytes 1032200 | tf_op jit(solution)/shard_map/ppermute | solution.py:266
  22.5 47.8 %collective-permute-start.3 = (bf16[21,64,128]{2,1,0:T(8,128)(2,1)S(1)}, bf16[21,64,128]{2,1,0:T(8,128)(2,1)S(1)}, u32[]{:S(2)}, u32[]{:S(2)}) collective-permute-start(bf16[21,64,128]{2,1,0:T(8,128)(2,1)S(1)} %collective-permute-done.2.below_mine), channel_id=1, source_target_pairs={{0,1},{1,0},{2,3},{3,2},{4,5},{5,4},{6,7},{7,6},{8,9},{9,8},{10,11... | collective-permute-start | bytes 1032200 | tf_op jit(solution)/shard_map/ppermute | solution.py:304
  30.1 40.3 %collective-permute-start.1 = (bf16[21,64,128]{2,1,0:T(8,128)(2,1)S(1)}, bf16[21,64,128]{2,1,0:T(8,128)(2,1)S(1)}, u32[]{:S(2)}, u32[]{:S(2)}) collective-permute-start(bf16[21,64,128]{2,1,0:T(8,128)(2,1)S(1)} %collective-permute-done.above_mine), channel_id=1, source_target_pairs={{0,1},{1,0},{2,3},{3,2},{4,5},{5,4},{6,7},{7,6},{8,9},{9,8},{10,11... | collective-permute-start | bytes 1032200 | tf_op jit(solution)/shard_map/ppermute | solution.py:303

commit v2 on v1

v2 whole, which is shorter than its diff:
```python
import functools

import jax
import jax.numpy as jnp
from jax import lax
from jax.experimental import pallas as pl
from jax.experimental.pallas import tpu as pltpu
from jax.sharding import PartitionSpec as P

SMEM = pl.BlockSpec(memory_space=pltpu.SMEM)
VMEM = pl.BlockSpec(memory_space=pltpu.VMEM)
ANY = pl.BlockSpec(memory_space=pl.ANY)
HBM = pl.BlockSpec(memory_space=pltpu.HBM)
F32 = jnp.float32
BF16 = jnp.bfloat16
MIB = 1 << 20
SMALL = pl.CostEstimate(flops=1, bytes_accessed=1, transcendentals=0)


def tail_blocks(rows, width):
    return [(rows - m, d) for m in range(1, width + 1) for d in range(m, width + 1)]


def head_blocks(width):
    return [(m, d) for m in range(width) for d in range(width - m)]


def runs(blocks):
    out = []
    for place, (row, d) in enumerate(blocks):
        if out and out[-1][0] == row:
            out[-1][2] += 1
        else:
            out.append([row, d, 1, place])
    return out


def is_kept(reach_ref, row, d, first_row, total_rows):
    return (d <= reach_ref[row]) & (first_row + row + d < total_rows)


def start_block(h, d, kept, bounds_ref, on_diag):
    high = bounds_ref[1]
    scale = jnp.where(kept, 1.0, 0.0) / (high + bounds_ref[0])
    if d == 0:
        return ((jnp.where(on_diag, high, 0.0) - h) * scale).astype(BF16)
    return (h * -scale).astype(BF16)


def diag_mask(half, size):
    rows = lax.broadcasted_iota(jnp.int32, (half, size), 0) + lax.axis_index("col") * half
    return lax.broadcasted_iota(jnp.int32, (half, size), 1) == rows


def start_kernel(
    dims, reach_hbm, bounds_hbm, flag_hbm, h_hbm, x_ref, tail_ref, head_ref, part_ref, h_ref, reach_ref, bounds_ref,
    flag_ref, row_sems, sems,
):
    rows, width, half, size = dims
    first_row = lax.axis_index("row") * rows
    total_rows = lax.axis_size("row") * rows
    small = [
        pltpu.make_async_copy(src, dst, sems.at[n])
        for n, (src, dst) in enumerate(((reach_hbm, reach_ref), (bounds_hbm, bounds_ref), (flag_hbm, flag_ref)))
    ]
    large = [pltpu.make_async_copy(h_hbm.at[i], h_ref.at[i], row_sems.at[i]) for i in range(rows)]
    for copy in small + large:
        copy.start()
    on_diag = diag_mask(half, size)
    place = {block: (tail_ref, n) for n, block in enumerate(tail_blocks(rows, width))}
    heads = {block: (head_ref, n) for n, block in enumerate(head_blocks(width))}

    def fold(block):
        return jnp.sum(block.reshape(half // 8, 8, size), axis=0)

    for copy in small:
        copy.wait()
    diag = jnp.zeros((8, size), F32)
    once = jnp.zeros((8, size), F32)
    twice = jnp.zeros((8, size), F32)
    for row in range(rows):
        large[row].wait()
        for d in range(width + 1):
            kept = is_kept(reach_ref, row, d, first_row, total_rows)
            x = start_block(h_ref[row, d], d, kept, bounds_ref, on_diag)
            x_ref[row, d] = x
            for table in (place, heads):
                if (row, d) in table:
                    ref, n = table[row, d]
                    ref[n] = x
            wide = x.astype(F32)
            if d == 0:
                diag = diag + fold(jnp.where(on_diag, wide, 0.0))
                once = once + fold(wide * wide)
            else:
                twice = twice + fold(wide * wide)
    norm = once + 2.0 * twice
    part_ref[...] = jnp.where(flag_ref[0] == 1, norm, 2.0 * diag - norm)


def strips(rows, width):
    out = []
    for j in range(0, rows + width, 2):
        cols = list(range(j, min(j + 2, rows + width)))
        i_lo, i_hi = max(0, j - width), min(rows - 1, cols[-1])
        k_lo = max(0, j - width)
        k_hi = min(rows + width - 1 if j < rows else rows - 1, cols[-1] + width, i_hi + width)
        out.append((cols, i_lo, i_hi, k_lo, k_hi))
    return out


def inner_kernel(dims, reach_ref, flag_ref, mine_ref, other_ref, out_ref, full, left):
    rows, width, half, size = dims
    column = lax.axis_index("col")
    first_row = lax.axis_index("row") * rows
    total_rows = lax.axis_size("row") * rows
    mine = pl.multiple_of(column * half, half)
    other = pl.multiple_of((1 - column) * half, half)
    zero_full = jnp.zeros((size, size), BF16)
    zero_left = jnp.zeros((half, size), BF16)

    def block(n):
        return pl.ds(n * size, size)

    for k in range(rows):
        for d in range(width + 1):
            full[pl.ds(k * size + mine, half), block(k + d)] = mine_ref[k, d]
            full[pl.ds(k * size + other, half), block(k + d)] = other_ref[k, d]
    have_full = {(k, k + d) for k in range(rows) for d in range(width + 1)}
    for j in range(rows):
        for d in range(1, width + 1):
            full[block(j + d), block(j)] = full[block(j), block(j + d)].T
            have_full.add((j + d, j))
    need_full, need_left = set(), set()
    for cols, i_lo, i_hi, k_lo, k_hi in strips(rows, width):
        need_full |= {(k, j) for k in range(k_lo, k_hi + 1) for j in cols}
        need_left |= {(i, k) for i in range(i_lo, i_hi + 1) for k in range(k_lo, k_hi + 1)}
    for k, j in sorted(need_full - have_full):
        full[block(k), block(j)] = zero_full
    for i, k in sorted(need_left):
        if k < i - width or k > i + width:
            piece = zero_left
        elif k >= i:
            piece = mine_ref[i, k - i]
        else:
            piece = full[pl.ds(i * size + mine, half), block(k)]
        left[pl.ds(i * half, half), block(k)] = piece

    sign = jnp.where(flag_ref[0] == 1, 1.0, -1.0)
    twice = jnp.where(flag_ref[0] == 1, 0.0, 2.0)
    for cols, i_lo, i_hi, k_lo, k_hi in strips(rows, width):
        depth = pl.ds(k_lo * size, (k_hi - k_lo + 1) * size)
        square = jnp.dot(
            left[pl.ds(i_lo * half, (i_hi - i_lo + 1) * half), depth],
            full[depth, pl.ds(cols[0] * size, len(cols) * size)],
            preferred_element_type=F32,
        )
        for n, j in enumerate(cols):
            for i in range(max(i_lo, j - width), min(i_hi, j) + 1):
                d = j - i
                kept = is_kept(reach_ref, i, d, first_row, total_rows)
                part = square[(i - i_lo) * half : (i - i_lo + 1) * half, n * size : (n + 1) * size]
                out_ref[i, d] = part * jnp.where(kept, sign, 0.0) + twice * mine_ref[i, d].astype(F32)


def fetch(base_ref, held, jobs, sems):
    copies = []
    for n, (row, d, count, at) in enumerate(jobs):
        copies.append(pltpu.make_async_copy(base_ref.at[row, pl.ds(d, count)], held.at[pl.ds(at, count)], sems.at[n]))
        copies[-1].start()
    return copies


def finish(dims, reach_ref, flag_ref, square, from_row, from_col, copies, jobs, held, out_ref, sems):
    rows, width, half, size = dims
    first_row = lax.axis_index("row") * rows
    total_rows = lax.axis_size("row") * rows
    sign = jnp.where(flag_ref[0] == 1, 1.0, -1.0)
    backs = []
    for n, (row, d, count, at) in enumerate(jobs):
        copies[n].wait()
        for e in range(count):
            i, j = row - from_row, row + d + e - from_col
            kept = is_kept(reach_ref, row, d + e, first_row, total_rows)
            part = square[i * half : (i + 1) * half, j * size : (j + 1) * size]
            held[at + e] = held[at + e] + part * jnp.where(kept, sign, 0.0)
        copy = pltpu.make_async_copy(held.at[pl.ds(at, count)], out_ref.at[row, pl.ds(d, count)], sems.at[n])
        copy.start()
        backs.append(copy)
    for copy in backs:
        copy.wait()


def halves(dims):
    half = dims[2]
    column = lax.axis_index("col")
    return pl.multiple_of(column * half, half), pl.multiple_of((1 - column) * half, half)


def above_kernel(
    dims, reach_ref, flag_ref, mine_ref, other_ref, base_ref, out_ref, above, above_t, left, held, in_sems, out_sems
):
    rows, width, half, size = dims
    mine, other = halves(dims)
    jobs = runs(head_blocks(width))
    copies = fetch(base_ref, held, jobs, in_sems)

    def block(n):
        return pl.ds(n * size, size)

    have = set()
    for n, (row, d) in enumerate(tail_blocks(rows, width)):
        k, j = row - rows + width, row + d - rows
        above[pl.ds(k * size + mine, half), block(j)] = mine_ref[n]
        above[pl.ds(k * size + other, half), block(j)] = other_ref[n]
        have.add((k, j))
    for k in range(width):
        for j in range(width):
            if (k, j) in have:
                above_t[block(j), block(k)] = above[block(k), block(j)].T
                left[pl.ds(j * half, half), block(k)] = above_t[pl.ds(j * size + mine, half), block(k)]
            else:
                above[block(k), block(j)] = jnp.zeros((size, size), BF16)
                left[pl.ds(j * half, half), block(k)] = jnp.zeros((half, size), BF16)
    square = jnp.dot(left[...], above[...], preferred_element_type=F32)
    finish(dims, reach_ref, flag_ref, square, 0, 0, copies, jobs, held, out_ref, out_sems)


def below_kernel(
    dims, reach_ref, flag_ref, mine_ref, other_ref, own_tail, base_ref, out_ref, below, left, held, in_sems, out_sems
):
    rows, width, half, size = dims
    mine, other = halves(dims)
    jobs = runs(tail_blocks(rows, width))
    copies = fetch(base_ref, held, jobs, in_sems)

    def block(n):
        return pl.ds(n * size, size)

    have = set()
    for n, (row, d) in enumerate(tail_blocks(rows, width)):
        i, k = row - rows + width, row + d - rows
        left[pl.ds(i * half, half), block(k)] = own_tail[n]
        have.add((i, k))
    for i in range(width):
        for k in range(width):
            if (i, k) not in have:
                left[pl.ds(i * half, half), block(k)] = jnp.zeros((half, size), BF16)
    for n, (k, d) in enumerate(head_blocks(width)):
        below[pl.ds(k * size + mine, half), block(k + d)] = mine_ref[n]
        below[pl.ds(k * size + other, half), block(k + d)] = other_ref[n]
        if d:
            below[block(k + d), block(k)] = below[block(k), block(k + d)].T
    square = jnp.dot(left[...], below[...], preferred_element_type=F32)
    finish(dims, reach_ref, flag_ref, square, rows - width, rows, copies, jobs, held, out_ref, out_sems)


def per_device(hamiltonian, bounds, block_reach, branch_flags):
    rows, offsets, half, size = hamiltonian.shape
    width = offsets - 1
    dims = (rows, width, half, size)
    halo = len(head_blocks(width))
    count = lax.axis_size("row")
    down = [(i, i + 1) for i in range(count - 1)]
    up = [(i + 1, i) for i in range(count - 1)]
    swap = [(0, 1), (1, 0)]
    packed = jax.ShapeDtypeStruct((halo, half, size), BF16)
    whole = jax.ShapeDtypeStruct(hamiltonian.shape, F32)

    current, tail, head, part = pl.pallas_call(
        functools.partial(start_kernel, dims),
        out_shape=(
            jax.ShapeDtypeStruct(hamiltonian.shape, BF16), packed, packed, jax.ShapeDtypeStruct((8, size), F32),
        ),
        in_specs=[HBM, HBM, HBM, HBM],
        out_specs=(VMEM, VMEM, VMEM, VMEM),
        scratch_shapes=[
            pltpu.VMEM(hamiltonian.shape, F32),
            pltpu.SMEM(block_reach.shape, jnp.int32),
            pltpu.SMEM(bounds.shape, F32),
            pltpu.SMEM(branch_flags.shape, jnp.int32),
            pltpu.SemaphoreType.DMA((rows,)),
            pltpu.SemaphoreType.DMA((3,)),
        ],
        compiler_params=pltpu.CompilerParams(vmem_limit_bytes=58 * MIB),
        cost_estimate=SMALL,
        name="start",
    )(block_reach, bounds, branch_flags, hamiltonian)
    swapped = lax.ppermute(current, "col", swap)
    below_mine = lax.ppermute(head, "row", up)
    above_mine = lax.ppermute(tail, "row", down)
    parts = lax.all_gather(part, ("row", "col"))

    base = pl.pallas_call(
        functools.partial(inner_kernel, dims),
        out_shape=whole,
        in_specs=[SMEM, SMEM, VMEM, VMEM],
        out_specs=VMEM,
        scratch_shapes=[
            pltpu.VMEM(((rows + width) * size, (rows + width) * size), BF16),
            pltpu.VMEM((rows * half, (rows + width) * size), BF16),
        ],
        compiler_params=pltpu.CompilerParams(vmem_limit_bytes=40 * MIB),
        cost_estimate=SMALL,
        name="inner",
    )(block_reach, branch_flags, current, swapped)

    square = pltpu.VMEM((width * size, width * size), BF16)
    strip = pltpu.VMEM((width * half, width * size), BF16)
    rest = [
        pltpu.VMEM((halo, half, size), F32),
        pltpu.SemaphoreType.DMA((width,)),
        pltpu.SemaphoreType.DMA((width,)),
    ]
    params = pltpu.CompilerParams(vmem_limit_bytes=16 * MIB)
    base, below_mine = lax.optimization_barrier((base, below_mine))
    below_other = lax.ppermute(below_mine, "col", swap)
    base = pl.pallas_call(
        functools.partial(below_kernel, dims),
        out_shape=whole,
        in_specs=[SMEM, SMEM, VMEM, VMEM, VMEM, ANY],
        out_specs=ANY,
        input_output_aliases={5: 0},
        scratch_shapes=[square, strip] + rest,
        compiler_params=params,
        cost_estimate=SMALL,
        name="below",
    )(block_reach, branch_flags, below_mine, below_other, tail, base)
    base, above_mine = lax.optimization_barrier((base, above_mine))
    above_other = lax.ppermute(above_mine, "col", swap)
    density = pl.pallas_call(
        functools.partial(above_kernel, dims),
        out_shape=whole,
        in_specs=[SMEM, SMEM, VMEM, VMEM, ANY],
        out_specs=ANY,
        input_output_aliases={4: 0},
        scratch_shapes=[square, square, strip] + rest,
        compiler_params=params,
        cost_estimate=SMALL,
        name="above",
    )(block_reach, branch_flags, above_mine, above_other, base)
    occupancy = jnp.sum(parts) / (count * rows * size)
    return density, occupancy.reshape(1)


def solution(mesh):
    placed = (
        P(("groups", "row"), None, "col", None),
        P("groups"),
        P(("groups", "row")),
        P("groups"),
    )
    return jax.shard_map(
        per_device,
        mesh=mesh,
        in_specs=placed,
        out_specs=(P(("groups", "row"), None, "col", None), P("groups")),
        check_vma=False,
    )
```

time: 75.9 us -> 57.5 us (0.76)
  blocking collectives: 32.2 us -> 20.7 us
  waiting for transfers between devices: 14.3 us -> 9.91 us
  local copies, waits for them, and re-layouts: 3.09 us -> 1.35 us
    psum x1 -> x0, blocking collectives: 32.2 us -> none  [per_device(): trace = lax.psum(part, ('row', 'col'))]
    all_gather x0 -> x1, blocking collectives: none -> 20.7 us  [per_device(): parts = lax.all_gather(part, ('row', 'col'))]
    ppermute x1, waiting for transfers between devices: 6.75 us -> 3.1 us  [per_device(): below_mine = lax.ppermute(head, 'row', up)]
    ppermute x1, waiting for transfers between devices: 7.55 us -> 5.13 us  [per_device(): above_mine = lax.ppermute(tail, 'row', down)]
    unnamed x12 -> x8, local copies, waits for them, and re-layouts: 3.09 us -> 1.35 us
    ppermute x1, waiting for transfers between devices: 0.01 us -> 1.68 us  [per_device(): swapped = lax.ppermute(current, 'col', swap)]
  transfers between devices with their start and end apart: 5 -> 5, of which waited for: 2 -> 3; matrix products, arithmetic and copies ran while one was open for 1% -> 1% of each run, Pallas kernels for 9% -> 15%
where the time goes in v2:
time: 57.5 us; the launch traced here: 57.2 us
  blocking collectives  20.7 us (36%)
  Pallas kernels  15.1 us (26%)
  waiting for transfers between devices  9.91 us (17%)
  starting transfers between devices  6.36 us (11%)
  between operations  3.14 us (5%)
  local copies, waits for them, and re-layouts  1.35 us (2%)
  other arithmetic  0.61 us (1%)
    all_gather x1, blocking collectives, per_device(): parts = lax.all_gather(part, ('row', 'col'))  20.7 us
    pallas_call x1, Pallas kernels, per_device(): pl.pallas_call(functools.partial(inner_kernel, dims), out_shape=whole, in...  5.94 us
    ppermute x1, waiting for transfers between devices, per_device(): above_mine = lax.ppermute(tail, 'row', down)  5.13 us
    ppermute x1, starting transfers between devices, per_device(): above_mine = lax.ppermute(tail, 'row', down)  4.56 us
    pallas_call x1, Pallas kernels, per_device(): pl.pallas_call(functools.partial(start_kernel, dims), out_shape=(jax.Shap...  3.47 us
    ppermute x1, waiting for transfers between devices, per_device(): below_mine = lax.ppermute(head, 'row', up)  3.1 us
    pallas_call x1, Pallas kernels, per_device(): pl.pallas_call(functools.partial(below_kernel, dims), out_shape=whole, in...  2.92 us
    pallas_call x1, Pallas kernels, per_device(): pl.pallas_call(functools.partial(above_kernel, dims), out_shape=whole, in...  2.81 us
  transfers between devices with their start and end apart: 5, of which 3 were waited for; matrix products, arithmetic and copies ran while one was open for 1% of the time, Pallas kernels for 15%

profile of v2, /device:TPU:0, one launch (start us, length us, event | category | flops | bytes accessed | tf_op | source)
XLA Modules:
  0.0 57.2 jit_solution(7471907091445950544)
XLA Ops:
  0.6 0.0 copy-start.2
  1.3 3.5 %start.1 = (bf16[12,7,64,128]{3,2,1,0:T(8,128)(2,1)}, bf16[21,64,128]{2,1,0:T(8,128)(2,1)}, bf16[21,64,128]{2,1,0:T(8,128)(2,1)}, f32[8,128]{1,0:T(8,128)}) custom-call(s32[12]{0:T(128)} %reach_ref.5, f32[2]{0:T(128)} %bounds_hbm.1, s32[1]{0:T(128)S(6)} %copy.10.flag_hbm.flag_ref, f32[12,7,64,128]{3,2,1,0:T(8,128)} %h_hbm.1), custom_call_target="tpu_custom_call" | custom-call | flops 1 | bytes 1 | tf_op jit(solution)/shard_map/start/pallas_call | solution.py:270
  4.8 0.5 collective-permute-start
  5.3 1.3 %collective-permute-start.1 = (bf16[21,64,128]{2,1,0:T(8,128)(2,1)}, bf16[21,64,128]{2,1,0:T(8,128)(2,1)S(1)}, u32[]{:S(2)}, u32[]{:S(2)}) collective-permute-start(bf16[21,64,128]{2,1,0:T(8,128)(2,1)} %get-tuple-element.11), channel_id=1, source_target_pairs={{2,0},{4,2},{6,4},{8,6},{10,8},{12,10},{14,12},{3,1},{5,3},{7,5},{... | collective-permute-start | bytes 1032200 | tf_op jit(solution)/shard_map/ppermute | solution.py:290
  6.6 1.7 %collective-permute-done.other_ref = bf16[12,7,64,128]{3,2,1,0:T(8,128)(2,1)S(1)} collective-permute-done((bf16[12,7,64,128]{3,2,1,0:T(8,128)(2,1)}, bf16[12,7,64,128]{3,2,1,0:T(8,128)(2,1)S(1)}, u32[]{:S(2)}, u32[]{:S(2)}) %collective-permute-start) | collective-permute-done | bytes 1376288 | tf_op jit(solution)/shard_map/ppermute | solution.py:289
  8.3 0.0 copy-done.2
  8.3 0.0 copy-start
  8.3 1.3 %copy-done = bf16[12,7,64,128]{3,2,1,0:T(8,128)(2,1)S(1)} copy-done((bf16[12,7,64,128]{3,2,1,0:T(8,128)(2,1)S(1)}, bf16[12,7,64,128]{3,2,1,0:T(8,128)(2,1)}, u32[]{:S(2)}) %copy-start) | copy-done | bytes 1376280
  9.6 0.0 copy-start.1
  9.6 5.9 %inner.1.base_ref = f32[12,7,64,128]{3,2,1,0:T(8,128)} custom-call(s32[12]{0:T(128)S(1)} %copy-done.2, s32[1]{0:T(128)S(6)} %copy.10.flag_hbm.flag_ref, bf16[12,7,64,128]{3,2,1,0:T(8,128)(2,1)S(1)} %copy-done, bf16[12,7,64,128]{3,2,1,0:T(8,128)(2,1)S(1)} %collective-permute-done.other_ref), custom_call_target="tpu_custom_call" | custom-call | flops 1 | bytes 1 | tf_op jit(solution)/shard_map/inner/pallas_call | solution.py:294
  15.5 3.1 %collective-permute-done.1.mine_ref = bf16[21,64,128]{2,1,0:T(8,128)(2,1)S(1)} collective-permute-done((bf16[21,64,128]{2,1,0:T(8,128)(2,1)}, bf16[21,64,128]{2,1,0:T(8,128)(2,1)S(1)}, u32[]{:S(2)}, u32[]{:S(2)}) %collective-permute-start.1) | collective-permute-done | bytes 344096 | tf_op jit(solution)/shard_map/ppermute | solution.py:290
  18.6 0.0 collective-permute-start.2
  18.6 0.0 copy-done.1
  18.6 0.0 copy-start.3
  18.7 4.6 %collective-permute-start.3 = (bf16[21,64,128]{2,1,0:T(8,128)(2,1)S(1)}, bf16[21,64,128]{2,1,0:T(8,128)(2,1)S(1)}, u32[]{:S(2)}, u32[]{:S(2)}) collective-permute-start(bf16[21,64,128]{2,1,0:T(8,128)(2,1)S(1)} %copy-done.1), channel_id=1, source_target_pairs={{0,2},{2,4},{4,6},{6,8},{8,10},{10,12},{12,14},{1,3},{3,5},{5,7},{... | collective-permute-start | bytes 1032200 | tf_op jit(solution)/shard_map/ppermute | solution.py:291
  23.2 0.0 collective-permute-done.2.other_ref
  23.2 2.9 %below.1.base_ref = f32[12,7,64,128]{3,2,1,0:T(8,128)} custom-call(s32[12]{0:T(128)S(1)} %copy-done.2, s32[1]{0:T(128)S(6)} %copy.10.flag_hbm.flag_ref, bf16[21,64,128]{2,1,0:T(8,128)(2,1)S(1)} %collective-permute-done.1.mine_ref, bf16[21,64,128]{2,1,0:T(8,128)(2,1)S(1)} %collective-permute-done.2.other_ref, ...), custom_call_target="tpu_custom_call", output_to_operand_aliasing={{}: (5, {})} | custom-call | flops 1 | bytes 1 | tf_op jit(solution)/shard_map/below/pallas_call | solution.py:318
  26.2 5.1 %collective-permute-done.3.mine_ref = bf16[21,64,128]{2,1,0:T(8,128)(2,1)S(1)} collective-permute-done((bf16[21,64,128]{2,1,0:T(8,128)(2,1)S(1)}, bf16[21,64,128]{2,1,0:T(8,128)(2,1)S(1)}, u32[]{:S(2)}, u32[]{:S(2)}) %collective-permute-start.3) | collective-permute-done | bytes 344096 | tf_op jit(solution)/shard_map/ppermute | solution.py:291
  31.3 0.0 collective-permute-start.4
  31.3 0.0 copy-done.3
  31.3 20.7 %all-gather = f32[128,128]{1,0:T(8,128)S(1)} all-gather(f32[8,128]{1,0:T(8,128)S(1)} %copy-done.3), channel_id=2, replica_groups=mesh['groups'=2,'row'=8,'col'=2] {'row','col'}, dimensions={0}, use_global_device_ids=true | all-gather | bytes 69632 | tf_op jit(solution)/shard_map/all_gather | solution.py:292
  52.0 0.6 %reduce_sum.9 = f32[]{:T(128)} reduce(f32[128,128]{1,0:T(8,128)S(1)} %all-gather, f32[]{:T(128)} %constant.1.clone.1), dimensions={0,1}, to_apply=%region_0.0 | reduce | flops 16383 | bytes 65544 | tf_op jit(solution)/shard_map/reduce_sum | solution.py:342
  53.2 0.0 collective-permute-done.4.other_ref
  53.3 2.8 %above.1 = f32[12,7,64,128]{3,2,1,0:T(8,128)} custom-call(s32[12]{0:T(128)S(1)} %copy-done.2, s32[1]{0:T(128)S(6)} %copy.10.flag_hbm.flag_ref, bf16[21,64,128]{2,1,0:T(8,128)(2,1)S(1)} %collective-permute-done.3.mine_ref, bf16[21,64,128]{2,1,0:T(8,128)(2,1)S(1)} %collective-permute-done.4.other_ref, ...), custom_call_target="tpu_custom_call", output_to_operand_aliasing={{}: (4, {})} | custom-call | flops 1 | bytes 1 | tf_op jit(solution)/shard_map/above/pallas_call | solution.py:331
Async XLA Ops:
  0.6 7.6 %copy-start.2 = (s32[12]{0:T(128)S(1)}, s32[12]{0:T(128)}, u32[]{:S(2)}) copy-start(s32[12]{0:T(128)} %reach_ref.5) | copy-start | bytes 148
  4.8 3.5 %collective-permute-start = (bf16[12,7,64,128]{3,2,1,0:T(8,128)(2,1)}, bf16[12,7,64,128]{3,2,1,0:T(8,128)(2,1)S(1)}, u32[]{:S(2)}, u32[]{:S(2)}) collective-permute-start(bf16[12,7,64,128]{3,2,1,0:T(8,128)(2,1)} %get-tuple-element.10.mine_ref), channel_id=1, source_target_pairs={{0,1},{1,0},{2,3},{3,2},{4,5},{5,4},{6,7},{7,6},{8,9},{9,8},{10,11... | collective-permute-start | bytes 4128776 | tf_op jit(solution)/shard_map/ppermute | solution.py:289
  5.3 13.3 %collective-permute-start.1 = (bf16[21,64,128]{2,1,0:T(8,128)(2,1)}, bf16[21,64,128]{2,1,0:T(8,128)(2,1)S(1)}, u32[]{:S(2)}, u32[]{:S(2)}) collective-permute-start(bf16[21,64,128]{2,1,0:T(8,128)(2,1)} %get-tuple-element.11), channel_id=1, source_target_pairs={{2,0},{4,2},{6,4},{8,6},{10,8},{12,10},{14,12},{3,1},{5,3},{7,5},{... | collective-permute-start | bytes 1032200 | tf_op jit(solution)/shard_map/ppermute | solution.py:290
  8.3 1.3 %copy-start = (bf16[12,7,64,128]{3,2,1,0:T(8,128)(2,1)S(1)}, bf16[12,7,64,128]{3,2,1,0:T(8,128)(2,1)}, u32[]{:S(2)}) copy-start(bf16[12,7,64,128]{3,2,1,0:T(8,128)(2,1)} %get-tuple-element.10.mine_ref) | copy-start | bytes 4128772
  9.6 9.0 %copy-start.1 = (bf16[21,64,128]{2,1,0:T(8,128)(2,1)S(1)}, bf16[21,64,128]{2,1,0:T(8,128)(2,1)}, u32[]{:S(2)}) copy-start(bf16[21,64,128]{2,1,0:T(8,128)(2,1)} %get-tuple-element.13.own_tail) | copy-start | bytes 1032196
  18.6 4.6 %collective-permute-start.2 = (bf16[21,64,128]{2,1,0:T(8,128)(2,1)S(1)}, bf16[21,64,128]{2,1,0:T(8,128)(2,1)S(1)}, u32[]{:S(2)}, u32[]{:S(2)}) collective-permute-start(bf16[21,64,128]{2,1,0:T(8,128)(2,1)S(1)} %collective-permute-done.1.mine_ref), channel_id=1, source_target_pairs={{0,1},{1,0},{2,3},{3,2},{4,5},{5,4},{6,7},{7,6},{8,9},{9,8},{10,11... | collective-permute-start | bytes 1032200 | tf_op jit(solution)/shard_map/ppermute | solution.py:317
  18.6 12.6 %copy-start.3 = (f32[8,128]{1,0:T(8,128)S(1)}, f32[8,128]{1,0:T(8,128)}, u32[]{:S(2)}) copy-start(f32[8,128]{1,0:T(8,128)} %get-tuple-element.17) | copy-start | bytes 12292
  18.7 12.6 %collective-permute-start.3 = (bf16[21,64,128]{2,1,0:T(8,128)(2,1)S(1)}, bf16[21,64,128]{2,1,0:T(8,128)(2,1)S(1)}, u32[]{:S(2)}, u32[]{:S(2)}) collective-permute-start(bf16[21,64,128]{2,1,0:T(8,128)(2,1)S(1)} %copy-done.1), channel_id=1, source_target_pairs={{0,2},{2,4},{4,6},{6,8},{8,10},{10,12},{12,14},{1,3},{3,5},{5,7},{... | collective-permute-start | bytes 1032200 | tf_op jit(solution)/shard_map/ppermute | solution.py:291
  31.3 22.0 %collective-permute-start.4 = (bf16[21,64,128]{2,1,0:T(8,128)(2,1)S(1)}, bf16[21,64,128]{2,1,0:T(8,128)(2,1)S(1)}, u32[]{:S(2)}, u32[]{:S(2)}) collective-permute-start(bf16[21,64,128]{2,1,0:T(8,128)(2,1)S(1)} %collective-permute-done.3.mine_ref), channel_id=1, source_target_pairs={{0,1},{1,0},{2,3},{3,2},{4,5},{5,4},{6,7},{7,6},{8,9},{9,8},{10,11... | collective-permute-start | bytes 1032200 | tf_op jit(solution)/shard_map/ppermute | solution.py:330

commit v3 on v1

--- a/solution.py
+++ b/solution.py
@@ -10,9 +10,11 @@
 SMEM = pl.BlockSpec(memory_space=pltpu.SMEM)
 VMEM = pl.BlockSpec(memory_space=pltpu.VMEM)
 ANY = pl.BlockSpec(memory_space=pl.ANY)
+HBM = pl.BlockSpec(memory_space=pltpu.HBM)
 F32 = jnp.float32
 BF16 = jnp.bfloat16
 MIB = 1 << 20
+SMALL = pl.CostEstimate(flops=1, bytes_accessed=1, transcendentals=0)
 
 
 def tail_blocks(rows, width):
@@ -50,63 +52,59 @@
     return lax.broadcasted_iota(jnp.int32, (half, size), 1) == rows
 
 
-def pack_kernel(dims, reach_ref, bounds_ref, h_ref, tail_ref, head_ref, buf, sems):
+def start_kernel(
+    dims, reach_hbm, bounds_hbm, flag_hbm, h_hbm, x_hbm, tail_hbm, head_hbm, part_ref, h_ref, x_ref, tail_ref, head_ref,
+    reach_ref, bounds_ref, flag_ref, in_sems, small_sems, x_sems, halo_sems,
+):
     rows, width, half, size = dims
     first_row = lax.axis_index("row") * rows
     total_rows = lax.axis_size("row") * rows
+    small = [
+        pltpu.make_async_copy(src, dst, small_sems.at[n])
+        for n, (src, dst) in enumerate(((reach_hbm, reach_ref), (bounds_hbm, bounds_ref), (flag_hbm, flag_ref)))
+    ]
+    large = [pltpu.make_async_copy(h_hbm.at[i], h_ref.at[i], in_sems.at[i]) for i in range(rows)]
+    for copy in small + large:
+        copy.start()
     on_diag = diag_mask(half, size)
-    jobs = [(out, run) for out, blocks in ((tail_ref, tail_blocks(rows, width)), (head_ref, head_blocks(width)))
-            for run in runs(blocks)]
-    copies = []
-    at = 0
-    for n, (out, (row, d, count, place)) in enumerate(jobs):
-        copy = pltpu.make_async_copy(h_ref.at[row, pl.ds(d, count)], buf.at[pl.ds(at, count)], sems.at[n])
-        copy.start()
-        copies.append((copy, at))
-        at += count
-    for (out, (row, d, count, place)), (copy, at) in zip(jobs, copies):
-        copy.wait()
-        for e in range(count):
-            kept = is_kept(reach_ref, row, d + e, first_row, total_rows)
-            out[place + e] = start_block(buf[at + e], d + e, kept, bounds_ref, on_diag)
-
-
-def start_kernel(dims, reach_ref, bounds_ref, flag_ref, h_ref, after_ref, x_ref, part_ref):
-    rows, width, half, size = dims
-    first_row = lax.axis_index("row") * rows
-    total_rows = lax.axis_size("row") * rows
-    on_diag = diag_mask(half, size)
-    count = h_ref.shape[0]
-    step = pl.program_id(0)
+    halos = ((head_ref, head_hbm, head_blocks(width)), (tail_ref, tail_hbm, tail_blocks(rows, width)))
 
     def fold(block):
         return jnp.sum(block.reshape(half // 8, 8, size), axis=0)
 
+    for copy in small:
+        copy.wait()
     diag = jnp.zeros((8, size), F32)
     once = jnp.zeros((8, size), F32)
     twice = jnp.zeros((8, size), F32)
-    for e in range(count):
-        row = step * count + e
+    out = []
+    for row in range(rows):
+        large[row].wait()
         for d in range(width + 1):
             kept = is_kept(reach_ref, row, d, first_row, total_rows)
-            x = start_block(h_ref[e, d], d, kept, bounds_ref, on_diag)
-            x_ref[e, d] = x
+            x = start_block(h_ref[row, d], d, kept, bounds_ref, on_diag)
+            x_ref[row, d] = x
+            for ref, _, blocks in halos:
+                if (row, d) in blocks:
+                    ref[blocks.index((row, d))] = x
             wide = x.astype(F32)
             if d == 0:
                 diag = diag + fold(jnp.where(on_diag, wide, 0.0))
                 once = once + fold(wide * wide)
             else:
                 twice = twice + fold(wide * wide)
+        out.append(pltpu.make_async_copy(x_ref.at[row], x_hbm.at[row], x_sems.at[row]))
+        out[-1].start()
+        for n, (ref, hbm, blocks) in enumerate(halos):
+            for at, _, count, place in runs(blocks):
+                if at == row:
+                    piece = pl.ds(place, count)
+                    out.append(pltpu.make_async_copy(ref.at[piece], hbm.at[piece], halo_sems.at[n, place]))
+                    out[-1].start()
     norm = once + 2.0 * twice
-    part = jnp.where(flag_ref[0] == 1, norm, 2.0 * diag - norm)
-
-    @pl.when(step == 0)
-    def _():
-        part_ref[...] = part
-
-    @pl.when(step > 0)
-    def _():
-        part_ref[...] += part
+    part_ref[...] = jnp.where(flag_ref[0] == 1, norm, 2.0 * diag - norm)
+    for copy in out:
+        copy.wait()
 
 
 def strips(rows, width):
@@ -120,7 +118,8 @@
     return out
 
 
-def inner_kernel(dims, reach_ref, flag_ref, mine_ref, other_ref, out_ref, full, left):
+def inner_kernel(dims, reach_ref, flag_ref, mine_ref, other_ref, part_ref, got_ref, out_ref, sum_ref, full, left):
+    sum_ref[...] = part_ref[...] + got_ref[...]
     rows, width, half, size = dims
     column = lax.axis_index("col")
     first_row = lax.axis_index("row") * rows
@@ -252,59 +251,63 @@
     up = [(i + 1, i) for i in range(count - 1)]
     swap = [(0, 1), (1, 0)]
     packed = jax.ShapeDtypeStruct((halo, half, size), BF16)
-    runs_count = 2 * width
-
-    tail, head = pl.pallas_call(
-        functools.partial(pack_kernel, dims),
-        out_shape=(packed, packed),
-        in_specs=[SMEM, SMEM, ANY],
+    whole = jax.ShapeDtypeStruct(hamiltonian.shape, F32)
+
+    current, tail, head, part = pl.pallas_call(
+        functools.partial(start_kernel, dims),
+        out_shape=(
+            jax.ShapeDtypeStruct(hamiltonian.shape, BF16), packed, packed, jax.ShapeDtypeStruct((8, size), F32),
+        ),
+        in_specs=[HBM, HBM, HBM, HBM],
+        out_specs=(HBM, HBM, HBM, VMEM),
+        scratch_shapes=[
+            pltpu.VMEM(hamiltonian.shape, F32),
+            pltpu.VMEM(hamiltonian.shape, BF16),
+            pltpu.VMEM((halo, half, size), BF16),
+            pltpu.VMEM((halo, half, size), BF16),
+            pltpu.SMEM(block_reach.shape, jnp.int32),
+            pltpu.SMEM(bounds.shape, F32),
+            pltpu.SMEM(branch_flags.shape, jnp.int32),
+            pltpu.SemaphoreType.DMA((rows,)),
+            pltpu.SemaphoreType.DMA((3,)),
+            pltpu.SemaphoreType.DMA((rows,)),
+            pltpu.SemaphoreType.DMA((2, halo)),
+        ],
+        compiler_params=pltpu.CompilerParams(vmem_limit_bytes=58 * MIB),
+        cost_estimate=SMALL,
+        name="start",
+    )(block_reach, bounds, branch_flags, hamiltonian)
+    swapped = lax.ppermute(current, "col", swap)
+    got = lax.ppermute(part, "col", swap)
+    below_mine = lax.ppermute(head, "row", up)
+    above_mine = lax.ppermute(tail, "row", down)
+
+    base, part = pl.pallas_call(
+        functools.partial(inner_kernel, dims),
+        out_shape=(whole, jax.ShapeDtypeStruct((8, size), F32)),
+        in_specs=[SMEM, SMEM, VMEM, VMEM, VMEM, VMEM],
         out_specs=(VMEM, VMEM),
-        scratch_shapes=[pltpu.VMEM((2 * halo, half, size), F32), pltpu.SemaphoreType.DMA((runs_count,))],
-        compiler_params=pltpu.CompilerParams(vmem_limit_bytes=8 * MIB),
-        name="pack",
-    )(block_reach, bounds, hamiltonian)
-    above_mine = lax.ppermute(tail, "row", down)
-    below_mine = lax.ppermute(head, "row", up)
-
-    per_step = 3 if rows % 3 == 0 else 1
-    current, part = pl.pallas_call(
-        functools.partial(start_kernel, dims),
-        grid=(rows // per_step,),
-        out_shape=(jax.ShapeDtypeStruct(hamiltonian.shape, BF16), jax.ShapeDtypeStruct((8, size), F32)),
-        in_specs=[SMEM, SMEM, SMEM, pl.BlockSpec((per_step, offsets, half, size), lambda s: (s, 0, 0, 0)), ANY],
-        out_specs=(
-            pl.BlockSpec((per_step, offsets, half, size), lambda s: (s, 0, 0, 0)),
-            pl.BlockSpec((8, size), lambda s: (0, 0)),
-        ),
-        compiler_params=pltpu.CompilerParams(vmem_limit_bytes=16 * MIB),
-        cost_estimate=pl.CostEstimate(flops=4 * hamiltonian.size, bytes_accessed=6 * hamiltonian.size, transcendentals=0),
-        name="start",
-    )(block_reach, bounds, branch_flags, hamiltonian, tail)
-    swapped = lax.ppermute(current, "col", swap)
-    trace = lax.psum(part, ("row", "col"))
-
-    products = rows * sum(2 * width + 1 - d for d in range(width + 1))
-    base = pl.pallas_call(
-        functools.partial(inner_kernel, dims),
-        out_shape=jax.ShapeDtypeStruct(hamiltonian.shape, F32),
-        in_specs=[SMEM, SMEM, VMEM, VMEM],
-        out_specs=VMEM,
         scratch_shapes=[
             pltpu.VMEM(((rows + width) * size, (rows + width) * size), BF16),
             pltpu.VMEM((rows * half, (rows + width) * size), BF16),
         ],
-        compiler_params=pltpu.CompilerParams(vmem_limit_bytes=40 * MIB),
-        cost_estimate=pl.CostEstimate(
-            flops=2 * products * half * size * size, bytes_accessed=8 * hamiltonian.size, transcendentals=0
-        ),
+        compiler_params=pltpu.CompilerParams(vmem_limit_bytes=58 * MIB),
+        cost_estimate=SMALL,
         name="inner",
-    )(block_reach, branch_flags, current, swapped)
-
+    )(block_reach, branch_flags, current, swapped, part, got)
+
+    far = count
+    while far > 2:
+        far //= 2
+        part = part + lax.ppermute(part, "row", [(i, i ^ far) for i in range(count)])
+
+    base, below_mine, above_mine, part = lax.optimization_barrier((base, below_mine, above_mine, part))
+    below_other = lax.ppermute(below_mine, "col", swap)
     above_other = lax.ppermute(above_mine, "col", swap)
-    below_other = lax.ppermute(below_mine, "col", swap)
+    part = part + lax.ppermute(part, "row", [(i, i ^ 1) for i in range(count)])
     density = pl.pallas_call(
         functools.partial(halo_kernel, dims),
-        out_shape=jax.ShapeDtypeStruct(hamiltonian.shape, F32),
+        out_shape=whole,
         in_specs=[SMEM, SMEM, VMEM, VMEM, VMEM, VMEM, VMEM, ANY],
         out_specs=ANY,
         input_output_aliases={7: 0},
@@ -315,13 +318,14 @@
             pltpu.VMEM((width * size, width * size), BF16),
             pltpu.VMEM((width * half, width * size), BF16),
             pltpu.VMEM((2 * halo, half, size), F32),
-            pltpu.SemaphoreType.DMA((runs_count,)),
-            pltpu.SemaphoreType.DMA((runs_count,)),
+            pltpu.SemaphoreType.DMA((2 * width,)),
+            pltpu.SemaphoreType.DMA((2 * width,)),
         ],
         compiler_params=pltpu.CompilerParams(vmem_limit_bytes=24 * MIB),
+        cost_estimate=SMALL,
         name="halo",
     )(block_reach, branch_flags, above_mine, above_other, below_mine, below_other, tail, base)
-    occupancy = jnp.sum(trace) / (count * rows * size)
+    occupancy = jnp.sum(part) / (count * rows * size)
     return density, occupancy.reshape(1)
 
 

time: 75.9 us -> 43.5 us (0.57)
  blocking collectives: 32.2 us -> 0 us
  starting transfers between devices: 6.94 us -> 15.5 us
  waiting for transfers between devices: 14.3 us -> 6.39 us
  local copies, waits for them, and re-layouts: 3.09 us -> 1.67 us
    psum x1 -> x0, blocking collectives: 32.2 us -> none  [per_device(): trace = lax.psum(part, ('row', 'col'))]
    ppermute x0 -> x4, starting transfers between devices: none -> 7.87 us  [the longest x2 4.98 us: per_device(): lax.ppermute(part, 'row', [(i, i ^ far) for i in range(count)])]
    ppermute x1, waiting for transfers between devices: 7.55 us -> 0.01 us  [per_device(): above_mine = lax.ppermute(tail, 'row', down)]
    ppermute x1, waiting for transfers between devices: 6.75 us -> 0.01 us  [per_device(): below_mine = lax.ppermute(head, 'row', up)]
    ppermute x0 -> x4, waiting for transfers between devices: none -> 6.38 us  [the longest x2 3.49 us: per_device(): lax.ppermute(part, 'row', [(i, i ^ far) for i in range(count)])]
    unnamed x12 -> x8, local copies, waits for them, and re-layouts: 3.09 us -> 1.67 us
    pallas_call x4 -> x3, Pallas kernels: 15.3 us -> 15.2 us  [the longest x1 7.12 us: per_device(): pl.pallas_call(functools.partial(inner_kernel, dims), out_shape=(whole, j...]
  transfers between devices with their start and end apart: 5 -> 9, of which waited for: 2 -> 4; matrix products, arithmetic and copies ran while one was open for 1% -> 3% of each run, Pallas kernels for 9% -> 16%
where the time goes in v3:
time: 43.5 us; the launch traced here: 43.2 us
  starting transfers between devices  15.5 us (36%)
  Pallas kernels  15.2 us (35%)
  waiting for transfers between devices  6.39 us (15%)
  between operations  3.16 us (7%)
  local copies, waits for them, and re-layouts  1.67 us (4%)
  other arithmetic  1.29 us (3%)
    pallas_call x1, Pallas kernels, per_device(): pl.pallas_call(functools.partial(inner_kernel, dims), out_shape=(whole, j...  7.12 us
    ppermute x1, starting transfers between devices, per_device(): above_mine = lax.ppermute(tail, 'row', down)  5.22 us
    ppermute x2, starting transfers between devices, per_device(): lax.ppermute(part, 'row', [(i, i ^ far) for i in range(count)])  4.98 us
    pallas_call x1, Pallas kernels, per_device(): pl.pallas_call(functools.partial(halo_kernel, dims), out_shape=whole, in_...  4.17 us
    pallas_call x1, Pallas kernels, per_device(): pl.pallas_call(functools.partial(start_kernel, dims), out_shape=(jax.Shap...  3.93 us
    ppermute x2, waiting for transfers between devices, per_device(): lax.ppermute(part, 'row', [(i, i ^ far) for i in range(count)])  3.49 us
    ppermute x1, starting transfers between devices, per_device(): part = part + lax.ppermute(part, 'row', [(i, i ^ 1) for i in range(count)])  2.75 us
    unnamed x8, local copies, waits for them, and re-layouts  1.67 us
  transfers between devices with their start and end apart: 9, of which 4 were waited for; matrix products, arithmetic and copies ran while one was open for 3% of the time, Pallas kernels for 16%

profile of v3, /device:TPU:0, one launch (start us, length us, event | category | flops | bytes accessed | tf_op | source)
XLA Modules:
  0.0 43.2 jit_solution(9371874633042543414)
XLA Ops:
  1.3 0.0 copy-start.1
  1.3 3.9 %start.1 = (bf16[12,7,64,128]{3,2,1,0:T(8,128)(2,1)}, bf16[21,64,128]{2,1,0:T(8,128)(2,1)}, bf16[21,64,128]{2,1,0:T(8,128)(2,1)}, f32[8,128]{1,0:T(8,128)}) custom-call(s32[12]{0:T(128)} %reach_ref.3, f32[2]{0:T(128)} %bounds_hbm.1, s32[1]{0:T(128)S(6)} %copy.8.flag_hbm.flag_ref, f32[12,7,64,128]{3,2,1,0:T(8,128)} %h_hbm.1), custom_call_target="tpu_custom_call" | custom-call | flops 1 | bytes 1 | tf_op jit(solution)/shard_map/start/pallas_call | solution.py:256
  5.2 0.0 copy-start
  5.2 0.5 %collective-permute-start = (bf16[12,7,64,128]{3,2,1,0:T(8,128)(2,1)}, bf16[12,7,64,128]{3,2,1,0:T(8,128)(2,1)S(1)}, u32[]{:S(2)}, u32[]{:S(2)}) collective-permute-start(bf16[12,7,64,128]{3,2,1,0:T(8,128)(2,1)} %get-tuple-element.12.mine_ref), channel_id=1, source_target_pairs={{0,1},{1,0},{2,3},{3,2},{4,5},{5,4},{6,7},{7,6},{8,9},{9,8},{10,11... | collective-permute-start | bytes 4128776 | tf_op jit(solution)/shard_map/ppermute | solution.py:280
  5.8 1.3 %collective-permute-start.2 = (bf16[21,64,128]{2,1,0:T(8,128)(2,1)}, bf16[21,64,128]{2,1,0:T(8,128)(2,1)S(1)}, u32[]{:S(2)}, u32[]{:S(2)}) collective-permute-start(bf16[21,64,128]{2,1,0:T(8,128)(2,1)} %get-tuple-element.15), channel_id=1, source_target_pairs={{2,0},{4,2},{6,4},{8,6},{10,8},{12,10},{14,12},{3,1},{5,3},{7,5},{... | collective-permute-start | bytes 1032200 | tf_op jit(solution)/shard_map/ppermute | solution.py:282
  7.0 5.2 %collective-permute-start.3 = (bf16[21,64,128]{2,1,0:T(8,128)(2,1)}, bf16[21,64,128]{2,1,0:T(8,128)(2,1)S(1)}, u32[]{:S(2)}, u32[]{:S(2)}) collective-permute-start(bf16[21,64,128]{2,1,0:T(8,128)(2,1)} %get-tuple-element.16.own_tail), channel_id=1, source_target_pairs={{0,2},{2,4},{4,6},{6,8},{8,10},{10,12},{12,14},{1,3},{3,5},{5,7},{... | collective-permute-start | bytes 1032200 | tf_op jit(solution)/shard_map/ppermute | solution.py:283
  12.3 0.1 collective-permute-start.1
  12.4 1.3 %collective-permute-done.1.got_ref = f32[8,128]{1,0:T(8,128)S(1)} collective-permute-done((f32[8,128]{1,0:T(8,128)}, f32[8,128]{1,0:T(8,128)S(1)}, u32[]{:S(2)}, u32[]{:S(2)}) %collective-permute-start.1) | collective-permute-done | bytes 4128 | tf_op jit(solution)/shard_map/ppermute | solution.py:281
  13.7 0.0 copy-start.3
  13.7 0.0 collective-permute-done.other_ref
  13.7 0.6 %copy-done.3 = f32[8,128]{1,0:T(8,128)} copy-done((f32[8,128]{1,0:T(8,128)}, f32[8,128]{1,0:T(8,128)S(1)}, u32[]{:S(2)}) %copy-start.3) | copy-done | bytes 4120
  14.3 0.0 copy-start.2
  14.3 1.1 %copy-done.2 = bf16[12,7,64,128]{3,2,1,0:T(8,128)(2,1)} copy-done((bf16[12,7,64,128]{3,2,1,0:T(8,128)(2,1)}, bf16[12,7,64,128]{3,2,1,0:T(8,128)(2,1)S(1)}, u32[]{:S(2)}) %copy-start.2) | copy-done | bytes 1376280
  15.4 7.1 %inner.1 = (f32[12,7,64,128]{3,2,1,0:T(8,128)}, f32[8,128]{1,0:T(8,128)}) custom-call(s32[12]{0:T(128)} %reach_ref.3, s32[1]{0:T(128)S(6)} %copy.8.flag_hbm.flag_ref, bf16[12,7,64,128]{3,2,1,0:T(8,128)(2,1)} %get-tuple-element.12.mine_ref, bf16[12,7,64,128]{3,2,1,0:T(8,128)(2,1)} %copy-done.2, f32[8,128]{1,0:T(8,128)} %get-tuple-element.13.part_ref, ...), custom_call_target="tpu_custom_call" | custom-call | flops 1 | bytes 1 | tf_op jit(solution)/shard_map/inner/pallas_call | solution.py:285
  22.5 3.1 %collective-permute-start.4 = (f32[8,128]{1,0:T(8,128)}, f32[8,128]{1,0:T(8,128)S(1)}, u32[]{:S(2)}, u32[]{:S(2)}) collective-permute-start(f32[8,128]{1,0:T(8,128)} %get-tuple-element.17), channel_id=1, source_target_pairs={{0,8},{2,10},{4,12},{6,14},{8,0},{10,2},{12,4},{14,6},{1,9},{3,11}... | collective-permute-start | bytes 12296 | tf_op jit(solution)/shard_map/ppermute | solution.py:302
  25.6 1.8 %collective-permute-done.4 = f32[8,128]{1,0:T(8,128)S(1)} collective-permute-done((f32[8,128]{1,0:T(8,128)}, f32[8,128]{1,0:T(8,128)S(1)}, u32[]{:S(2)}, u32[]{:S(2)}) %collective-permute-start.4) | collective-permute-done | bytes 4128 | tf_op jit(solution)/shard_map/ppermute | solution.py:302
  27.4 0.7 %add.9 = f32[8,128]{1,0:T(8,128)S(1)} add(f32[8,128]{1,0:T(8,128)} %get-tuple-element.17, f32[8,128]{1,0:T(8,128)S(1)} %collective-permute-done.4) | non-fusion elementwise | flops 1024 | bytes 12288 | tf_op jit(solution)/shard_map/add | solution.py:302
  28.1 1.9 %collective-permute-start.5 = (f32[8,128]{1,0:T(8,128)S(1)}, f32[8,128]{1,0:T(8,128)S(1)}, u32[]{:S(2)}, u32[]{:S(2)}) collective-permute-start(f32[8,128]{1,0:T(8,128)S(1)} %add.9), channel_id=1, source_target_pairs={{0,4},{2,6},{4,0},{6,2},{8,12},{10,14},{12,8},{14,10},{1,5},{3,7},... | collective-permute-start | bytes 12296 | tf_op jit(solution)/shard_map/ppermute | solution.py:302
  30.0 1.7 %collective-permute-done.5 = f32[8,128]{1,0:T(8,128)S(1)} collective-permute-done((f32[8,128]{1,0:T(8,128)S(1)}, f32[8,128]{1,0:T(8,128)S(1)}, u32[]{:S(2)}, u32[]{:S(2)}) %collective-permute-start.5) | collective-permute-done | bytes 4128 | tf_op jit(solution)/shard_map/ppermute | solution.py:302
  31.7 0.0 collective-permute-done.2.below_mine
  31.7 0.0 collective-permute-done.3.above_mine
  31.7 0.1 collective-permute-start.6
  31.8 0.5 %collective-permute-start.7 = (bf16[21,64,128]{2,1,0:T(8,128)(2,1)S(1)}, bf16[21,64,128]{2,1,0:T(8,128)(2,1)S(1)}, u32[]{:S(2)}, u32[]{:S(2)}) collective-permute-start(bf16[21,64,128]{2,1,0:T(8,128)(2,1)S(1)} %collective-permute-done.2.below_mine), channel_id=1, source_target_pairs={{0,1},{1,0},{2,3},{3,2},{4,5},{5,4},{6,7},{7,6},{8,9},{9,8},{10,11... | collective-permute-start | bytes 1032200 | tf_op jit(solution)/shard_map/ppermute | solution.py:305
  32.3 2.8 %collective-permute-start.8 = (f32[8,128]{1,0:T(8,128)S(1)}, f32[8,128]{1,0:T(8,128)S(1)}, u32[]{:S(2)}, u32[]{:S(2)}) collective-permute-start(f32[8,128]{1,0:T(8,128)S(1)} %add.10), channel_id=1, source_target_pairs={{0,2},{2,0},{4,6},{6,4},{8,10},{10,8},{12,14},{14,12},{1,3},{3,1},... | collective-permute-start | bytes 12296 | tf_op jit(solution)/shard_map/ppermute | solution.py:307
  35.0 1.6 %collective-permute-done.8 = f32[8,128]{1,0:T(8,128)S(1)} collective-permute-done((f32[8,128]{1,0:T(8,128)S(1)}, f32[8,128]{1,0:T(8,128)S(1)}, u32[]{:S(2)}, u32[]{:S(2)}) %collective-permute-start.8) | collective-permute-done | bytes 4128 | tf_op jit(solution)/shard_map/ppermute | solution.py:307
  36.6 0.6 %add_reduce_fusion = f32[]{:T(128)} fusion(f32[8,128]{1,0:T(8,128)S(1)} %add.10, f32[8,128]{1,0:T(8,128)S(1)} %collective-permute-done.8), kind=kLoop, calls=%fused_computation | loop fusion | flops 2047 | bytes 8196 | tf_op jit(solution)/shard_map/reduce_sum | solution.py:328
  37.8 0.0 collective-permute-done.6.above_other
  37.9 0.0 collective-permute-done.7.below_other
  37.9 0.0 copy-done.1
  37.9 0.0 copy-done
  37.9 4.2 %halo.1 = f32[12,7,64,128]{3,2,1,0:T(8,128)} custom-call(s32[12]{0:T(128)S(1)} %copy-done.1, s32[1]{0:T(128)S(6)} %copy.8.flag_hbm.flag_ref, bf16[21,64,128]{2,1,0:T(8,128)(2,1)S(1)} %collective-permute-done.3.above_mine, bf16[21,64,128]{2,1,0:T(8,128)(2,1)S(1)} %collective-permute-done.6.above_other, ...), custom_call_target="tpu_custom_call", output_to_operand_aliasing={{}: (7, {})} | custom-call | flops 1 | bytes 1 | tf_op jit(solution)/shard_map/halo/pallas_call | solution.py:308
  (1 shorter events, 0.0 us)
Async XLA Ops:
  1.3 36.6 %copy-start.1 = (s32[12]{0:T(128)S(1)}, s32[12]{0:T(128)}, u32[]{:S(2)}) copy-start(s32[12]{0:T(128)} %reach_ref.3) | copy-start | bytes 148
  5.2 32.6 %copy-start = (bf16[21,64,128]{2,1,0:T(8,128)(2,1)S(1)}, bf16[21,64,128]{2,1,0:T(8,128)(2,1)}, u32[]{:S(2)}) copy-start(bf16[21,64,128]{2,1,0:T(8,128)(2,1)} %get-tuple-element.16.own_tail) | copy-start | bytes 1032196
  5.2 8.5 %collective-permute-start = (bf16[12,7,64,128]{3,2,1,0:T(8,128)(2,1)}, bf16[12,7,64,128]{3,2,1,0:T(8,128)(2,1)S(1)}, u32[]{:S(2)}, u32[]{:S(2)}) collective-permute-start(bf16[12,7,64,128]{3,2,1,0:T(8,128)(2,1)} %get-tuple-element.12.mine_ref), channel_id=1, source_target_pairs={{0,1},{1,0},{2,3},{3,2},{4,5},{5,4},{6,7},{7,6},{8,9},{9,8},{10,11... | collective-permute-start | bytes 4128776 | tf_op jit(solution)/shard_map/ppermute | solution.py:280
  5.8 25.9 %collective-permute-start.2 = (bf16[21,64,128]{2,1,0:T(8,128)(2,1)}, bf16[21,64,128]{2,1,0:T(8,128)(2,1)S(1)}, u32[]{:S(2)}, u32[]{:S(2)}) collective-permute-start(bf16[21,64,128]{2,1,0:T(8,128)(2,1)} %get-tuple-element.15), channel_id=1, source_target_pairs={{2,0},{4,2},{6,4},{8,6},{10,8},{12,10},{14,12},{3,1},{5,3},{7,5},{... | collective-permute-start | bytes 1032200 | tf_op jit(solution)/shard_map/ppermute | solution.py:282
  7.0 24.6 %collective-permute-start.3 = (bf16[21,64,128]{2,1,0:T(8,128)(2,1)}, bf16[21,64,128]{2,1,0:T(8,128)(2,1)S(1)}, u32[]{:S(2)}, u32[]{:S(2)}) collective-permute-start(bf16[21,64,128]{2,1,0:T(8,128)(2,1)} %get-tuple-element.16.own_tail), channel_id=1, source_target_pairs={{0,2},{2,4},{4,6},{6,8},{8,10},{10,12},{12,14},{1,3},{3,5},{5,7},{... | collective-permute-start | bytes 1032200 | tf_op jit(solution)/shard_map/ppermute | solution.py:283
  12.3 1.4 %collective-permute-start.1 = (f32[8,128]{1,0:T(8,128)}, f32[8,128]{1,0:T(8,128)S(1)}, u32[]{:S(2)}, u32[]{:S(2)}) collective-permute-start(f32[8,128]{1,0:T(8,128)} %get-tuple-element.13.part_ref), channel_id=1, source_target_pairs={{0,1},{1,0},{2,3},{3,2},{4,5},{5,4},{6,7},{7,6},{8,9},{9,8},{10,11... | collective-permute-start | bytes 12296 | tf_op jit(solution)/shard_map/ppermute | solution.py:281
  13.7 0.6 %copy-start.3 = (f32[8,128]{1,0:T(8,128)}, f32[8,128]{1,0:T(8,128)S(1)}, u32[]{:S(2)}) copy-start(f32[8,128]{1,0:T(8,128)S(1)} %collective-permute-done.1.got_ref) | copy-start | bytes 12292
  14.3 1.1 %copy-start.2 = (bf16[12,7,64,128]{3,2,1,0:T(8,128)(2,1)}, bf16[12,7,64,128]{3,2,1,0:T(8,128)(2,1)S(1)}, u32[]{:S(2)}) copy-start(bf16[12,7,64,128]{3,2,1,0:T(8,128)(2,1)S(1)} %collective-permute-done.other_ref) | copy-start | bytes 4128772
  22.5 4.9 %collective-permute-start.4 = (f32[8,128]{1,0:T(8,128)}, f32[8,128]{1,0:T(8,128)S(1)}, u32[]{:S(2)}, u32[]{:S(2)}) collective-permute-start(f32[8,128]{1,0:T(8,128)} %get-tuple-element.17), channel_id=1, source_target_pairs={{0,8},{2,10},{4,12},{6,14},{8,0},{10,2},{12,4},{14,6},{1,9},{3,11}... | collective-permute-start | bytes 12296 | tf_op jit(solution)/shard_map/ppermute | solution.py:302
  28.1 3.6 %collective-permute-start.5 = (f32[8,128]{1,0:T(8,128)S(1)}, f32[8,128]{1,0:T(8,128)S(1)}, u32[]{:S(2)}, u32[]{:S(2)}) collective-permute-start(f32[8,128]{1,0:T(8,128)S(1)} %add.9), channel_id=1, source_target_pairs={{0,4},{2,6},{4,0},{6,2},{8,12},{10,14},{12,8},{14,10},{1,5},{3,7},... | collective-permute-start | bytes 12296 | tf_op jit(solution)/shard_map/ppermute | solution.py:302
  31.7 6.2 %collective-permute-start.6 = (bf16[21,64,128]{2,1,0:T(8,128)(2,1)S(1)}, bf16[21,64,128]{2,1,0:T(8,128)(2,1)S(1)}, u32[]{:S(2)}, u32[]{:S(2)}) collective-permute-start(bf16[21,64,128]{2,1,0:T(8,128)(2,1)S(1)} %collective-permute-done.3.above_mine), channel_id=1, source_target_pairs={{0,1},{1,0},{2,3},{3,2},{4,5},{5,4},{6,7},{7,6},{8,9},{9,8},{10,11... | collective-permute-start | bytes 1032200 | tf_op jit(solution)/shard_map/ppermute | solution.py:306
  31.8 6.1 %collective-permute-start.7 = (bf16[21,64,128]{2,1,0:T(8,128)(2,1)S(1)}, bf16[21,64,128]{2,1,0:T(8,128)(2,1)S(1)}, u32[]{:S(2)}, u32[]{:S(2)}) collective-permute-start(bf16[21,64,128]{2,1,0:T(8,128)(2,1)S(1)} %collective-permute-done.2.below_mine), channel_id=1, source_target_pairs={{0,1},{1,0},{2,3},{3,2},{4,5},{5,4},{6,7},{7,6},{8,9},{9,8},{10,11... | collective-permute-start | bytes 1032200 | tf_op jit(solution)/shard_map/ppermute | solution.py:305
  32.3 4.3 %collective-permute-start.8 = (f32[8,128]{1,0:T(8,128)S(1)}, f32[8,128]{1,0:T(8,128)S(1)}, u32[]{:S(2)}, u32[]{:S(2)}) collective-permute-start(f32[8,128]{1,0:T(8,128)S(1)} %add.10), channel_id=1, source_target_pairs={{0,2},{2,0},{4,6},{6,4},{8,10},{10,8},{12,14},{14,12},{1,3},{3,1},... | collective-permute-start | bytes 12296 | tf_op jit(solution)/shard_map/ppermute | solution.py:307

commit v4 on v2

--- a/solution.py
+++ b/solution.py
@@ -14,6 +14,7 @@
 F32 = jnp.float32
 BF16 = jnp.bfloat16
 MIB = 1 << 20
+LINES = 16
 SMALL = pl.CostEstimate(flops=1, bytes_accessed=1, transcendentals=0)
 
 
@@ -53,41 +54,35 @@
 
 
 def start_kernel(
-    dims, reach_hbm, bounds_hbm, flag_hbm, h_hbm, x_ref, tail_ref, head_ref, part_ref, h_ref, reach_ref, bounds_ref,
-    flag_ref, row_sems, sems,
+    dims, reach_hbm, bounds_hbm, flag_hbm, h_hbm, x_ref, near_ref, far_ref, part_ref, h_ref, reach_ref, bounds_ref,
+    flag_ref, in_sems, small_sems,
 ):
     rows, width, half, size = dims
     first_row = lax.axis_index("row") * rows
     total_rows = lax.axis_size("row") * rows
     small = [
-        pltpu.make_async_copy(src, dst, sems.at[n])
+        pltpu.make_async_copy(src, dst, small_sems.at[n])
         for n, (src, dst) in enumerate(((reach_hbm, reach_ref), (bounds_hbm, bounds_ref), (flag_hbm, flag_ref)))
     ]
-    large = [pltpu.make_async_copy(h_hbm.at[i], h_ref.at[i], row_sems.at[i]) for i in range(rows)]
+    large = [pltpu.make_async_copy(h_hbm.at[i], h_ref.at[i], in_sems.at[i]) for i in range(rows)]
     for copy in small + large:
         copy.start()
     on_diag = diag_mask(half, size)
-    place = {block: (tail_ref, n) for n, block in enumerate(tail_blocks(rows, width))}
-    heads = {block: (head_ref, n) for n, block in enumerate(head_blocks(width))}
 
     def fold(block):
-        return jnp.sum(block.reshape(half // 8, 8, size), axis=0)
+        return jnp.sum(block.reshape(half // LINES, LINES, size), axis=0)
 
     for copy in small:
         copy.wait()
-    diag = jnp.zeros((8, size), F32)
-    once = jnp.zeros((8, size), F32)
-    twice = jnp.zeros((8, size), F32)
+    diag = jnp.zeros((LINES, size), F32)
+    once = jnp.zeros((LINES, size), F32)
+    twice = jnp.zeros((LINES, size), F32)
     for row in range(rows):
         large[row].wait()
         for d in range(width + 1):
             kept = is_kept(reach_ref, row, d, first_row, total_rows)
             x = start_block(h_ref[row, d], d, kept, bounds_ref, on_diag)
             x_ref[row, d] = x
-            for table in (place, heads):
-                if (row, d) in table:
-                    ref, n = table[row, d]
-                    ref[n] = x
             wide = x.astype(F32)
             if d == 0:
                 diag = diag + fold(jnp.where(on_diag, wide, 0.0))
@@ -95,7 +90,22 @@
             else:
                 twice = twice + fold(wide * wide)
     norm = once + 2.0 * twice
-    part_ref[...] = jnp.where(flag_ref[0] == 1, norm, 2.0 * diag - norm)
+    part = jnp.where(flag_ref[0] == 1, norm, 2.0 * diag - norm)
+    part_ref[...] = part
+
+    tails, heads = tail_blocks(rows, width), head_blocks(width)
+    for parity, near, far in ((0, tails, heads), (1, heads, tails)):
+
+        @pl.when(lax.axis_index("row") % 2 == parity)
+        def _(near=near, far=far):
+            for ref, blocks in ((near_ref, near), (far_ref, far)):
+                for n, (row, d) in enumerate(blocks):
+                    ref[n] = x_ref[row, d]
+
+    for n in range(half // LINES):
+        term = part.astype(BF16) if n < 3 else jnp.zeros((LINES, size), BF16)
+        near_ref[len(heads), pl.ds(n * LINES, LINES)] = term
+        part = part - term.astype(F32)
 
 
 def strips(rows, width):
@@ -109,7 +119,7 @@
     return out
 
 
-def inner_kernel(dims, reach_ref, flag_ref, mine_ref, other_ref, out_ref, full, left):
+def inner_kernel(dims, reach_ref, flag_ref, mine_ref, other_ref, out_hbm, out_ref, full, left, sems):
     rows, width, half, size = dims
     column = lax.axis_index("col")
     first_row = lax.axis_index("row") * rows
@@ -161,6 +171,10 @@
                 kept = is_kept(reach_ref, i, d, first_row, total_rows)
                 part = square[(i - i_lo) * half : (i - i_lo + 1) * half, n * size : (n + 1) * size]
                 out_ref[i, d] = part * jnp.where(kept, sign, 0.0) + twice * mine_ref[i, d].astype(F32)
+                if d == width:
+                    pltpu.make_async_copy(out_ref.at[i], out_hbm.at[i], sems.at[i]).start()
+    for i in range(rows):
+        pltpu.make_async_copy(out_ref.at[i], out_hbm.at[i], sems.at[i]).wait()
 
 
 def fetch(base_ref, held, jobs, sems):
@@ -197,9 +211,7 @@
     return pl.multiple_of(column * half, half), pl.multiple_of((1 - column) * half, half)
 
 
-def above_kernel(
-    dims, reach_ref, flag_ref, mine_ref, other_ref, base_ref, out_ref, above, above_t, left, held, in_sems, out_sems
-):
+def add_above(dims, reach_ref, flag_ref, mine_ref, other_ref, base_ref, out_ref, whole, turned, left, held, in_sems, out_sems):
     rows, width, half, size = dims
     mine, other = halves(dims)
     jobs = runs(head_blocks(width))
@@ -211,24 +223,22 @@
     have = set()
     for n, (row, d) in enumerate(tail_blocks(rows, width)):
         k, j = row - rows + width, row + d - rows
-        above[pl.ds(k * size + mine, half), block(j)] = mine_ref[n]
-        above[pl.ds(k * size + other, half), block(j)] = other_ref[n]
+        whole[pl.ds(k * size + mine, half), block(j)] = mine_ref[n]
+        whole[pl.ds(k * size + other, half), block(j)] = other_ref[n]
         have.add((k, j))
     for k in range(width):
         for j in range(width):
             if (k, j) in have:
-                above_t[block(j), block(k)] = above[block(k), block(j)].T
-                left[pl.ds(j * half, half), block(k)] = above_t[pl.ds(j * size + mine, half), block(k)]
+                turned[block(j), block(k)] = whole[block(k), block(j)].T
+                left[pl.ds(j * half, half), block(k)] = turned[pl.ds(j * size + mine, half), block(k)]
             else:
-                above[block(k), block(j)] = jnp.zeros((size, size), BF16)
+                whole[block(k), block(j)] = jnp.zeros((size, size), BF16)
                 left[pl.ds(j * half, half), block(k)] = jnp.zeros((half, size), BF16)
-    square = jnp.dot(left[...], above[...], preferred_element_type=F32)
+    square = jnp.dot(left[...], whole[...], preferred_element_type=F32)
     finish(dims, reach_ref, flag_ref, square, 0, 0, copies, jobs, held, out_ref, out_sems)
 
 
-def below_kernel(
-    dims, reach_ref, flag_ref, mine_ref, other_ref, own_tail, base_ref, out_ref, below, left, held, in_sems, out_sems
-):
+def add_below(dims, reach_ref, flag_ref, mine_ref, other_ref, sent_ref, base_ref, out_ref, whole, left, held, in_sems, out_sems):
     rows, width, half, size = dims
     mine, other = halves(dims)
     jobs = runs(tail_blocks(rows, width))
@@ -240,19 +250,37 @@
     have = set()
     for n, (row, d) in enumerate(tail_blocks(rows, width)):
         i, k = row - rows + width, row + d - rows
-        left[pl.ds(i * half, half), block(k)] = own_tail[n]
+        left[pl.ds(i * half, half), block(k)] = sent_ref[n]
         have.add((i, k))
     for i in range(width):
         for k in range(width):
             if (i, k) not in have:
                 left[pl.ds(i * half, half), block(k)] = jnp.zeros((half, size), BF16)
     for n, (k, d) in enumerate(head_blocks(width)):
-        below[pl.ds(k * size + mine, half), block(k + d)] = mine_ref[n]
-        below[pl.ds(k * size + other, half), block(k + d)] = other_ref[n]
+        whole[pl.ds(k * size + mine, half), block(k + d)] = mine_ref[n]
+        whole[pl.ds(k * size + other, half), block(k + d)] = other_ref[n]
         if d:
-            below[block(k + d), block(k)] = below[block(k), block(k + d)].T
-    square = jnp.dot(left[...], below[...], preferred_element_type=F32)
+            whole[block(k + d), block(k)] = whole[block(k), block(k + d)].T
+    square = jnp.dot(left[...], whole[...], preferred_element_type=F32)
     finish(dims, reach_ref, flag_ref, square, rows - width, rows, copies, jobs, held, out_ref, out_sems)
+
+
+def halo_kernel(
+    dims, reach_ref, flag_ref, near_mine, near_other, near_sent, far_mine, far_other, far_sent, trace_ref, got_ref, base_ref,
+    out_ref, sum_ref, whole, turned, left, held, whole2, left2, held2, sems,
+):
+    rows, width, half, size = dims
+    sum_ref[...] = jnp.broadcast_to(jnp.sum(trace_ref[...] + got_ref[...]), sum_ref.shape)
+
+    for parity, above, below in (
+        (0, (far_mine, far_other), (near_mine, near_other, near_sent)),
+        (1, (near_mine, near_other), (far_mine, far_other, far_sent)),
+    ):
+
+        @pl.when(lax.axis_index("row") % 2 == parity)
+        def _(above=above, below=below):
+            add_above(dims, reach_ref, flag_ref, *above, base_ref, out_ref, whole, turned, left, held, sems.at[0], sems.at[1])
+            add_below(dims, reach_ref, flag_ref, *below, base_ref, out_ref, whole2, left2, held2, sems.at[2], sems.at[3])
 
 
 def per_device(hamiltonian, bounds, block_reach, branch_flags):
@@ -261,16 +289,18 @@
     dims = (rows, width, half, size)
     halo = len(head_blocks(width))
     count = lax.axis_size("row")
-    down = [(i, i + 1) for i in range(count - 1)]
-    up = [(i + 1, i) for i in range(count - 1)]
+    near_pairs = [(i, i ^ 1) for i in range(count)]
+    far_pairs = [(i, j) for i in range(count) for j in [((i + 1) ^ 1) - 1] if 0 <= j < count]
     swap = [(0, 1), (1, 0)]
-    packed = jax.ShapeDtypeStruct((halo, half, size), BF16)
     whole = jax.ShapeDtypeStruct(hamiltonian.shape, F32)
 
-    current, tail, head, part = pl.pallas_call(
+    current, near, far, part = pl.pallas_call(
         functools.partial(start_kernel, dims),
         out_shape=(
-            jax.ShapeDtypeStruct(hamiltonian.shape, BF16), packed, packed, jax.ShapeDtypeStruct((8, size), F32),
+            jax.ShapeDtypeStruct(hamiltonian.shape, BF16),
+            jax.ShapeDtypeStruct((halo + 1, half, size), BF16),
+            jax.ShapeDtypeStruct((halo, half, size), BF16),
+            jax.ShapeDtypeStruct((LINES, size), F32),
         ),
         in_specs=[HBM, HBM, HBM, HBM],
         out_specs=(VMEM, VMEM, VMEM, VMEM),
@@ -287,60 +317,52 @@
         name="start",
     )(block_reach, bounds, branch_flags, hamiltonian)
     swapped = lax.ppermute(current, "col", swap)
-    below_mine = lax.ppermute(head, "row", up)
-    above_mine = lax.ppermute(tail, "row", down)
-    parts = lax.all_gather(part, ("row", "col"))
+    near_mine = lax.ppermute(near, "row", near_pairs)
+    far_mine = lax.ppermute(far, "row", far_pairs)
 
     base = pl.pallas_call(
         functools.partial(inner_kernel, dims),
         out_shape=whole,
         in_specs=[SMEM, SMEM, VMEM, VMEM],
-        out_specs=VMEM,
+        out_specs=HBM,
         scratch_shapes=[
+            pltpu.VMEM(hamiltonian.shape, F32),
             pltpu.VMEM(((rows + width) * size, (rows + width) * size), BF16),
             pltpu.VMEM((rows * half, (rows + width) * size), BF16),
+            pltpu.SemaphoreType.DMA((rows,)),
         ],
-        compiler_params=pltpu.CompilerParams(vmem_limit_bytes=40 * MIB),
+        compiler_params=pltpu.CompilerParams(vmem_limit_bytes=24 * MIB),
         cost_estimate=SMALL,
         name="inner",
     )(block_reach, branch_flags, current, swapped)
 
+    base, near_mine = lax.optimization_barrier((base, near_mine))
+    terms = near_mine[halo].astype(F32).reshape(half // LINES, LINES, size)
+    trace = part + (terms[0] + terms[1] + terms[2])
+    far_step = count // 2
+    while far_step > 1:
+        trace = trace + lax.ppermute(trace, "row", [(i, i ^ far_step) for i in range(count)])
+        far_step //= 2
+
+    base, near_mine, far_mine, trace = lax.optimization_barrier((base, near_mine, far_mine, trace))
+    near_other = lax.ppermute(near_mine, "col", swap)
+    far_other = lax.ppermute(far_mine, "col", swap)
+    got = lax.ppermute(trace, "col", swap)
     square = pltpu.VMEM((width * size, width * size), BF16)
     strip = pltpu.VMEM((width * half, width * size), BF16)
-    rest = [
-        pltpu.VMEM((halo, half, size), F32),
-        pltpu.SemaphoreType.DMA((width,)),
-        pltpu.SemaphoreType.DMA((width,)),
-    ]
-    params = pltpu.CompilerParams(vmem_limit_bytes=16 * MIB)
-    base, below_mine = lax.optimization_barrier((base, below_mine))
-    below_other = lax.ppermute(below_mine, "col", swap)
-    base = pl.pallas_call(
-        functools.partial(below_kernel, dims),
-        out_shape=whole,
-        in_specs=[SMEM, SMEM, VMEM, VMEM, VMEM, ANY],
-        out_specs=ANY,
-        input_output_aliases={5: 0},
-        scratch_shapes=[square, strip] + rest,
-        compiler_params=params,
+    held = pltpu.VMEM((halo, half, size), F32)
+    density, total = pl.pallas_call(
+        functools.partial(halo_kernel, dims),
+        out_shape=(whole, jax.ShapeDtypeStruct((8, size), F32)),
+        in_specs=[SMEM, SMEM] + [VMEM] * 8 + [ANY],
+        out_specs=(ANY, VMEM),
+        input_output_aliases={10: 0},
+        scratch_shapes=[square, square, strip, held, square, strip, held, pltpu.SemaphoreType.DMA((4, width))],
+        compiler_params=pltpu.CompilerParams(vmem_limit_bytes=24 * MIB),
         cost_estimate=SMALL,
-        name="below",
-    )(block_reach, branch_flags, below_mine, below_other, tail, base)
-    base, above_mine = lax.optimization_barrier((base, above_mine))
-    above_other = lax.ppermute(above_mine, "col", swap)
-    density = pl.pallas_call(
-        functools.partial(above_kernel, dims),
-        out_shape=whole,
-        in_specs=[SMEM, SMEM, VMEM, VMEM, ANY],
-        out_specs=ANY,
-        input_output_aliases={4: 0},
-        scratch_shapes=[square, square, strip] + rest,
-        compiler_params=params,
-        cost_estimate=SMALL,
-        name="above",
-    )(block_reach, branch_flags, above_mine, above_other, base)
-    occupancy = jnp.sum(parts) / (count * rows * size)
-    return density, occupancy.reshape(1)
+        name="halo",
+    )(block_reach, branch_flags, near_mine, near_other, near, far_mine, far_other, far, trace, got, base)
+    return density, total[0, :1] / (count * rows * size)
 
 
 def solution(mesh):

time: 57.5 us -> 43.1 us (0.75)
  blocking collectives: 20.7 us -> 0 us
  starting transfers between devices: 6.36 us -> 9.77 us
  waiting for transfers between devices: 9.91 us -> 13.2 us
  other arithmetic: 0.61 us -> 0.02 us
    all_gather x1 -> x0, blocking collectives: 20.7 us -> none  [per_device(): parts = lax.all_gather(part, ('row', 'col'))]
    ppermute x4 -> x7, waiting for transfers between devices: 8.23 us -> 13.2 us  [the longest x1 8.23 us: per_device(): near_mine = lax.ppermute(near, 'row', near_pairs)]
    ppermute x4 -> x7, starting transfers between devices: 5.84 us -> 9.25 us  [the longest x2 5.4 us: per_device(): lax.ppermute(trace, 'row', [(i, i ^ far_step) for i in range(count)])]
    ppermute x1, waiting for transfers between devices: 1.68 us -> 0.01 us  [per_device(): swapped = lax.ppermute(current, 'col', swap)]
    reduce_sum x1 -> x0, other arithmetic: 0.61 us -> none  [per_device(): occupancy = jnp.sum(parts) / (count * rows * size)]
    pallas_call x2 -> x1, Pallas kernels: 5.73 us -> 5.72 us  [per_device(): pl.pallas_call(functools.partial(halo_kernel, dims), out_shape=(whole, ja...]
    unnamed x8 -> x10, local copies, waits for them, and re-layouts: 1.35 us -> 1.35 us
  transfers between devices with their start and end apart: 5 -> 8, of which waited for: 3 -> 4; matrix products, arithmetic and copies ran while one was open for 1% -> 0% of each run, Pallas kernels for 15% -> 13%
where the time goes in v4:
time: 43.1 us; the launch traced here: 42.9 us
  Pallas kernels  14.8 us (34%)
  waiting for transfers between devices  13.2 us (31%)
  starting transfers between devices  9.77 us (23%)
  between operations  3.16 us (7%)
  local copies, waits for them, and re-layouts  1.86 us (4%)
    ppermute x1, waiting for transfers between devices, per_device(): near_mine = lax.ppermute(near, 'row', near_pairs)  8.23 us
    pallas_call x1, Pallas kernels, per_device(): pl.pallas_call(functools.partial(halo_kernel, dims), out_shape=(whole, ja...  5.72 us
    pallas_call x1, Pallas kernels, per_device(): pl.pallas_call(functools.partial(inner_kernel, dims), out_shape=whole, in...  5.69 us
    ppermute x2, starting transfers between devices, per_device(): lax.ppermute(trace, 'row', [(i, i ^ far_step) for i in range(count)])  5.4 us
    pallas_call x1, Pallas kernels, per_device(): pl.pallas_call(functools.partial(start_kernel, dims), out_shape=(jax.Shap...  3.44 us
    ppermute x2, waiting for transfers between devices, per_device(): lax.ppermute(trace, 'row', [(i, i ^ far_step) for i in range(count)])  3.4 us
    ppermute x1, starting transfers between devices, per_device(): near_mine = lax.ppermute(near, 'row', near_pairs)  2.6 us
    ppermute x1, waiting for transfers between devices, per_device(): got = lax.ppermute(trace, 'col', swap)  1.6 us
  transfers between devices with their start and end apart: 8, of which 4 were waited for; matrix products, arithmetic and copies ran while one was open for 0% of the time, Pallas kernels for 13%

profile of v4, /device:TPU:0, one launch (start us, length us, event | category | flops | bytes accessed | tf_op | source)
XLA Modules:
  0.0 42.9 jit_solution(5366664001123965647)
XLA Ops:
  0.6 0.0 copy-start.3
  1.3 3.4 %start.1 = (bf16[12,7,64,128]{3,2,1,0:T(8,128)(2,1)}, bf16[22,64,128]{2,1,0:T(8,128)(2,1)}, bf16[21,64,128]{2,1,0:T(8,128)(2,1)}, f32[16,128]{1,0:T(8,128)}) custom-call(s32[12]{0:T(128)} %reach_ref.3, f32[2]{0:T(128)} %bounds_hbm.1, s32[1]{0:T(128)S(6)} %copy.8.flag_hbm.flag_ref, f32[12,7,64,128]{3,2,1,0:T(8,128)} %h_hbm.1), custom_call_target="tpu_custom_call" | custom-call | flops 1 | bytes 1 | tf_op jit(solution)/shard_map/start/pallas_call | solution.py:297
  4.7 0.5 %collective-permute-start = (bf16[12,7,64,128]{3,2,1,0:T(8,128)(2,1)}, bf16[12,7,64,128]{3,2,1,0:T(8,128)(2,1)S(1)}, u32[]{:S(2)}, u32[]{:S(2)}) collective-permute-start(bf16[12,7,64,128]{3,2,1,0:T(8,128)(2,1)} %get-tuple-element.14.mine_ref), channel_id=1, source_target_pairs={{0,1},{1,0},{2,3},{3,2},{4,5},{5,4},{6,7},{7,6},{8,9},{9,8},{10,11... | collective-permute-start | bytes 4128776 | tf_op jit(solution)/shard_map/ppermute | solution.py:319
  5.3 2.6 %collective-permute-start.1 = (bf16[22,64,128]{2,1,0:T(8,128)(2,1)}, bf16[22,64,128]{2,1,0:T(8,128)(2,1)S(1)}, u32[]{:S(2)}, u32[]{:S(2)}) collective-permute-start(bf16[22,64,128]{2,1,0:T(8,128)(2,1)} %get-tuple-element.15.near_sent), channel_id=1, source_target_pairs={{0,2},{2,0},{4,6},{6,4},{8,10},{10,8},{12,14},{14,12},{1,3},{3,1},... | collective-permute-start | bytes 1081352 | tf_op jit(solution)/shard_map/ppermute | solution.py:320
  7.9 0.7 %collective-permute-start.2 = (bf16[21,64,128]{2,1,0:T(8,128)(2,1)}, bf16[21,64,128]{2,1,0:T(8,128)(2,1)S(1)}, u32[]{:S(2)}, u32[]{:S(2)}) collective-permute-start(bf16[21,64,128]{2,1,0:T(8,128)(2,1)} %get-tuple-element.18.far_sent), channel_id=1, source_target_pairs={{2,4},{4,2},{6,8},{8,6},{10,12},{12,10},{3,5},{5,3},{7,9},{9,7},{1... | collective-permute-start | bytes 1032200 | tf_op jit(solution)/shard_map/ppermute | solution.py:321
  8.5 0.0 collective-permute-done.other_ref
  8.6 0.0 copy-done.3
  8.6 0.0 copy-start
  8.6 1.3 %copy-done = bf16[12,7,64,128]{3,2,1,0:T(8,128)(2,1)S(1)} copy-done((bf16[12,7,64,128]{3,2,1,0:T(8,128)(2,1)S(1)}, bf16[12,7,64,128]{3,2,1,0:T(8,128)(2,1)}, u32[]{:S(2)}) %copy-start) | copy-done | bytes 1376280
  9.9 0.0 copy-start.4
  9.9 0.0 copy-start.1
  9.9 0.0 copy-start.2
  9.9 5.7 %inner.1.base_ref = f32[12,7,64,128]{3,2,1,0:T(8,128)} custom-call(s32[12]{0:T(128)S(1)} %copy-done.3, s32[1]{0:T(128)S(6)} %copy.8.flag_hbm.flag_ref, bf16[12,7,64,128]{3,2,1,0:T(8,128)(2,1)S(1)} %copy-done, bf16[12,7,64,128]{3,2,1,0:T(8,128)(2,1)S(1)} %collective-permute-done.other_ref), custom_call_target="tpu_custom_call" | custom-call | flops 1 | bytes 1 | tf_op jit(solution)/shard_map/inner/pallas_call | solution.py:323
  15.6 8.2 %collective-permute-done.1.near_mine = bf16[22,64,128]{2,1,0:T(8,128)(2,1)S(1)} collective-permute-done((bf16[22,64,128]{2,1,0:T(8,128)(2,1)}, bf16[22,64,128]{2,1,0:T(8,128)(2,1)S(1)}, u32[]{:S(2)}, u32[]{:S(2)}) %collective-permute-start.1) | collective-permute-done | bytes 360480 | tf_op jit(solution)/shard_map/ppermute | solution.py:320
  23.8 0.0 copy-done.4
  23.9 3.5 %collective-permute-start.3 = (f32[16,128]{1,0:T(8,128)S(1)}, f32[16,128]{1,0:T(8,128)S(1)}, u32[]{:S(2)}, u32[]{:S(2)}) collective-permute-start(f32[16,128]{1,0:T(8,128)S(1)} %fusion.1), channel_id=1, source_target_pairs={{0,8},{2,10},{4,12},{6,14},{8,0},{10,2},{12,4},{14,6},{1,9},{3,11}... | collective-permute-start | bytes 24584 | tf_op jit(solution)/shard_map/ppermute | solution.py:344
  27.4 1.6 %collective-permute-done.3 = f32[16,128]{1,0:T(8,128)S(1)} collective-permute-done((f32[16,128]{1,0:T(8,128)S(1)}, f32[16,128]{1,0:T(8,128)S(1)}, u32[]{:S(2)}, u32[]{:S(2)}) %collective-permute-start.3) | collective-permute-done | bytes 8224 | tf_op jit(solution)/shard_map/ppermute | solution.py:344
  29.0 1.9 %collective-permute-start.4 = (f32[16,128]{1,0:T(8,128)S(1)}, f32[16,128]{1,0:T(8,128)S(1)}, u32[]{:S(2)}, u32[]{:S(2)}) collective-permute-start(f32[16,128]{1,0:T(8,128)S(1)} %add.23), channel_id=1, source_target_pairs={{0,4},{2,6},{4,0},{6,2},{8,12},{10,14},{12,8},{14,10},{1,5},{3,7},... | collective-permute-start | bytes 24584 | tf_op jit(solution)/shard_map/ppermute | solution.py:344
  30.9 1.8 %collective-permute-done.4 = f32[16,128]{1,0:T(8,128)S(1)} collective-permute-done((f32[16,128]{1,0:T(8,128)S(1)}, f32[16,128]{1,0:T(8,128)S(1)}, u32[]{:S(2)}, u32[]{:S(2)}) %collective-permute-start.4) | collective-permute-done | bytes 8224 | tf_op jit(solution)/shard_map/ppermute | solution.py:344
  32.7 0.0 collective-permute-done.2.far_mine
  32.7 0.0 collective-permute-start.5
  32.7 0.5 %collective-permute-start.6 = (bf16[21,64,128]{2,1,0:T(8,128)(2,1)S(1)}, bf16[21,64,128]{2,1,0:T(8,128)(2,1)S(1)}, u32[]{:S(2)}, u32[]{:S(2)}) collective-permute-start(bf16[21,64,128]{2,1,0:T(8,128)(2,1)S(1)} %collective-permute-done.2.far_mine), channel_id=1, source_target_pairs={{0,1},{1,0},{2,3},{3,2},{4,5},{5,4},{6,7},{7,6},{8,9},{9,8},{10,11... | collective-permute-start | bytes 1032200 | tf_op jit(solution)/shard_map/ppermute | solution.py:349
  33.2 0.1 collective-permute-start.7
  33.2 1.6 %collective-permute-done.7.got_ref = f32[16,128]{1,0:T(8,128)S(1)} collective-permute-done((f32[16,128]{1,0:T(8,128)S(1)}, f32[16,128]{1,0:T(8,128)S(1)}, u32[]{:S(2)}, u32[]{:S(2)}) %collective-permute-start.7) | collective-permute-done | bytes 8224 | tf_op jit(solution)/shard_map/ppermute | solution.py:350
  34.8 0.0 collective-permute-done.6.far_other
  34.8 0.0 collective-permute-done.5.near_other
  34.9 0.0 copy-done.1
  34.9 0.0 copy-done.2
  34.9 5.7 %halo.1 = (f32[12,7,64,128]{3,2,1,0:T(8,128)}, f32[8,128]{1,0:T(8,128)S(1)}) custom-call(s32[12]{0:T(128)S(1)} %copy-done.3, s32[1]{0:T(128)S(6)} %copy.8.flag_hbm.flag_ref, bf16[22,64,128]{2,1,0:T(8,128)(2,1)S(1)} %collective-permute-done.1.near_mine, bf16[22,64,128]{2,1,0:T(8,128)(2,1)S(1)} %collective-permute-done.5.near_other, ...), custom_call_target="tpu_custom_call", output_to_operand_aliasing={{0}: (10, {})} | custom-call | flops 1 | bytes 1 | tf_op jit(solution)/shard_map/halo/pallas_call | solution.py:354
  40.6 0.5 %slice.25 = f32[1,1]{1,0:T(1,128)} slice(f32[8,128]{1,0:T(8,128)S(1)} %get-tuple-element.25), slice={[0:1], [0:1]} | slice | bytes 8 | tf_op jit(solution)/shard_map/slice | solution.py:365
  (4 shorter events, 0.0 us)
Async XLA Ops:
  0.6 7.9 %copy-start.3 = (s32[12]{0:T(128)S(1)}, s32[12]{0:T(128)}, u32[]{:S(2)}) copy-start(s32[12]{0:T(128)} %reach_ref.3) | copy-start | bytes 148
  4.7 3.8 %collective-permute-start = (bf16[12,7,64,128]{3,2,1,0:T(8,128)(2,1)}, bf16[12,7,64,128]{3,2,1,0:T(8,128)(2,1)S(1)}, u32[]{:S(2)}, u32[]{:S(2)}) collective-permute-start(bf16[12,7,64,128]{3,2,1,0:T(8,128)(2,1)} %get-tuple-element.14.mine_ref), channel_id=1, source_target_pairs={{0,1},{1,0},{2,3},{3,2},{4,5},{5,4},{6,7},{7,6},{8,9},{9,8},{10,11... | collective-permute-start | bytes 4128776 | tf_op jit(solution)/shard_map/ppermute | solution.py:319
  5.3 18.6 %collective-permute-start.1 = (bf16[22,64,128]{2,1,0:T(8,128)(2,1)}, bf16[22,64,128]{2,1,0:T(8,128)(2,1)S(1)}, u32[]{:S(2)}, u32[]{:S(2)}) collective-permute-start(bf16[22,64,128]{2,1,0:T(8,128)(2,1)} %get-tuple-element.15.near_sent), channel_id=1, source_target_pairs={{0,2},{2,0},{4,6},{6,4},{8,10},{10,8},{12,14},{14,12},{1,3},{3,1},... | collective-permute-start | bytes 1081352 | tf_op jit(solution)/shard_map/ppermute | solution.py:320
  7.9 24.8 %collective-permute-start.2 = (bf16[21,64,128]{2,1,0:T(8,128)(2,1)}, bf16[21,64,128]{2,1,0:T(8,128)(2,1)S(1)}, u32[]{:S(2)}, u32[]{:S(2)}) collective-permute-start(bf16[21,64,128]{2,1,0:T(8,128)(2,1)} %get-tuple-element.18.far_sent), channel_id=1, source_target_pairs={{2,4},{4,2},{6,8},{8,6},{10,12},{12,10},{3,5},{5,3},{7,9},{9,7},{1... | collective-permute-start | bytes 1032200 | tf_op jit(solution)/shard_map/ppermute | solution.py:321
  8.6 1.3 %copy-start = (bf16[12,7,64,128]{3,2,1,0:T(8,128)(2,1)S(1)}, bf16[12,7,64,128]{3,2,1,0:T(8,128)(2,1)}, u32[]{:S(2)}) copy-start(bf16[12,7,64,128]{3,2,1,0:T(8,128)(2,1)} %get-tuple-element.14.mine_ref) | copy-start | bytes 4128772
  9.9 13.9 %copy-start.4 = (f32[16,128]{1,0:T(8,128)S(1)}, f32[16,128]{1,0:T(8,128)}, u32[]{:S(2)}) copy-start(f32[16,128]{1,0:T(8,128)} %get-tuple-element.19) | copy-start | bytes 24580
  9.9 24.9 %copy-start.1 = (bf16[22,64,128]{2,1,0:T(8,128)(2,1)S(1)}, bf16[22,64,128]{2,1,0:T(8,128)(2,1)}, u32[]{:S(2)}) copy-start(bf16[22,64,128]{2,1,0:T(8,128)(2,1)} %get-tuple-element.15.near_sent) | copy-start | bytes 1081348
  9.9 24.9 %copy-start.2 = (bf16[21,64,128]{2,1,0:T(8,128)(2,1)S(1)}, bf16[21,64,128]{2,1,0:T(8,128)(2,1)}, u32[]{:S(2)}) copy-start(bf16[21,64,128]{2,1,0:T(8,128)(2,1)} %get-tuple-element.18.far_sent) | copy-start | bytes 1032196
  23.9 5.1 %collective-permute-start.3 = (f32[16,128]{1,0:T(8,128)S(1)}, f32[16,128]{1,0:T(8,128)S(1)}, u32[]{:S(2)}, u32[]{:S(2)}) collective-permute-start(f32[16,128]{1,0:T(8,128)S(1)} %fusion.1), channel_id=1, source_target_pairs={{0,8},{2,10},{4,12},{6,14},{8,0},{10,2},{12,4},{14,6},{1,9},{3,11}... | collective-permute-start | bytes 24584 | tf_op jit(solution)/shard_map/ppermute | solution.py:344
  29.0 3.7 %collective-permute-start.4 = (f32[16,128]{1,0:T(8,128)S(1)}, f32[16,128]{1,0:T(8,128)S(1)}, u32[]{:S(2)}, u32[]{:S(2)}) collective-permute-start(f32[16,128]{1,0:T(8,128)S(1)} %add.23), channel_id=1, source_target_pairs={{0,4},{2,6},{4,0},{6,2},{8,12},{10,14},{12,8},{14,10},{1,5},{3,7},... | collective-permute-start | bytes 24584 | tf_op jit(solution)/shard_map/ppermute | solution.py:344
  32.7 2.2 %collective-permute-start.5 = (bf16[22,64,128]{2,1,0:T(8,128)(2,1)S(1)}, bf16[22,64,128]{2,1,0:T(8,128)(2,1)S(1)}, u32[]{:S(2)}, u32[]{:S(2)}) collective-permute-start(bf16[22,64,128]{2,1,0:T(8,128)(2,1)S(1)} %collective-permute-done.1.near_mine), channel_id=1, source_target_pairs={{0,1},{1,0},{2,3},{3,2},{4,5},{5,4},{6,7},{7,6},{8,9},{9,8},{10,11... | collective-permute-start | bytes 1081352 | tf_op jit(solution)/shard_map/ppermute | solution.py:348
  32.7 2.2 %collective-permute-start.6 = (bf16[21,64,128]{2,1,0:T(8,128)(2,1)S(1)}, bf16[21,64,128]{2,1,0:T(8,128)(2,1)S(1)}, u32[]{:S(2)}, u32[]{:S(2)}) collective-permute-start(bf16[21,64,128]{2,1,0:T(8,128)(2,1)S(1)} %collective-permute-done.2.far_mine), channel_id=1, source_target_pairs={{0,1},{1,0},{2,3},{3,2},{4,5},{5,4},{6,7},{7,6},{8,9},{9,8},{10,11... | collective-permute-start | bytes 1032200 | tf_op jit(solution)/shard_map/ppermute | solution.py:349
  33.2 1.7 %collective-permute-start.7 = (f32[16,128]{1,0:T(8,128)S(1)}, f32[16,128]{1,0:T(8,128)S(1)}, u32[]{:S(2)}, u32[]{:S(2)}) collective-permute-start(f32[16,128]{1,0:T(8,128)S(1)} %add.24.trace_ref), channel_id=1, source_target_pairs={{0,1},{1,0},{2,3},{3,2},{4,5},{5,4},{6,7},{7,6},{8,9},{9,8},{10,11... | collective-permute-start | bytes 24584 | tf_op jit(solution)/shard_map/ppermute | solution.py:350

commit v5 on v4

--- a/solution.py
+++ b/solution.py
@@ -53,8 +53,19 @@
     return lax.broadcasted_iota(jnp.int32, (half, size), 1) == rows
 
 
+def pack_halo(dims, tail_parity, x_ref, out_ref):
+    rows, width = dims[:2]
+    for parity in (0, 1):
+
+        @pl.when(lax.axis_index("row") % 2 == parity)
+        def _(parity=parity):
+            blocks = tail_blocks(rows, width) if parity == tail_parity else head_blocks(width)
+            for n, (row, d) in enumerate(blocks):
+                out_ref[n] = x_ref[row, d]
+
+
 def start_kernel(
-    dims, reach_hbm, bounds_hbm, flag_hbm, h_hbm, x_ref, near_ref, far_ref, part_ref, h_ref, reach_ref, bounds_ref,
+    dims, reach_hbm, bounds_hbm, flag_hbm, h_hbm, x_ref, near_ref, part_ref, h_ref, reach_ref, bounds_ref,
     flag_ref, in_sems, small_sems,
 ):
     rows, width, half, size = dims
@@ -93,18 +104,10 @@
     part = jnp.where(flag_ref[0] == 1, norm, 2.0 * diag - norm)
     part_ref[...] = part
 
-    tails, heads = tail_blocks(rows, width), head_blocks(width)
-    for parity, near, far in ((0, tails, heads), (1, heads, tails)):
-
-        @pl.when(lax.axis_index("row") % 2 == parity)
-        def _(near=near, far=far):
-            for ref, blocks in ((near_ref, near), (far_ref, far)):
-                for n, (row, d) in enumerate(blocks):
-                    ref[n] = x_ref[row, d]
-
+    pack_halo(dims, 0, x_ref, near_ref)
     for n in range(half // LINES):
         term = part.astype(BF16) if n < 3 else jnp.zeros((LINES, size), BF16)
-        near_ref[len(heads), pl.ds(n * LINES, LINES)] = term
+        near_ref[near_ref.shape[0] - 1, pl.ds(n * LINES, LINES)] = term
         part = part - term.astype(F32)
 
 
@@ -119,7 +122,8 @@
     return out
 
 
-def inner_kernel(dims, reach_ref, flag_ref, mine_ref, other_ref, out_hbm, out_ref, full, left, sems):
+def inner_kernel(dims, reach_ref, flag_ref, mine_ref, other_ref, out_hbm, far_ref, out_ref, full, left, sems):
+    pack_halo(dims, 1, mine_ref, far_ref)
     rows, width, half, size = dims
     column = lax.axis_index("col")
     first_row = lax.axis_index("row") * rows
@@ -266,21 +270,24 @@
 
 
 def halo_kernel(
-    dims, reach_ref, flag_ref, near_mine, near_other, near_sent, far_mine, far_other, far_sent, trace_ref, got_ref, base_ref,
-    out_ref, sum_ref, whole, turned, left, held, whole2, left2, held2, sems,
+    dims, above_parity, reach_ref, flag_ref, mine_ref, other_ref, sent_ref, trace_ref, got_ref, base_ref, out_ref, sum_ref,
+    whole, turned, left, held, sems,
 ):
-    rows, width, half, size = dims
-    sum_ref[...] = jnp.broadcast_to(jnp.sum(trace_ref[...] + got_ref[...]), sum_ref.shape)
-
-    for parity, above, below in (
-        (0, (far_mine, far_other), (near_mine, near_other, near_sent)),
-        (1, (near_mine, near_other), (far_mine, far_other, far_sent)),
-    ):
-
-        @pl.when(lax.axis_index("row") % 2 == parity)
-        def _(above=above, below=below):
-            add_above(dims, reach_ref, flag_ref, *above, base_ref, out_ref, whole, turned, left, held, sems.at[0], sems.at[1])
-            add_below(dims, reach_ref, flag_ref, *below, base_ref, out_ref, whole2, left2, held2, sems.at[2], sems.at[3])
+    total = jnp.sum(trace_ref[...] + got_ref[...])
+    sum_ref[0] = total / (lax.axis_size("row") * dims[0] * dims[3])
+    parity = lax.axis_index("row") % 2
+
+    @pl.when(parity == above_parity)
+    def _():
+        add_above(
+            dims, reach_ref, flag_ref, mine_ref, other_ref, base_ref, out_ref, whole, turned, left, held, sems.at[0], sems.at[1]
+        )
+
+    @pl.when(parity != above_parity)
+    def _():
+        add_below(
+            dims, reach_ref, flag_ref, mine_ref, other_ref, sent_ref, base_ref, out_ref, whole, left, held, sems.at[0], sems.at[1]
+        )
 
 
 def per_device(hamiltonian, bounds, block_reach, branch_flags):
@@ -294,16 +301,15 @@
     swap = [(0, 1), (1, 0)]
     whole = jax.ShapeDtypeStruct(hamiltonian.shape, F32)
 
-    current, near, far, part = pl.pallas_call(
+    current, near, part = pl.pallas_call(
         functools.partial(start_kernel, dims),
         out_shape=(
             jax.ShapeDtypeStruct(hamiltonian.shape, BF16),
             jax.ShapeDtypeStruct((halo + 1, half, size), BF16),
-            jax.ShapeDtypeStruct((halo, half, size), BF16),
             jax.ShapeDtypeStruct((LINES, size), F32),
         ),
         in_specs=[HBM, HBM, HBM, HBM],
-        out_specs=(VMEM, VMEM, VMEM, VMEM),
+        out_specs=(VMEM, VMEM, VMEM),
         scratch_shapes=[
             pltpu.VMEM(hamiltonian.shape, F32),
             pltpu.SMEM(block_reach.shape, jnp.int32),
@@ -317,14 +323,14 @@
         name="start",
     )(block_reach, bounds, branch_flags, hamiltonian)
     swapped = lax.ppermute(current, "col", swap)
+    got = lax.ppermute(part, "col", swap)
     near_mine = lax.ppermute(near, "row", near_pairs)
-    far_mine = lax.ppermute(far, "row", far_pairs)
-
-    base = pl.pallas_call(
+
+    base, far = pl.pallas_call(
         functools.partial(inner_kernel, dims),
-        out_shape=whole,
+        out_shape=(whole, jax.ShapeDtypeStruct((halo, half, size), BF16)),
         in_specs=[SMEM, SMEM, VMEM, VMEM],
-        out_specs=HBM,
+        out_specs=(HBM, VMEM),
         scratch_shapes=[
             pltpu.VMEM(hamiltonian.shape, F32),
             pltpu.VMEM(((rows + width) * size, (rows + width) * size), BF16),
@@ -336,33 +342,43 @@
         name="inner",
     )(block_reach, branch_flags, current, swapped)
 
+    far_mine = lax.ppermute(far, "row", far_pairs)
+
+    def add_halo(above_parity, mine, other, sent, trace, got, base):
+        square = pltpu.VMEM((width * size, width * size), BF16)
+        return pl.pallas_call(
+            functools.partial(halo_kernel, dims, above_parity),
+            out_shape=(whole, jax.ShapeDtypeStruct((1,), F32)),
+            in_specs=[SMEM, SMEM, VMEM, VMEM, VMEM, VMEM, VMEM, ANY],
+            out_specs=(ANY, SMEM),
+            input_output_aliases={7: 0},
+            scratch_shapes=[
+                square, square, pltpu.VMEM((width * half, width * size), BF16), pltpu.VMEM((halo, half, size), F32),
+                pltpu.SemaphoreType.DMA((2, width)),
+            ],
+            compiler_params=pltpu.CompilerParams(vmem_limit_bytes=16 * MIB),
+            cost_estimate=SMALL,
+            name="halo",
+        )(block_reach, branch_flags, mine, other, sent, trace, got, base)
+
     base, near_mine = lax.optimization_barrier((base, near_mine))
-    terms = near_mine[halo].astype(F32).reshape(half // LINES, LINES, size)
-    trace = part + (terms[0] + terms[1] + terms[2])
-    far_step = count // 2
-    while far_step > 1:
-        trace = trace + lax.ppermute(trace, "row", [(i, i ^ far_step) for i in range(count)])
-        far_step //= 2
-
-    base, near_mine, far_mine, trace = lax.optimization_barrier((base, near_mine, far_mine, trace))
     near_other = lax.ppermute(near_mine, "col", swap)
+    terms = (near_mine[halo].astype(F32) + near_other[halo].astype(F32)).reshape(half // LINES, LINES, size)
+    trace = part + got + (terms[0] + terms[1] + terms[2])
+    got, step = jnp.zeros_like(part), count // 2
+    while step > 2:
+        got = lax.ppermute(trace, "row", [(i, i ^ step) for i in range(count)])
+        step //= 2
+        if step > 2:
+            trace = trace + got
+    base, _ = add_halo(1, near_mine, near_other, near, part, part, base)
+    base, got = lax.optimization_barrier((base, got))
+    trace = trace + got
+    got = lax.ppermute(trace, "row", [(i, i ^ 2) for i in range(count)])
+
+    base, far_mine, trace = lax.optimization_barrier((base, far_mine, trace))
     far_other = lax.ppermute(far_mine, "col", swap)
-    got = lax.ppermute(trace, "col", swap)
-    square = pltpu.VMEM((width * size, width * size), BF16)
-    strip = pltpu.VMEM((width * half, width * size), BF16)
-    held = pltpu.VMEM((halo, half, size), F32)
-    density, total = pl.pallas_call(
-        functools.partial(halo_kernel, dims),
-        out_shape=(whole, jax.ShapeDtypeStruct((8, size), F32)),
-        in_specs=[SMEM, SMEM] + [VMEM] * 8 + [ANY],
-        out_specs=(ANY, VMEM),
-        input_output_aliases={10: 0},
-        scratch_shapes=[square, square, strip, held, square, strip, held, pltpu.SemaphoreType.DMA((4, width))],
-        compiler_params=pltpu.CompilerParams(vmem_limit_bytes=24 * MIB),
-        cost_estimate=SMALL,
-        name="halo",
-    )(block_reach, branch_flags, near_mine, near_other, near, far_mine, far_other, far, trace, got, base)
-    return density, total[0, :1] / (count * rows * size)
+    return add_halo(0, far_mine, far_other, far, trace, got, base)
 
 
 def solution(mesh):

time: 43.1 us -> 39.2 us (0.910)
  waiting for transfers between devices: 13.2 us -> 9.36 us
  between operations: 3.16 us -> 1.35 us
  Pallas kernels: 14.8 us -> 16 us
  starting transfers between devices: 9.77 us -> 10.9 us
  local copies, waits for them, and re-layouts: 1.86 us -> 1.35 us
    ppermute x1, waiting for transfers between devices: 8.23 us -> 1.77 us  [per_device(): near_mine = lax.ppermute(near, 'row', near_pairs)]
    ppermute x3, waiting for transfers between devices: 4.99 us -> 6.74 us  [the longest x1 4.57 us: per_device(): got = lax.ppermute(trace, 'row', [(i, i ^ step) for i in range(count)])]
    ppermute x3, starting transfers between devices: 5.47 us -> 7.12 us  [the longest x1 5.06 us: per_device(): got = lax.ppermute(trace, 'row', [(i, i ^ step) for i in range(count)])]
    pallas_call x2 -> x3, Pallas kernels: 11.4 us -> 12.7 us  [the longest x2 6.96 us: add_halo(): pl.pallas_call(functools.partial(halo_kernel, dims, above_parity), out_sh...]
    slice x1 -> x0, local copies, waits for them, and re-layouts: 0.51 us -> none  [per_device(): return (density, total[0, :1] / (count * rows * size))]
    ppermute x1, starting transfers between devices: 0.5 us -> 0.01 us  [per_device(): far_other = lax.ppermute(far_mine, 'col', swap)]
    ppermute x1, waiting for transfers between devices: 0.01 us -> 0.48 us  [per_device(): near_other = lax.ppermute(near_mine, 'col', swap)]
    unnamed x10 -> x8, local copies, waits for them, and re-layouts: 1.35 us -> 1.35 us
  transfers between devices with their start and end apart: 8 -> 8, of which waited for: 4 -> 5; matrix products, arithmetic and copies ran while one was open for 0% -> 0% of each run, Pallas kernels for 13% -> 24%
where the time goes in v5:
time: 39.2 us; the launch traced here: 39 us
  Pallas kernels  16 us (41%)
  starting transfers between devices  10.9 us (28%)
  waiting for transfers between devices  9.36 us (24%)
  local copies, waits for them, and re-layouts  1.35 us (3%)
  between operations  1.35 us (3%)
    pallas_call x2, Pallas kernels, add_halo(): pl.pallas_call(functools.partial(halo_kernel, dims, above_parity), out_sh...  6.96 us
    pallas_call x1, Pallas kernels, per_device(): pl.pallas_call(functools.partial(inner_kernel, dims), out_shape=(whole, j...  5.73 us
    ppermute x1, starting transfers between devices, per_device(): got = lax.ppermute(trace, 'row', [(i, i ^ step) for i in range(count)])  5.06 us
    ppermute x1, waiting for transfers between devices, per_device(): got = lax.ppermute(trace, 'row', [(i, i ^ step) for i in range(count)])  4.57 us
    pallas_call x1, Pallas kernels, per_device(): pl.pallas_call(functools.partial(start_kernel, dims), out_shape=(jax.Shap...  3.3 us
    ppermute x1, starting transfers between devices, per_device(): near_mine = lax.ppermute(near, 'row', near_pairs)  2.6 us
    ppermute x1, waiting for transfers between devices, per_device(): got = lax.ppermute(trace, 'row', [(i, i ^ 2) for i in range(count)])  2.16 us
    ppermute x1, waiting for transfers between devices, per_device(): near_mine = lax.ppermute(near, 'row', near_pairs)  1.77 us
  transfers between devices with their start and end apart: 8, of which 5 were waited for; matrix products, arithmetic and copies ran while one was open for 0% of the time, Pallas kernels for 24%

profile of v5, /device:TPU:0, one launch (start us, length us, event | category | flops | bytes accessed | tf_op | source)
XLA Modules:
  0.0 39.0 jit_solution(15135699951286018949)
XLA Ops:
  0.6 0.0 copy-start.3
  1.3 3.3 %start.1 = (bf16[12,7,64,128]{3,2,1,0:T(8,128)(2,1)}, bf16[22,64,128]{2,1,0:T(8,128)(2,1)}, f32[16,128]{1,0:T(8,128)}) custom-call(s32[12]{0:T(128)} %reach_ref.5, f32[2]{0:T(128)} %bounds_hbm.1, s32[1]{0:T(128)S(6)} %copy.10.flag_hbm.flag_ref, f32[12,7,64,128]{3,2,1,0:T(8,128)} %h_hbm.1), custom_call_target="tpu_custom_call" | custom-call | flops 1 | bytes 1 | tf_op jit(solution)/shard_map/start/pallas_call | solution.py:304
  4.6 0.5 %collective-permute-start = (bf16[12,7,64,128]{3,2,1,0:T(8,128)(2,1)}, bf16[12,7,64,128]{3,2,1,0:T(8,128)(2,1)S(1)}, u32[]{:S(2)}, u32[]{:S(2)}) collective-permute-start(bf16[12,7,64,128]{3,2,1,0:T(8,128)(2,1)} %get-tuple-element.15.mine_ref), channel_id=1, source_target_pairs={{0,1},{1,0},{2,3},{3,2},{4,5},{5,4},{6,7},{7,6},{8,9},{9,8},{10,11... | collective-permute-start | bytes 4128776 | tf_op jit(solution)/shard_map/ppermute | solution.py:325
  5.1 2.6 %collective-permute-start.1 = (bf16[22,64,128]{2,1,0:T(8,128)(2,1)}, bf16[22,64,128]{2,1,0:T(8,128)(2,1)S(1)}, u32[]{:S(2)}, u32[]{:S(2)}) collective-permute-start(bf16[22,64,128]{2,1,0:T(8,128)(2,1)} %get-tuple-element.17.sent_ref), channel_id=1, source_target_pairs={{0,2},{2,0},{4,6},{6,4},{8,10},{10,8},{12,14},{14,12},{1,3},{3,1},... | collective-permute-start | bytes 1081352 | tf_op jit(solution)/shard_map/ppermute | solution.py:327
  7.7 0.4 collective-permute-done.other_ref
  8.1 0.0 copy-done.3
  8.1 0.0 copy-start
  8.1 1.3 %copy-done = bf16[12,7,64,128]{3,2,1,0:T(8,128)(2,1)S(1)} copy-done((bf16[12,7,64,128]{3,2,1,0:T(8,128)(2,1)S(1)}, bf16[12,7,64,128]{3,2,1,0:T(8,128)(2,1)}, u32[]{:S(2)}) %copy-start) | copy-done | bytes 1376280
  9.4 0.0 copy-start.2
  9.4 0.0 copy-start.1
  9.4 5.7 %inner.1 = (f32[12,7,64,128]{3,2,1,0:T(8,128)}, bf16[21,64,128]{2,1,0:T(8,128)(2,1)S(1)}) custom-call(s32[12]{0:T(128)S(1)} %copy-done.3, s32[1]{0:T(128)S(6)} %copy.10.flag_hbm.flag_ref, bf16[12,7,64,128]{3,2,1,0:T(8,128)(2,1)S(1)} %copy-done, bf16[12,7,64,128]{3,2,1,0:T(8,128)(2,1)S(1)} %collective-permute-done.other_ref), custom_call_target="tpu_custom_call" | custom-call | flops 1 | bytes 1 | tf_op jit(solution)/shard_map/inner/pallas_call | solution.py:329
  15.2 1.8 %collective-permute-done.1.mine_ref = bf16[22,64,128]{2,1,0:T(8,128)(2,1)S(1)} collective-permute-done((bf16[22,64,128]{2,1,0:T(8,128)(2,1)}, bf16[22,64,128]{2,1,0:T(8,128)(2,1)S(1)}, u32[]{:S(2)}, u32[]{:S(2)}) %collective-permute-start.1) | collective-permute-done | bytes 360480 | tf_op jit(solution)/shard_map/ppermute | solution.py:327
  16.9 0.0 collective-permute-start.2
  16.9 0.0 copy-done.2
  16.9 0.5 %collective-permute-start.3 = (f32[16,128]{1,0:T(8,128)S(1)}, f32[16,128]{1,0:T(8,128)S(1)}, u32[]{:S(2)}, u32[]{:S(2)}) collective-permute-start(f32[16,128]{1,0:T(8,128)S(1)} %copy-done.2), channel_id=1, source_target_pairs={{0,1},{1,0},{2,3},{3,2},{4,5},{5,4},{6,7},{7,6},{8,9},{9,8},{10,11... | collective-permute-start | bytes 24584 | tf_op jit(solution)/shard_map/ppermute | solution.py:326
  17.5 0.7 %collective-permute-start.5 = (bf16[21,64,128]{2,1,0:T(8,128)(2,1)S(1)}, bf16[21,64,128]{2,1,0:T(8,128)(2,1)S(1)}, u32[]{:S(2)}, u32[]{:S(2)}) collective-permute-start(bf16[21,64,128]{2,1,0:T(8,128)(2,1)S(1)} %get-tuple-element.23.sent_ref), channel_id=1, source_target_pairs={{2,4},{4,2},{6,8},{8,6},{10,12},{12,10},{3,5},{5,3},{7,9},{9,7},{1... | collective-permute-start | bytes 1032200 | tf_op jit(solution)/shard_map/ppermute | solution.py:345
  18.1 0.5 %collective-permute-done.2.other_ref = bf16[22,64,128]{2,1,0:T(8,128)(2,1)S(1)} collective-permute-done((bf16[22,64,128]{2,1,0:T(8,128)(2,1)S(1)}, bf16[22,64,128]{2,1,0:T(8,128)(2,1)S(1)}, u32[]{:S(2)}, u32[]{:S(2)}) %collective-permute-start.2) | collective-permute-done | bytes 360480 | tf_op jit(solution)/shard_map/ppermute | solution.py:365
  18.6 0.0 collective-permute-done.3
  18.6 5.1 %collective-permute-start.4 = (f32[16,128]{1,0:T(8,128)S(1)}, f32[16,128]{1,0:T(8,128)S(1)}, u32[]{:S(2)}, u32[]{:S(2)}) collective-permute-start(f32[16,128]{1,0:T(8,128)S(1)} %fusion.1), channel_id=1, source_target_pairs={{0,8},{2,10},{4,12},{6,14},{8,0},{10,2},{12,4},{14,6},{1,9},{3,11}... | collective-permute-start | bytes 24584 | tf_op jit(solution)/shard_map/ppermute | solution.py:370
  23.7 0.0 copy-done.1
  23.7 3.5 %halo.2 = (f32[12,7,64,128]{3,2,1,0:T(8,128)}, f32[1]{0:T(128)}) custom-call(s32[12]{0:T(128)S(1)} %copy-done.3, s32[1]{0:T(128)S(6)} %copy.10.flag_hbm.flag_ref, bf16[22,64,128]{2,1,0:T(8,128)(2,1)S(1)} %collective-permute-done.1.mine_ref, bf16[22,64,128]{2,1,0:T(8,128)(2,1)S(1)} %collective-permute-done.2.other_ref, ...), custom_call_target="tpu_custom_call", output_to_operand_aliasing={{0}: (7, {})} | custom-call | flops 1 | bytes 1 | tf_op jit(solution)/shard_map/halo/pallas_call | solution.py:349
  27.2 4.6 %collective-permute-done.4 = f32[16,128]{1,0:T(8,128)S(1)} collective-permute-done((f32[16,128]{1,0:T(8,128)S(1)}, f32[16,128]{1,0:T(8,128)S(1)}, u32[]{:S(2)}, u32[]{:S(2)}) %collective-permute-start.4) | collective-permute-done | bytes 8224 | tf_op jit(solution)/shard_map/ppermute | solution.py:370
  31.8 0.0 collective-permute-done.5.mine_ref
  31.8 0.0 collective-permute-start.6
  31.8 1.6 %collective-permute-start.7 = (f32[16,128]{1,0:T(8,128)S(1)}, f32[16,128]{1,0:T(8,128)S(1)}, u32[]{:S(2)}, u32[]{:S(2)}) collective-permute-start(f32[16,128]{1,0:T(8,128)S(1)} %add.29.trace_ref), channel_id=1, source_target_pairs={{0,4},{2,6},{4,0},{6,2},{8,12},{10,14},{12,8},{14,10},{1,5},{3,7},... | collective-permute-start | bytes 24584 | tf_op jit(solution)/shard_map/ppermute | solution.py:377
  33.3 2.2 %collective-permute-done.7.got_ref = f32[16,128]{1,0:T(8,128)S(1)} collective-permute-done((f32[16,128]{1,0:T(8,128)S(1)}, f32[16,128]{1,0:T(8,128)S(1)}, u32[]{:S(2)}, u32[]{:S(2)}) %collective-permute-start.7) | collective-permute-done | bytes 8224 | tf_op jit(solution)/shard_map/ppermute | solution.py:377
  35.5 0.0 collective-permute-done.6.other_ref
  35.5 3.5 %halo.3 = (f32[12,7,64,128]{3,2,1,0:T(8,128)}, f32[1]{0:T(128)}) custom-call(s32[12]{0:T(128)S(1)} %copy-done.3, s32[1]{0:T(128)S(6)} %copy.10.flag_hbm.flag_ref, bf16[21,64,128]{2,1,0:T(8,128)(2,1)S(1)} %collective-permute-done.5.mine_ref, bf16[21,64,128]{2,1,0:T(8,128)(2,1)S(1)} %collective-permute-done.6.other_ref, ...), custom_call_target="tpu_custom_call", output_to_operand_aliasing={{0}: (7, {})} | custom-call | flops 1 | bytes 1 | tf_op jit(solution)/shard_map/halo/pallas_call | solution.py:349
  (3 shorter events, 0.0 us)
Async XLA Ops:
  0.6 7.5 %copy-start.3 = (s32[12]{0:T(128)S(1)}, s32[12]{0:T(128)}, u32[]{:S(2)}) copy-start(s32[12]{0:T(128)} %reach_ref.5) | copy-start | bytes 148
  4.6 3.5 %collective-permute-start = (bf16[12,7,64,128]{3,2,1,0:T(8,128)(2,1)}, bf16[12,7,64,128]{3,2,1,0:T(8,128)(2,1)S(1)}, u32[]{:S(2)}, u32[]{:S(2)}) collective-permute-start(bf16[12,7,64,128]{3,2,1,0:T(8,128)(2,1)} %get-tuple-element.15.mine_ref), channel_id=1, source_target_pairs={{0,1},{1,0},{2,3},{3,2},{4,5},{5,4},{6,7},{7,6},{8,9},{9,8},{10,11... | collective-permute-start | bytes 4128776 | tf_op jit(solution)/shard_map/ppermute | solution.py:325
  5.1 11.8 %collective-permute-start.1 = (bf16[22,64,128]{2,1,0:T(8,128)(2,1)}, bf16[22,64,128]{2,1,0:T(8,128)(2,1)S(1)}, u32[]{:S(2)}, u32[]{:S(2)}) collective-permute-start(bf16[22,64,128]{2,1,0:T(8,128)(2,1)} %get-tuple-element.17.sent_ref), channel_id=1, source_target_pairs={{0,2},{2,0},{4,6},{6,4},{8,10},{10,8},{12,14},{14,12},{1,3},{3,1},... | collective-permute-start | bytes 1081352 | tf_op jit(solution)/shard_map/ppermute | solution.py:327
  8.1 1.3 %copy-start = (bf16[12,7,64,128]{3,2,1,0:T(8,128)(2,1)S(1)}, bf16[12,7,64,128]{3,2,1,0:T(8,128)(2,1)}, u32[]{:S(2)}) copy-start(bf16[12,7,64,128]{3,2,1,0:T(8,128)(2,1)} %get-tuple-element.15.mine_ref) | copy-start | bytes 4128772
  9.4 7.5 %copy-start.2 = (f32[16,128]{1,0:T(8,128)S(1)}, f32[16,128]{1,0:T(8,128)}, u32[]{:S(2)}) copy-start(f32[16,128]{1,0:T(8,128)} %get-tuple-element.19.trace_ref.got_ref) | copy-start | bytes 24580
  9.4 14.3 %copy-start.1 = (bf16[22,64,128]{2,1,0:T(8,128)(2,1)S(1)}, bf16[22,64,128]{2,1,0:T(8,128)(2,1)}, u32[]{:S(2)}) copy-start(bf16[22,64,128]{2,1,0:T(8,128)(2,1)} %get-tuple-element.17.sent_ref) | copy-start | bytes 1081348
  16.9 1.7 %collective-permute-start.2 = (bf16[22,64,128]{2,1,0:T(8,128)(2,1)S(1)}, bf16[22,64,128]{2,1,0:T(8,128)(2,1)S(1)}, u32[]{:S(2)}, u32[]{:S(2)}) collective-permute-start(bf16[22,64,128]{2,1,0:T(8,128)(2,1)S(1)} %collective-permute-done.1.mine_ref), channel_id=1, source_target_pairs={{0,1},{1,0},{2,3},{3,2},{4,5},{5,4},{6,7},{7,6},{8,9},{9,8},{10,11... | collective-permute-start | bytes 1081352 | tf_op jit(solution)/shard_map/ppermute | solution.py:365
  16.9 1.7 %collective-permute-start.3 = (f32[16,128]{1,0:T(8,128)S(1)}, f32[16,128]{1,0:T(8,128)S(1)}, u32[]{:S(2)}, u32[]{:S(2)}) collective-permute-start(f32[16,128]{1,0:T(8,128)S(1)} %copy-done.2), channel_id=1, source_target_pairs={{0,1},{1,0},{2,3},{3,2},{4,5},{5,4},{6,7},{7,6},{8,9},{9,8},{10,11... | collective-permute-start | bytes 24584 | tf_op jit(solution)/shard_map/ppermute | solution.py:326
  17.5 14.3 %collective-permute-start.5 = (bf16[21,64,128]{2,1,0:T(8,128)(2,1)S(1)}, bf16[21,64,128]{2,1,0:T(8,128)(2,1)S(1)}, u32[]{:S(2)}, u32[]{:S(2)}) collective-permute-start(bf16[21,64,128]{2,1,0:T(8,128)(2,1)S(1)} %get-tuple-element.23.sent_ref), channel_id=1, source_target_pairs={{2,4},{4,2},{6,8},{8,6},{10,12},{12,10},{3,5},{5,3},{7,9},{9,7},{1... | collective-permute-start | bytes 1032200 | tf_op jit(solution)/shard_map/ppermute | solution.py:345
  18.6 13.1 %collective-permute-start.4 = (f32[16,128]{1,0:T(8,128)S(1)}, f32[16,128]{1,0:T(8,128)S(1)}, u32[]{:S(2)}, u32[]{:S(2)}) collective-permute-start(f32[16,128]{1,0:T(8,128)S(1)} %fusion.1), channel_id=1, source_target_pairs={{0,8},{2,10},{4,12},{6,14},{8,0},{10,2},{12,4},{14,6},{1,9},{3,11}... | collective-permute-start | bytes 24584 | tf_op jit(solution)/shard_map/ppermute | solution.py:370
  31.8 3.7 %collective-permute-start.6 = (bf16[21,64,128]{2,1,0:T(8,128)(2,1)S(1)}, bf16[21,64,128]{2,1,0:T(8,128)(2,1)S(1)}, u32[]{:S(2)}, u32[]{:S(2)}) collective-permute-start(bf16[21,64,128]{2,1,0:T(8,128)(2,1)S(1)} %collective-permute-done.5.mine_ref), channel_id=1, source_target_pairs={{0,1},{1,0},{2,3},{3,2},{4,5},{5,4},{6,7},{7,6},{8,9},{9,8},{10,11... | collective-permute-start | bytes 1032200 | tf_op jit(solution)/shard_map/ppermute | solution.py:380
  31.8 3.7 %collective-permute-start.7 = (f32[16,128]{1,0:T(8,128)S(1)}, f32[16,128]{1,0:T(8,128)S(1)}, u32[]{:S(2)}, u32[]{:S(2)}) collective-permute-start(f32[16,128]{1,0:T(8,128)S(1)} %add.29.trace_ref), channel_id=1, source_target_pairs={{0,4},{2,6},{4,0},{6,2},{8,12},{10,14},{12,8},{14,10},{1,5},{3,7},... | collective-permute-start | bytes 24584 | tf_op jit(solution)/shard_map/ppermute | solution.py:377

commit v6 on v5

--- a/solution.py
+++ b/solution.py
@@ -15,6 +15,7 @@
 BF16 = jnp.bfloat16
 MIB = 1 << 20
 LINES = 16
+CUT = 5
 SMALL = pl.CostEstimate(flops=1, bytes_accessed=1, transcendentals=0)
 
 
@@ -105,11 +106,6 @@
     part_ref[...] = part
 
     pack_halo(dims, 0, x_ref, near_ref)
-    for n in range(half // LINES):
-        term = part.astype(BF16) if n < 3 else jnp.zeros((LINES, size), BF16)
-        near_ref[near_ref.shape[0] - 1, pl.ds(n * LINES, LINES)] = term
-        part = part - term.astype(F32)
-
 
 def strips(rows, width):
     out = []
@@ -122,38 +118,35 @@
     return out
 
 
-def inner_kernel(dims, reach_ref, flag_ref, mine_ref, other_ref, out_hbm, far_ref, out_ref, full, left, sems):
-    pack_halo(dims, 1, mine_ref, far_ref)
+def inner_kernel(dims, first, last, reach_ref, flag_ref, mine_ref, other_ref, out_hbm, out_ref, full, left, sems):
     rows, width, half, size = dims
     column = lax.axis_index("col")
     first_row = lax.axis_index("row") * rows
     total_rows = lax.axis_size("row") * rows
     mine = pl.multiple_of(column * half, half)
     other = pl.multiple_of((1 - column) * half, half)
-    zero_full = jnp.zeros((size, size), BF16)
-    zero_left = jnp.zeros((half, size), BF16)
+    jobs = strips(rows, width)[first:last]
 
     def block(n):
         return pl.ds(n * size, size)
 
-    for k in range(rows):
-        for d in range(width + 1):
-            full[pl.ds(k * size + mine, half), block(k + d)] = mine_ref[k, d]
-            full[pl.ds(k * size + other, half), block(k + d)] = other_ref[k, d]
-    have_full = {(k, k + d) for k in range(rows) for d in range(width + 1)}
-    for j in range(rows):
-        for d in range(1, width + 1):
-            full[block(j + d), block(j)] = full[block(j), block(j + d)].T
-            have_full.add((j + d, j))
     need_full, need_left = set(), set()
-    for cols, i_lo, i_hi, k_lo, k_hi in strips(rows, width):
+    for cols, i_lo, i_hi, k_lo, k_hi in jobs:
         need_full |= {(k, j) for k in range(k_lo, k_hi + 1) for j in cols}
         need_left |= {(i, k) for i in range(i_lo, i_hi + 1) for k in range(k_lo, k_hi + 1)}
-    for k, j in sorted(need_full - have_full):
-        full[block(k), block(j)] = zero_full
+    below = {(k, j) for k, j in need_full if j < k <= j + width}
+    turned = below | {(i, k) for i, k in need_left if k < i <= k + width}
+    for k, j in sorted({(k, j) for k, j in need_full if k <= j <= k + width} | {(j, k) for k, j in turned}):
+        full[pl.ds(k * size + mine, half), block(j)] = mine_ref[k, j - k]
+        full[pl.ds(k * size + other, half), block(j)] = other_ref[k, j - k]
+    for k, j in sorted(turned):
+        full[block(k), block(j)] = full[block(j), block(k)].T
+    for k, j in sorted(need_full):
+        if abs(k - j) > width:
+            full[block(k), block(j)] = jnp.zeros((size, size), BF16)
     for i, k in sorted(need_left):
-        if k < i - width or k > i + width:
-            piece = zero_left
+        if abs(i - k) > width:
+            piece = jnp.zeros((half, size), BF16)
         elif k >= i:
             piece = mine_ref[i, k - i]
         else:
@@ -162,23 +155,36 @@
 
     sign = jnp.where(flag_ref[0] == 1, 1.0, -1.0)
     twice = jnp.where(flag_ref[0] == 1, 0.0, 2.0)
-    for cols, i_lo, i_hi, k_lo, k_hi in strips(rows, width):
+    copies = []
+    for cols, i_lo, i_hi, k_lo, k_hi in jobs:
         depth = pl.ds(k_lo * size, (k_hi - k_lo + 1) * size)
         square = jnp.dot(
             left[pl.ds(i_lo * half, (i_hi - i_lo + 1) * half), depth],
             full[depth, pl.ds(cols[0] * size, len(cols) * size)],
             preferred_element_type=F32,
         )
-        for n, j in enumerate(cols):
-            for i in range(max(i_lo, j - width), min(i_hi, j) + 1):
-                d = j - i
+        for i in range(i_lo, i_hi + 1):
+            ready = [j - i for j in cols if 0 <= j - i <= width]
+            for d in ready:
+                n = i + d - cols[0]
                 kept = is_kept(reach_ref, i, d, first_row, total_rows)
                 part = square[(i - i_lo) * half : (i - i_lo + 1) * half, n * size : (n + 1) * size]
                 out_ref[i, d] = part * jnp.where(kept, sign, 0.0) + twice * mine_ref[i, d].astype(F32)
-                if d == width:
-                    pltpu.make_async_copy(out_ref.at[i], out_hbm.at[i], sems.at[i]).start()
-    for i in range(rows):
-        pltpu.make_async_copy(out_ref.at[i], out_hbm.at[i], sems.at[i]).wait()
+            if ready:
+                run = pl.ds(ready[0], len(ready))
+                copies.append(pltpu.make_async_copy(out_ref.at[i, run], out_hbm.at[i, run], sems.at[len(copies)]))
+                copies[-1].start()
+    for copy in copies:
+        copy.wait()
+
+
+def inner_first_kernel(dims, cut, reach_ref, flag_ref, mine_ref, other_ref, out_hbm, far_ref, *scratch):
+    pack_halo(dims, 1, mine_ref, far_ref)
+    inner_kernel(dims, 0, cut, reach_ref, flag_ref, mine_ref, other_ref, out_hbm, *scratch)
+
+
+def inner_last_kernel(dims, cut, reach_ref, flag_ref, mine_ref, other_ref, base_hbm, out_hbm, *scratch):
+    inner_kernel(dims, cut, None, reach_ref, flag_ref, mine_ref, other_ref, out_hbm, *scratch)
 
 
 def fetch(base_ref, held, jobs, sems):
@@ -300,12 +306,13 @@
     far_pairs = [(i, j) for i in range(count) for j in [((i + 1) ^ 1) - 1] if 0 <= j < count]
     swap = [(0, 1), (1, 0)]
     whole = jax.ShapeDtypeStruct(hamiltonian.shape, F32)
+    packed = jax.ShapeDtypeStruct((halo, half, size), BF16)
 
     current, near, part = pl.pallas_call(
         functools.partial(start_kernel, dims),
         out_shape=(
             jax.ShapeDtypeStruct(hamiltonian.shape, BF16),
-            jax.ShapeDtypeStruct((halo + 1, half, size), BF16),
+            packed,
             jax.ShapeDtypeStruct((LINES, size), F32),
         ),
         in_specs=[HBM, HBM, HBM, HBM],
@@ -318,31 +325,54 @@
             pltpu.SemaphoreType.DMA((rows,)),
             pltpu.SemaphoreType.DMA((3,)),
         ],
-        compiler_params=pltpu.CompilerParams(vmem_limit_bytes=58 * MIB),
+        compiler_params=pltpu.CompilerParams(vmem_limit_bytes=51 * MIB),
         cost_estimate=SMALL,
         name="start",
     )(block_reach, bounds, branch_flags, hamiltonian)
     swapped = lax.ppermute(current, "col", swap)
-    got = lax.ppermute(part, "col", swap)
     near_mine = lax.ppermute(near, "row", near_pairs)
-
+    steps = [1 << n for n in reversed(range(count.bit_length() - 1))]
+    trace, got = part, jnp.zeros_like(part)
+    for step in steps[:-2]:
+        trace = trace + got
+        got = lax.ppermute(trace, "row", [(i, i ^ step) for i in range(count)])
+
+    cut = CUT
+    inner_scratch = [
+        pltpu.VMEM(hamiltonian.shape, F32),
+        pltpu.VMEM(((rows + width) * size, (rows + width) * size), BF16),
+        pltpu.VMEM((rows * half, (rows + width) * size), BF16),
+        pltpu.SemaphoreType.DMA((rows * (rows + width),)),
+    ]
     base, far = pl.pallas_call(
-        functools.partial(inner_kernel, dims),
-        out_shape=(whole, jax.ShapeDtypeStruct((halo, half, size), BF16)),
+        functools.partial(inner_first_kernel, dims, cut),
+        out_shape=(whole, packed),
         in_specs=[SMEM, SMEM, VMEM, VMEM],
         out_specs=(HBM, VMEM),
-        scratch_shapes=[
-            pltpu.VMEM(hamiltonian.shape, F32),
-            pltpu.VMEM(((rows + width) * size, (rows + width) * size), BF16),
-            pltpu.VMEM((rows * half, (rows + width) * size), BF16),
-            pltpu.SemaphoreType.DMA((rows,)),
-        ],
+        scratch_shapes=inner_scratch,
         compiler_params=pltpu.CompilerParams(vmem_limit_bytes=24 * MIB),
         cost_estimate=SMALL,
-        name="inner",
+        name="inner_first",
     )(block_reach, branch_flags, current, swapped)
-
     far_mine = lax.ppermute(far, "row", far_pairs)
+    base, near_mine, got = lax.optimization_barrier((base, near_mine, got))
+    near_other = lax.ppermute(near_mine, "col", swap)
+    trace = trace + got
+    got = lax.ppermute(trace, "row", [(i, i ^ 2) for i in range(count)])
+    base = pl.pallas_call(
+        functools.partial(inner_last_kernel, dims, cut),
+        out_shape=whole,
+        in_specs=[SMEM, SMEM, VMEM, VMEM, HBM],
+        out_specs=HBM,
+        input_output_aliases={4: 0},
+        scratch_shapes=inner_scratch,
+        compiler_params=pltpu.CompilerParams(vmem_limit_bytes=24 * MIB),
+        cost_estimate=SMALL,
+        name="inner_last",
+    )(block_reach, branch_flags, current, swapped, base)
+    base, got = lax.optimization_barrier((base, got))
+    trace = trace + got
+    got = lax.ppermute(trace, "row", [(i, i ^ 1) for i in range(count)])
 
     def add_halo(above_parity, mine, other, sent, trace, got, base):
         square = pltpu.VMEM((width * size, width * size), BF16)
@@ -361,23 +391,11 @@
             name="halo",
         )(block_reach, branch_flags, mine, other, sent, trace, got, base)
 
-    base, near_mine = lax.optimization_barrier((base, near_mine))
-    near_other = lax.ppermute(near_mine, "col", swap)
-    terms = (near_mine[halo].astype(F32) + near_other[halo].astype(F32)).reshape(half // LINES, LINES, size)
-    trace = part + got + (terms[0] + terms[1] + terms[2])
-    got, step = jnp.zeros_like(part), count // 2
-    while step > 2:
-        got = lax.ppermute(trace, "row", [(i, i ^ step) for i in range(count)])
-        step //= 2
-        if step > 2:
-            trace = trace + got
     base, _ = add_halo(1, near_mine, near_other, near, part, part, base)
-    base, got = lax.optimization_barrier((base, got))
+    base, far_mine, got = lax.optimization_barrier((base, far_mine, got))
+    far_other = lax.ppermute(far_mine, "col", swap)
     trace = trace + got
-    got = lax.ppermute(trace, "row", [(i, i ^ 2) for i in range(count)])
-
-    base, far_mine, trace = lax.optimization_barrier((base, far_mine, trace))
-    far_other = lax.ppermute(far_mine, "col", swap)
+    got = lax.ppermute(trace, "col", swap)
     return add_halo(0, far_mine, far_other, far, trace, got, base)
 
 

time: 39.2 us -> 39.2 us (level)
  waiting for transfers between devices: 9.36 us -> 4.73 us
  Pallas kernels: 16 us -> 20.2 us
  starting transfers between devices: 10.9 us -> 11.4 us
    pallas_call x1 -> x2, Pallas kernels: 5.73 us -> 11.1 us  [the longest x1 6.07 us: per_device(): pl.pallas_call(functools.partial(inner_first_kernel, dims, cut), out_shap...]
    ppermute x1, waiting for transfers between devices: 4.57 us -> 0.01 us  [per_device(): got = lax.ppermute(trace, 'row', [(i, i ^ step) for i in range(count)])]
    ppermute x1, starting transfers between devices: 1.55 us -> 4.39 us  [per_device(): got = lax.ppermute(trace, 'row', [(i, i ^ 2) for i in range(count)])]
    ppermute x1, starting transfers between devices: 5.06 us -> 2.59 us  [per_device(): got = lax.ppermute(trace, 'row', [(i, i ^ step) for i in range(count)])]
    ppermute x1, waiting for transfers between devices: 1.77 us -> 0.01 us  [per_device(): near_mine = lax.ppermute(near, 'row', near_pairs)]
    ppermute x1, waiting for transfers between devices: 2.16 us -> 3.44 us  [per_device(): got = lax.ppermute(trace, 'row', [(i, i ^ 2) for i in range(count)])]
    ppermute x1 -> x2, waiting for transfers between devices: 0.01 us -> 1.28 us  [the longest x1 1.15 us: per_device(): got = lax.ppermute(trace, 'col', swap)]
    pallas_call x1, Pallas kernels: 3.3 us -> 2.11 us  [per_device(): pl.pallas_call(functools.partial(start_kernel, dims), out_shape=(jax.Shap...]
  transfers between devices with their start and end apart: 8 -> 9, of which waited for: 5 -> 3; matrix products, arithmetic and copies ran while one was open for 0% -> 0% of each run, Pallas kernels for 24% -> 38%
where the time goes in v6:
time: 39.2 us; the launch traced here: 39 us
  Pallas kernels  20.2 us (52%)
  starting transfers between devices  11.4 us (29%)
  waiting for transfers between devices  4.73 us (12%)
  between operations  1.37 us (3%)
  local copies, waits for them, and re-layouts  1.3 us (3%)
    pallas_call x2, Pallas kernels, add_halo(): pl.pallas_call(functools.partial(halo_kernel, dims, above_parity), out_sh...  6.98 us
    pallas_call x1, Pallas kernels, per_device(): pl.pallas_call(functools.partial(inner_first_kernel, dims, cut), out_shap...  6.07 us
    pallas_call x1, Pallas kernels, per_device(): pl.pallas_call(functools.partial(inner_last_kernel, dims, cut), out_shape...  5.07 us
    ppermute x1, starting transfers between devices, per_device(): got = lax.ppermute(trace, 'row', [(i, i ^ 2) for i in range(count)])  4.39 us
    ppermute x1, waiting for transfers between devices, per_device(): got = lax.ppermute(trace, 'row', [(i, i ^ 2) for i in range(count)])  3.44 us
    ppermute x1, starting transfers between devices, per_device(): near_mine = lax.ppermute(near, 'row', near_pairs)  2.6 us
    ppermute x1, starting transfers between devices, per_device(): got = lax.ppermute(trace, 'row', [(i, i ^ step) for i in range(count)])  2.59 us
    pallas_call x1, Pallas kernels, per_device(): pl.pallas_call(functools.partial(start_kernel, dims), out_shape=(jax.Shap...  2.11 us
  transfers between devices with their start and end apart: 9, of which 3 were waited for; matrix products, arithmetic and copies ran while one was open for 0% of the time, Pallas kernels for 38%

profile of v6, /device:TPU:0, one launch (start us, length us, event | category | flops | bytes accessed | tf_op | source)
XLA Modules:
  0.0 39.0 jit_solution(15655853372493629301)
XLA Ops:
  1.3 0.0 copy-start
  1.3 0.6 %copy-done = s32[12]{0:T(128)S(1)} copy-done((s32[12]{0:T(128)S(1)}, s32[12]{0:T(128)}, u32[]{:S(2)}) %copy-start) | copy-done | bytes 72
  1.9 0.0 copy-start.1
  1.9 0.7 %copy-done.1 = f32[2]{0:T(128)S(1)} copy-done((f32[2]{0:T(128)S(1)}, f32[2]{0:T(128)}, u32[]{:S(2)}) %copy-start.1) | copy-done | bytes 32
  2.6 2.1 %start.1 = (bf16[12,7,64,128]{3,2,1,0:T(8,128)(2,1)S(1)}, bf16[21,64,128]{2,1,0:T(8,128)(2,1)S(1)}, f32[16,128]{1,0:T(8,128)S(1)}) custom-call(s32[12]{0:T(128)S(1)} %copy-done, f32[2]{0:T(128)S(1)} %copy-done.1, s32[1]{0:T(128)S(6)} %copy.12.flag_hbm.flag_ref, f32[12,7,64,128]{3,2,1,0:T(8,128)} %h_hbm.1), custom_call_target="tpu_custom_call" | custom-call | flops 1 | bytes 1 | tf_op jit(solution)/shard_map/start/pallas_call | solution.py:311
  4.7 0.5 %collective-permute-start = (bf16[12,7,64,128]{3,2,1,0:T(8,128)(2,1)S(1)}, bf16[12,7,64,128]{3,2,1,0:T(8,128)(2,1)S(1)}, u32[]{:S(2)}, u32[]{:S(2)}) collective-permute-start(bf16[12,7,64,128]{3,2,1,0:T(8,128)(2,1)S(1)} %get-tuple-element.16.mine_ref), channel_id=1, source_target_pairs={{0,1},{1,0},{2,3},{3,2},{4,5},{5,4},{6,7},{7,6},{8,9},{9,8},{10,11... | collective-permute-start | bytes 4128776 | tf_op jit(solution)/shard_map/ppermute | solution.py:332
  5.2 2.6 %collective-permute-start.1 = (bf16[21,64,128]{2,1,0:T(8,128)(2,1)S(1)}, bf16[21,64,128]{2,1,0:T(8,128)(2,1)S(1)}, u32[]{:S(2)}, u32[]{:S(2)}) collective-permute-start(bf16[21,64,128]{2,1,0:T(8,128)(2,1)S(1)} %get-tuple-element.18.sent_ref), channel_id=1, source_target_pairs={{0,2},{2,0},{4,6},{6,4},{8,10},{10,8},{12,14},{14,12},{1,3},{3,1},... | collective-permute-start | bytes 1032200 | tf_op jit(solution)/shard_map/ppermute | solution.py:333
  7.8 2.6 %collective-permute-start.2 = (f32[16,128]{1,0:T(8,128)S(1)}, f32[16,128]{1,0:T(8,128)S(1)}, u32[]{:S(2)}, u32[]{:S(2)}) collective-permute-start(f32[16,128]{1,0:T(8,128)S(1)} %get-tuple-element.19.trace_ref.got_ref), channel_id=1, source_target_pairs={{0,8},{2,10},{4,12},{6,14},{8,0},{10,2},{12,4},{14,6},{1,9},{3,11}... | collective-permute-start | bytes 24584 | tf_op jit(solution)/shard_map/ppermute | solution.py:338
  10.4 0.0 collective-permute-done.other_ref
  10.4 6.1 %inner_first.1 = (f32[12,7,64,128]{3,2,1,0:T(8,128)}, bf16[21,64,128]{2,1,0:T(8,128)(2,1)S(1)}) custom-call(s32[12]{0:T(128)S(1)} %copy-done, s32[1]{0:T(128)S(6)} %copy.12.flag_hbm.flag_ref, bf16[12,7,64,128]{3,2,1,0:T(8,128)(2,1)S(1)} %get-tuple-element.16.mine_ref, bf16[12,7,64,128]{3,2,1,0:T(8,128)(2,1)S(1)} %collective-permute-done.other_ref), custom_call_target="tpu_custom_call" | custom-call | flops 1 | bytes 1 | tf_op jit(solution)/shard_map/inner_first/pallas_call | solution.py:347
  16.5 0.0 collective-permute-done.2
  16.5 0.0 collective-permute-done.1.mine_ref
  16.5 0.1 collective-permute-start.3
  16.6 0.7 %collective-permute-start.5 = (bf16[21,64,128]{2,1,0:T(8,128)(2,1)S(1)}, bf16[21,64,128]{2,1,0:T(8,128)(2,1)S(1)}, u32[]{:S(2)}, u32[]{:S(2)}) collective-permute-start(bf16[21,64,128]{2,1,0:T(8,128)(2,1)S(1)} %get-tuple-element.25.sent_ref), channel_id=1, source_target_pairs={{2,4},{4,2},{6,8},{8,6},{10,12},{12,10},{3,5},{5,3},{7,9},{9,7},{1... | collective-permute-start | bytes 1032200 | tf_op jit(solution)/shard_map/ppermute | solution.py:357
  17.3 4.4 %collective-permute-start.4 = (f32[16,128]{1,0:T(8,128)S(1)}, f32[16,128]{1,0:T(8,128)S(1)}, u32[]{:S(2)}, u32[]{:S(2)}) collective-permute-start(f32[16,128]{1,0:T(8,128)S(1)} %add.9), channel_id=1, source_target_pairs={{0,4},{2,6},{4,0},{6,2},{8,12},{10,14},{12,8},{14,10},{1,5},{3,7},... | collective-permute-start | bytes 24584 | tf_op jit(solution)/shard_map/ppermute | solution.py:361
  21.7 5.1 %inner_last.1.base_ref = f32[12,7,64,128]{3,2,1,0:T(8,128)} custom-call(s32[12]{0:T(128)S(1)} %copy-done, s32[1]{0:T(128)S(6)} %copy.12.flag_hbm.flag_ref, bf16[12,7,64,128]{3,2,1,0:T(8,128)(2,1)S(1)} %get-tuple-element.16.mine_ref, bf16[12,7,64,128]{3,2,1,0:T(8,128)(2,1)S(1)} %collective-permute-done.other_ref, ...), custom_call_target="tpu_custom_call", output_to_operand_aliasing={{}: (4, {})} | custom-call | flops 1 | bytes 1 | tf_op jit(solution)/shard_map/inner_last/pallas_call | solution.py:362
  26.8 3.4 %collective-permute-done.4 = f32[16,128]{1,0:T(8,128)S(1)} collective-permute-done((f32[16,128]{1,0:T(8,128)S(1)}, f32[16,128]{1,0:T(8,128)S(1)}, u32[]{:S(2)}, u32[]{:S(2)}) %collective-permute-start.4) | collective-permute-done | bytes 8224 | tf_op jit(solution)/shard_map/ppermute | solution.py:361
  30.2 0.0 collective-permute-start.6
  30.2 0.0 collective-permute-done.3.other_ref
  30.2 3.5 %halo.2 = (f32[12,7,64,128]{3,2,1,0:T(8,128)}, f32[1]{0:T(128)}) custom-call(s32[12]{0:T(128)S(1)} %copy-done, s32[1]{0:T(128)S(6)} %copy.12.flag_hbm.flag_ref, bf16[21,64,128]{2,1,0:T(8,128)(2,1)S(1)} %collective-permute-done.1.mine_ref, bf16[21,64,128]{2,1,0:T(8,128)(2,1)S(1)} %collective-permute-done.3.other_ref, ...), custom_call_target="tpu_custom_call", output_to_operand_aliasing={{0}: (7, {})} | custom-call | flops 1 | bytes 1 | tf_op jit(solution)/shard_map/halo/pallas_call | solution.py:379
  33.7 0.1 collective-permute-done.6
  33.9 0.0 collective-permute-done.5.mine_ref
  33.9 0.0 collective-permute-start.7
  33.9 0.5 %collective-permute-start.8 = (f32[16,128]{1,0:T(8,128)S(1)}, f32[16,128]{1,0:T(8,128)S(1)}, u32[]{:S(2)}, u32[]{:S(2)}) collective-permute-start(f32[16,128]{1,0:T(8,128)S(1)} %add.11.trace_ref), channel_id=1, source_target_pairs={{0,1},{1,0},{2,3},{3,2},{4,5},{5,4},{6,7},{7,6},{8,9},{9,8},{10,11... | collective-permute-start | bytes 24584 | tf_op jit(solution)/shard_map/ppermute | solution.py:398
  34.4 1.1 %collective-permute-done.8.got_ref = f32[16,128]{1,0:T(8,128)S(1)} collective-permute-done((f32[16,128]{1,0:T(8,128)S(1)}, f32[16,128]{1,0:T(8,128)S(1)}, u32[]{:S(2)}, u32[]{:S(2)}) %collective-permute-start.8) | collective-permute-done | bytes 8224 | tf_op jit(solution)/shard_map/ppermute | solution.py:398
  35.5 0.0 collective-permute-done.7.other_ref
  35.5 3.5 %halo.3 = (f32[12,7,64,128]{3,2,1,0:T(8,128)}, f32[1]{0:T(128)}) custom-call(s32[12]{0:T(128)S(1)} %copy-done, s32[1]{0:T(128)S(6)} %copy.12.flag_hbm.flag_ref, bf16[21,64,128]{2,1,0:T(8,128)(2,1)S(1)} %collective-permute-done.5.mine_ref, bf16[21,64,128]{2,1,0:T(8,128)(2,1)S(1)} %collective-permute-done.7.other_ref, ...), custom_call_target="tpu_custom_call", output_to_operand_aliasing={{0}: (7, {})} | custom-call | flops 1 | bytes 1 | tf_op jit(solution)/shard_map/halo/pallas_call | solution.py:379
  (3 shorter events, 0.0 us)
Async XLA Ops:
  1.3 0.7 %copy-start = (s32[12]{0:T(128)S(1)}, s32[12]{0:T(128)}, u32[]{:S(2)}) copy-start(s32[12]{0:T(128)} %reach_ref.7) | copy-start | bytes 148
  1.9 0.7 %copy-start.1 = (f32[2]{0:T(128)S(1)}, f32[2]{0:T(128)}, u32[]{:S(2)}) copy-start(f32[2]{0:T(128)} %bounds_hbm.1) | copy-start | bytes 28
  4.7 5.7 %collective-permute-start = (bf16[12,7,64,128]{3,2,1,0:T(8,128)(2,1)S(1)}, bf16[12,7,64,128]{3,2,1,0:T(8,128)(2,1)S(1)}, u32[]{:S(2)}, u32[]{:S(2)}) collective-permute-start(bf16[12,7,64,128]{3,2,1,0:T(8,128)(2,1)S(1)} %get-tuple-element.16.mine_ref), channel_id=1, source_target_pairs={{0,1},{1,0},{2,3},{3,2},{4,5},{5,4},{6,7},{7,6},{8,9},{9,8},{10,11... | collective-permute-start | bytes 4128776 | tf_op jit(solution)/shard_map/ppermute | solution.py:332
  5.2 11.3 %collective-permute-start.1 = (bf16[21,64,128]{2,1,0:T(8,128)(2,1)S(1)}, bf16[21,64,128]{2,1,0:T(8,128)(2,1)S(1)}, u32[]{:S(2)}, u32[]{:S(2)}) collective-permute-start(bf16[21,64,128]{2,1,0:T(8,128)(2,1)S(1)} %get-tuple-element.18.sent_ref), channel_id=1, source_target_pairs={{0,2},{2,0},{4,6},{6,4},{8,10},{10,8},{12,14},{14,12},{1,3},{3,1},... | collective-permute-start | bytes 1032200 | tf_op jit(solution)/shard_map/ppermute | solution.py:333
  7.8 8.7 %collective-permute-start.2 = (f32[16,128]{1,0:T(8,128)S(1)}, f32[16,128]{1,0:T(8,128)S(1)}, u32[]{:S(2)}, u32[]{:S(2)}) collective-permute-start(f32[16,128]{1,0:T(8,128)S(1)} %get-tuple-element.19.trace_ref.got_ref), channel_id=1, source_target_pairs={{0,8},{2,10},{4,12},{6,14},{8,0},{10,2},{12,4},{14,6},{1,9},{3,11}... | collective-permute-start | bytes 24584 | tf_op jit(solution)/shard_map/ppermute | solution.py:338
  16.5 13.7 %collective-permute-start.3 = (bf16[21,64,128]{2,1,0:T(8,128)(2,1)S(1)}, bf16[21,64,128]{2,1,0:T(8,128)(2,1)S(1)}, u32[]{:S(2)}, u32[]{:S(2)}) collective-permute-start(bf16[21,64,128]{2,1,0:T(8,128)(2,1)S(1)} %collective-permute-done.1.mine_ref), channel_id=1, source_target_pairs={{0,1},{1,0},{2,3},{3,2},{4,5},{5,4},{6,7},{7,6},{8,9},{9,8},{10,11... | collective-permute-start | bytes 1032200 | tf_op jit(solution)/shard_map/ppermute | solution.py:359
  16.6 17.3 %collective-permute-start.5 = (bf16[21,64,128]{2,1,0:T(8,128)(2,1)S(1)}, bf16[21,64,128]{2,1,0:T(8,128)(2,1)S(1)}, u32[]{:S(2)}, u32[]{:S(2)}) collective-permute-start(bf16[21,64,128]{2,1,0:T(8,128)(2,1)S(1)} %get-tuple-element.25.sent_ref), channel_id=1, source_target_pairs={{2,4},{4,2},{6,8},{8,6},{10,12},{12,10},{3,5},{5,3},{7,9},{9,7},{1... | collective-permute-start | bytes 1032200 | tf_op jit(solution)/shard_map/ppermute | solution.py:357
  17.3 12.9 %collective-permute-start.4 = (f32[16,128]{1,0:T(8,128)S(1)}, f32[16,128]{1,0:T(8,128)S(1)}, u32[]{:S(2)}, u32[]{:S(2)}) collective-permute-start(f32[16,128]{1,0:T(8,128)S(1)} %add.9), channel_id=1, source_target_pairs={{0,4},{2,6},{4,0},{6,2},{8,12},{10,14},{12,8},{14,10},{1,5},{3,7},... | collective-permute-start | bytes 24584 | tf_op jit(solution)/shard_map/ppermute | solution.py:361
  30.2 3.7 %collective-permute-start.6 = (f32[16,128]{1,0:T(8,128)S(1)}, f32[16,128]{1,0:T(8,128)S(1)}, u32[]{:S(2)}, u32[]{:S(2)}) collective-permute-start(f32[16,128]{1,0:T(8,128)S(1)} %add.10), channel_id=1, source_target_pairs={{0,2},{2,0},{4,6},{6,4},{8,10},{10,8},{12,14},{14,12},{1,3},{3,1},... | collective-permute-start | bytes 24584 | tf_op jit(solution)/shard_map/ppermute | solution.py:375
  33.9 1.7 %collective-permute-start.7 = (bf16[21,64,128]{2,1,0:T(8,128)(2,1)S(1)}, bf16[21,64,128]{2,1,0:T(8,128)(2,1)S(1)}, u32[]{:S(2)}, u32[]{:S(2)}) collective-permute-start(bf16[21,64,128]{2,1,0:T(8,128)(2,1)S(1)} %collective-permute-done.5.mine_ref), channel_id=1, source_target_pairs={{0,1},{1,0},{2,3},{3,2},{4,5},{5,4},{6,7},{7,6},{8,9},{9,8},{10,11... | collective-permute-start | bytes 1032200 | tf_op jit(solution)/shard_map/ppermute | solution.py:396
  33.9 1.7 %collective-permute-start.8 = (f32[16,128]{1,0:T(8,128)S(1)}, f32[16,128]{1,0:T(8,128)S(1)}, u32[]{:S(2)}, u32[]{:S(2)}) collective-permute-start(f32[16,128]{1,0:T(8,128)S(1)} %add.11.trace_ref), channel_id=1, source_target_pairs={{0,1},{1,0},{2,3},{3,2},{4,5},{5,4},{6,7},{7,6},{8,9},{9,8},{10,11... | collective-permute-start | bytes 24584 | tf_op jit(solution)/shard_map/ppermute | solution.py:398

commit v7 on v6

--- a/solution.py
+++ b/solution.py
@@ -14,8 +14,8 @@
 F32 = jnp.float32
 BF16 = jnp.bfloat16
 MIB = 1 << 20
-LINES = 16
-CUT = 5
+LINES = 64
+PAD = 1
 SMALL = pl.CostEstimate(flops=1, bytes_accessed=1, transcendentals=0)
 
 
@@ -63,10 +63,12 @@
             blocks = tail_blocks(rows, width) if parity == tail_parity else head_blocks(width)
             for n, (row, d) in enumerate(blocks):
                 out_ref[n] = x_ref[row, d]
+    for n in range(len(head_blocks(width)), out_ref.shape[0]):
+        out_ref[n] = jnp.zeros(out_ref.shape[1:], BF16)
 
 
 def start_kernel(
-    dims, reach_hbm, bounds_hbm, flag_hbm, h_hbm, x_ref, near_ref, part_ref, h_ref, reach_ref, bounds_ref,
+    dims, reach_hbm, bounds_hbm, flag_hbm, h_hbm, x_ref, near_ref, far_ref, part_ref, h_ref, reach_ref, bounds_ref,
     flag_ref, in_sems, small_sems,
 ):
     rows, width, half, size = dims
@@ -106,6 +108,7 @@
     part_ref[...] = part
 
     pack_halo(dims, 0, x_ref, near_ref)
+    pack_halo(dims, 1, x_ref, far_ref)
 
 def strips(rows, width):
     out = []
@@ -118,14 +121,14 @@
     return out
 
 
-def inner_kernel(dims, first, last, reach_ref, flag_ref, mine_ref, other_ref, out_hbm, out_ref, full, left, sems):
+def inner_kernel(dims, reach_ref, flag_ref, mine_ref, other_ref, out_hbm, out_ref, full, left, sems):
     rows, width, half, size = dims
     column = lax.axis_index("col")
     first_row = lax.axis_index("row") * rows
     total_rows = lax.axis_size("row") * rows
     mine = pl.multiple_of(column * half, half)
     other = pl.multiple_of((1 - column) * half, half)
-    jobs = strips(rows, width)[first:last]
+    jobs = strips(rows, width)
 
     def block(n):
         return pl.ds(n * size, size)
@@ -164,27 +167,16 @@
             preferred_element_type=F32,
         )
         for i in range(i_lo, i_hi + 1):
-            ready = [j - i for j in cols if 0 <= j - i <= width]
-            for d in ready:
+            for d in [j - i for j in cols if 0 <= j - i <= width]:
                 n = i + d - cols[0]
                 kept = is_kept(reach_ref, i, d, first_row, total_rows)
                 part = square[(i - i_lo) * half : (i - i_lo + 1) * half, n * size : (n + 1) * size]
                 out_ref[i, d] = part * jnp.where(kept, sign, 0.0) + twice * mine_ref[i, d].astype(F32)
-            if ready:
-                run = pl.ds(ready[0], len(ready))
-                copies.append(pltpu.make_async_copy(out_ref.at[i, run], out_hbm.at[i, run], sems.at[len(copies)]))
-                copies[-1].start()
+                if d == width:
+                    copies.append(pltpu.make_async_copy(out_ref.at[i], out_hbm.at[i], sems.at[i]))
+                    copies[-1].start()
     for copy in copies:
         copy.wait()
-
-
-def inner_first_kernel(dims, cut, reach_ref, flag_ref, mine_ref, other_ref, out_hbm, far_ref, *scratch):
-    pack_halo(dims, 1, mine_ref, far_ref)
-    inner_kernel(dims, 0, cut, reach_ref, flag_ref, mine_ref, other_ref, out_hbm, *scratch)
-
-
-def inner_last_kernel(dims, cut, reach_ref, flag_ref, mine_ref, other_ref, base_hbm, out_hbm, *scratch):
-    inner_kernel(dims, cut, None, reach_ref, flag_ref, mine_ref, other_ref, out_hbm, *scratch)
 
 
 def fetch(base_ref, held, jobs, sems):
@@ -276,10 +268,10 @@
 
 
 def halo_kernel(
-    dims, above_parity, reach_ref, flag_ref, mine_ref, other_ref, sent_ref, trace_ref, got_ref, base_ref, out_ref, sum_ref,
+    dims, above_parity, reach_ref, flag_ref, mine_ref, other_ref, sent_ref, trace_ref, base_ref, out_ref, sum_ref,
     whole, turned, left, held, sems,
 ):
-    total = jnp.sum(trace_ref[...] + got_ref[...])
+    total = jnp.sum(trace_ref[...])
     sum_ref[0] = total / (lax.axis_size("row") * dims[0] * dims[3])
     parity = lax.axis_index("row") % 2
 
@@ -308,15 +300,16 @@
     whole = jax.ShapeDtypeStruct(hamiltonian.shape, F32)
     packed = jax.ShapeDtypeStruct((halo, half, size), BF16)
 
-    current, near, part = pl.pallas_call(
+    current, near, far, part = pl.pallas_call(
         functools.partial(start_kernel, dims),
         out_shape=(
             jax.ShapeDtypeStruct(hamiltonian.shape, BF16),
             packed,
+            jax.ShapeDtypeStruct((halo + PAD, half, size), BF16),
             jax.ShapeDtypeStruct((LINES, size), F32),
         ),
         in_specs=[HBM, HBM, HBM, HBM],
-        out_specs=(VMEM, VMEM, VMEM),
+        out_specs=(VMEM, VMEM, VMEM, VMEM),
         scratch_shapes=[
             pltpu.VMEM(hamiltonian.shape, F32),
             pltpu.SMEM(block_reach.shape, jnp.int32),
@@ -325,63 +318,40 @@
             pltpu.SemaphoreType.DMA((rows,)),
             pltpu.SemaphoreType.DMA((3,)),
         ],
-        compiler_params=pltpu.CompilerParams(vmem_limit_bytes=51 * MIB),
+        compiler_params=pltpu.CompilerParams(vmem_limit_bytes=50 * MIB),
         cost_estimate=SMALL,
         name="start",
     )(block_reach, bounds, branch_flags, hamiltonian)
     swapped = lax.ppermute(current, "col", swap)
     near_mine = lax.ppermute(near, "row", near_pairs)
-    steps = [1 << n for n in reversed(range(count.bit_length() - 1))]
-    trace, got = part, jnp.zeros_like(part)
-    for step in steps[:-2]:
-        trace = trace + got
-        got = lax.ppermute(trace, "row", [(i, i ^ step) for i in range(count)])
-
-    cut = CUT
-    inner_scratch = [
-        pltpu.VMEM(hamiltonian.shape, F32),
-        pltpu.VMEM(((rows + width) * size, (rows + width) * size), BF16),
-        pltpu.VMEM((rows * half, (rows + width) * size), BF16),
-        pltpu.SemaphoreType.DMA((rows * (rows + width),)),
-    ]
-    base, far = pl.pallas_call(
-        functools.partial(inner_first_kernel, dims, cut),
-        out_shape=(whole, packed),
+    parts = lax.all_gather(part, ("row", "col"), tiled=True)
+    far_mine = lax.ppermute(far, "row", far_pairs)
+    base = pl.pallas_call(
+        functools.partial(inner_kernel, dims),
+        out_shape=whole,
         in_specs=[SMEM, SMEM, VMEM, VMEM],
-        out_specs=(HBM, VMEM),
-        scratch_shapes=inner_scratch,
+        out_specs=HBM,
+        scratch_shapes=[
+            pltpu.VMEM(hamiltonian.shape, F32),
+            pltpu.VMEM(((rows + width) * size, (rows + width) * size), BF16),
+            pltpu.VMEM((rows * half, (rows + width) * size), BF16),
+            pltpu.SemaphoreType.DMA((rows,)),
+        ],
         compiler_params=pltpu.CompilerParams(vmem_limit_bytes=24 * MIB),
         cost_estimate=SMALL,
-        name="inner_first",
+        name="inner",
     )(block_reach, branch_flags, current, swapped)
-    far_mine = lax.ppermute(far, "row", far_pairs)
-    base, near_mine, got = lax.optimization_barrier((base, near_mine, got))
+    base, near_mine = lax.optimization_barrier((base, near_mine))
     near_other = lax.ppermute(near_mine, "col", swap)
-    trace = trace + got
-    got = lax.ppermute(trace, "row", [(i, i ^ 2) for i in range(count)])
-    base = pl.pallas_call(
-        functools.partial(inner_last_kernel, dims, cut),
-        out_shape=whole,
-        in_specs=[SMEM, SMEM, VMEM, VMEM, HBM],
-        out_specs=HBM,
-        input_output_aliases={4: 0},
-        scratch_shapes=inner_scratch,
-        compiler_params=pltpu.CompilerParams(vmem_limit_bytes=24 * MIB),
-        cost_estimate=SMALL,
-        name="inner_last",
-    )(block_reach, branch_flags, current, swapped, base)
-    base, got = lax.optimization_barrier((base, got))
-    trace = trace + got
-    got = lax.ppermute(trace, "row", [(i, i ^ 1) for i in range(count)])
-
-    def add_halo(above_parity, mine, other, sent, trace, got, base):
+
+    def add_halo(above_parity, mine, other, sent, trace, base):
         square = pltpu.VMEM((width * size, width * size), BF16)
         return pl.pallas_call(
             functools.partial(halo_kernel, dims, above_parity),
             out_shape=(whole, jax.ShapeDtypeStruct((1,), F32)),
-            in_specs=[SMEM, SMEM, VMEM, VMEM, VMEM, VMEM, VMEM, ANY],
+            in_specs=[SMEM, SMEM, VMEM, VMEM, VMEM, VMEM, ANY],
             out_specs=(ANY, SMEM),
-            input_output_aliases={7: 0},
+            input_output_aliases={6: 0},
             scratch_shapes=[
                 square, square, pltpu.VMEM((width * half, width * size), BF16), pltpu.VMEM((halo, half, size), F32),
                 pltpu.SemaphoreType.DMA((2, width)),
@@ -389,14 +359,12 @@
             compiler_params=pltpu.CompilerParams(vmem_limit_bytes=16 * MIB),
             cost_estimate=SMALL,
             name="halo",
-        )(block_reach, branch_flags, mine, other, sent, trace, got, base)
-
-    base, _ = add_halo(1, near_mine, near_other, near, part, part, base)
-    base, far_mine, got = lax.optimization_barrier((base, far_mine, got))
+        )(block_reach, branch_flags, mine, other, sent, trace, base)
+
+    base, _ = add_halo(1, near_mine, near_other, near, part, base)
+    base, far_mine, parts = lax.optimization_barrier((base, far_mine, parts))
     far_other = lax.ppermute(far_mine, "col", swap)
-    trace = trace + got
-    got = lax.ppermute(trace, "col", swap)
-    return add_halo(0, far_mine, far_other, far, trace, got, base)
+    return add_halo(0, far_mine, far_other, far, parts, base)
 
 
 def solution(mesh):

time: 39.2 us -> 54.6 us (1.39)
  blocking collectives: 0 us -> 22.1 us
  starting transfers between devices: 11.4 us -> 4.2 us
  waiting for transfers between devices: 4.73 us -> 10.6 us
  Pallas kernels: 20.2 us -> 14.9 us
    all_gather x0 -> x1, blocking collectives: none -> 22.1 us  [per_device(): parts = lax.all_gather(part, ('row', 'col'), tiled=True)]
    ppermute x1, waiting for transfers between devices: 0.01 us -> 9.26 us  [per_device(): near_mine = lax.ppermute(near, 'row', near_pairs)]
    ppermute x4 -> x0, starting transfers between devices: 7.49 us -> none  [the longest x1 4.39 us: per_device(): got = lax.ppermute(trace, 'row', [(i, i ^ 2) for i in range(count)])]
    pallas_call x2 -> x1, Pallas kernels: 11.1 us -> 5.7 us  [per_device(): pl.pallas_call(functools.partial(inner_kernel, dims), out_shape=whole, in...]
    ppermute x4 -> x0, waiting for transfers between devices: 4.72 us -> none  [the longest x1 3.44 us: per_device(): got = lax.ppermute(trace, 'row', [(i, i ^ 2) for i in range(count)])]
    ppermute x1, waiting for transfers between devices: 0.01 us -> 1.33 us  [per_device(): far_other = lax.ppermute(far_mine, 'col', swap)]
  transfers between devices with their start and end apart: 9 -> 5, of which waited for: 3 -> 2; matrix products, arithmetic and copies ran while one was open for 0% -> 0% of each run, Pallas kernels for 38% -> 17%
where the time goes in v7:
time: 54.6 us; the launch traced here: 54.4 us
  blocking collectives  22.1 us (40%)
  Pallas kernels  14.9 us (27%)
  waiting for transfers between devices  10.6 us (19%)
  starting transfers between devices  4.2 us (8%)
  between operations  1.34 us (2%)
  local copies, waits for them, and re-layouts  1.3 us (2%)
    all_gather x1, blocking collectives, per_device(): parts = lax.all_gather(part, ('row', 'col'), tiled=True)  22.1 us
    ppermute x1, waiting for transfers between devices, per_device(): near_mine = lax.ppermute(near, 'row', near_pairs)  9.26 us
    pallas_call x2, Pallas kernels, add_halo(): pl.pallas_call(functools.partial(halo_kernel, dims, above_parity), out_sh...  7.1 us
    pallas_call x1, Pallas kernels, per_device(): pl.pallas_call(functools.partial(inner_kernel, dims), out_shape=whole, in...  5.7 us
    ppermute x1, starting transfers between devices, per_device(): near_mine = lax.ppermute(near, 'row', near_pairs)  2.6 us
    pallas_call x1, Pallas kernels, per_device(): pl.pallas_call(functools.partial(start_kernel, dims), out_shape=(jax.Shap...  2.09 us
    ppermute x1, waiting for transfers between devices, per_device(): far_other = lax.ppermute(far_mine, 'col', swap)  1.33 us
    unnamed x4, local copies, waits for them, and re-layouts  1.3 us
  transfers between devices with their start and end apart: 5, of which 2 were waited for; matrix products, arithmetic and copies ran while one was open for 0% of the time, Pallas kernels for 17%

profile of v7, /device:TPU:0, one launch (start us, length us, event | category | flops | bytes accessed | tf_op | source)
XLA Modules:
  0.0 54.4 jit_solution(309336721557452388)
XLA Ops:
  1.3 0.0 copy-start
  1.3 0.6 %copy-done = s32[12]{0:T(128)S(1)} copy-done((s32[12]{0:T(128)S(1)}, s32[12]{0:T(128)}, u32[]{:S(2)}) %copy-start) | copy-done | bytes 72
  1.9 0.0 copy-start.1
  1.9 0.7 %copy-done.1 = f32[2]{0:T(128)S(1)} copy-done((f32[2]{0:T(128)S(1)}, f32[2]{0:T(128)}, u32[]{:S(2)}) %copy-start.1) | copy-done | bytes 32
  2.6 2.1 %start.1 = (bf16[12,7,64,128]{3,2,1,0:T(8,128)(2,1)S(1)}, bf16[21,64,128]{2,1,0:T(8,128)(2,1)S(1)}, bf16[22,64,128]{2,1,0:T(8,128)(2,1)S(1)}, f32[64,128]{1,0:T(8,128)S(1)}) custom-call(s32[12]{0:T(128)S(1)} %copy-done, f32[2]{0:T(128)S(1)} %copy-done.1, s32[1]{0:T(128)S(6)} %copy.10.flag_hbm.flag_ref, f32[12,7,64,128]{3,2,1,0:T(8,128)} %h_hbm.1), custom_call_target="tpu_custom_call" | custom-call | flops 1 | bytes 1 | tf_op jit(solution)/shard_map/start/pallas_call | solution.py:303
  4.7 0.5 collective-permute-start
  5.2 2.6 %collective-permute-start.1 = (bf16[21,64,128]{2,1,0:T(8,128)(2,1)S(1)}, bf16[21,64,128]{2,1,0:T(8,128)(2,1)S(1)}, u32[]{:S(2)}, u32[]{:S(2)}) collective-permute-start(bf16[21,64,128]{2,1,0:T(8,128)(2,1)S(1)} %get-tuple-element.13.sent_ref), channel_id=1, source_target_pairs={{0,2},{2,0},{4,6},{6,4},{8,10},{10,8},{12,14},{14,12},{1,3},{3,1},... | collective-permute-start | bytes 1032200 | tf_op jit(solution)/shard_map/ppermute | solution.py:326
  7.8 0.7 %collective-permute-start.3 = (bf16[22,64,128]{2,1,0:T(8,128)(2,1)S(1)}, bf16[22,64,128]{2,1,0:T(8,128)(2,1)S(1)}, u32[]{:S(2)}, u32[]{:S(2)}) collective-permute-start(bf16[22,64,128]{2,1,0:T(8,128)(2,1)S(1)} %get-tuple-element.18.sent_ref), channel_id=1, source_target_pairs={{2,4},{4,2},{6,8},{8,6},{10,12},{12,10},{3,5},{5,3},{7,9},{9,7},{1... | collective-permute-start | bytes 1081352 | tf_op jit(solution)/shard_map/ppermute | solution.py:328
  8.5 0.0 collective-permute-done.other_ref
  8.5 5.7 %inner.1.base_ref = f32[12,7,64,128]{3,2,1,0:T(8,128)} custom-call(s32[12]{0:T(128)S(1)} %copy-done, s32[1]{0:T(128)S(6)} %copy.10.flag_hbm.flag_ref, bf16[12,7,64,128]{3,2,1,0:T(8,128)(2,1)S(1)} %get-tuple-element.12.mine_ref, bf16[12,7,64,128]{3,2,1,0:T(8,128)(2,1)S(1)} %collective-permute-done.other_ref), custom_call_target="tpu_custom_call" | custom-call | flops 1 | bytes 1 | tf_op jit(solution)/shard_map/inner/pallas_call | solution.py:329
  14.2 9.3 %collective-permute-done.1.mine_ref = bf16[21,64,128]{2,1,0:T(8,128)(2,1)S(1)} collective-permute-done((bf16[21,64,128]{2,1,0:T(8,128)(2,1)S(1)}, bf16[21,64,128]{2,1,0:T(8,128)(2,1)S(1)}, u32[]{:S(2)}, u32[]{:S(2)}) %collective-permute-start.1) | collective-permute-done | bytes 344096 | tf_op jit(solution)/shard_map/ppermute | solution.py:326
  23.5 0.0 collective-permute-start.2
  23.5 22.1 %all_gather.3.trace_ref = f32[1024,128]{1,0:T(8,128)S(1)} all-gather(f32[64,128]{1,0:T(8,128)S(1)} %get-tuple-element.15.trace_ref), channel_id=1, replica_groups=mesh['groups'=2,'row'=8,'col'=2] {'row','col'}, dimensions={0}, use_global_device_ids=true | all-gather | bytes 557056 | tf_op jit(solution)/shard_map/all_gather | solution.py:327
  45.5 0.0 collective-permute-done.2.other_ref
  45.5 3.5 %halo.2 = (f32[12,7,64,128]{3,2,1,0:T(8,128)}, f32[1]{0:T(128)}) custom-call(s32[12]{0:T(128)S(1)} %copy-done, s32[1]{0:T(128)S(6)} %copy.10.flag_hbm.flag_ref, bf16[21,64,128]{2,1,0:T(8,128)(2,1)S(1)} %collective-permute-done.1.mine_ref, bf16[21,64,128]{2,1,0:T(8,128)(2,1)S(1)} %collective-permute-done.2.other_ref, ...), custom_call_target="tpu_custom_call", output_to_operand_aliasing={{0}: (6, {})} | custom-call | flops 1 | bytes 1 | tf_op jit(solution)/shard_map/halo/pallas_call | solution.py:349
  49.0 0.0 collective-permute-done.3.mine_ref
  49.1 0.4 collective-permute-start.4
  49.5 1.3 %collective-permute-done.4.other_ref = bf16[22,64,128]{2,1,0:T(8,128)(2,1)S(1)} collective-permute-done((bf16[22,64,128]{2,1,0:T(8,128)(2,1)S(1)}, bf16[22,64,128]{2,1,0:T(8,128)(2,1)S(1)}, u32[]{:S(2)}, u32[]{:S(2)}) %collective-permute-start.4) | collective-permute-done | bytes 360480 | tf_op jit(solution)/shard_map/ppermute | solution.py:366
  50.8 3.6 %halo.3 = (f32[12,7,64,128]{3,2,1,0:T(8,128)}, f32[1]{0:T(128)}) custom-call(s32[12]{0:T(128)S(1)} %copy-done, s32[1]{0:T(128)S(6)} %copy.10.flag_hbm.flag_ref, bf16[22,64,128]{2,1,0:T(8,128)(2,1)S(1)} %collective-permute-done.3.mine_ref, bf16[22,64,128]{2,1,0:T(8,128)(2,1)S(1)} %collective-permute-done.4.other_ref, ...), custom_call_target="tpu_custom_call", output_to_operand_aliasing={{0}: (6, {})} | custom-call | flops 1 | bytes 1 | tf_op jit(solution)/shard_map/halo/pallas_call | solution.py:349
Async XLA Ops:
  1.3 0.7 %copy-start = (s32[12]{0:T(128)S(1)}, s32[12]{0:T(128)}, u32[]{:S(2)}) copy-start(s32[12]{0:T(128)} %reach_ref.5) | copy-start | bytes 148
  1.9 0.7 %copy-start.1 = (f32[2]{0:T(128)S(1)}, f32[2]{0:T(128)}, u32[]{:S(2)}) copy-start(f32[2]{0:T(128)} %bounds_hbm.1) | copy-start | bytes 28
  4.7 3.8 %collective-permute-start = (bf16[12,7,64,128]{3,2,1,0:T(8,128)(2,1)S(1)}, bf16[12,7,64,128]{3,2,1,0:T(8,128)(2,1)S(1)}, u32[]{:S(2)}, u32[]{:S(2)}) collective-permute-start(bf16[12,7,64,128]{3,2,1,0:T(8,128)(2,1)S(1)} %get-tuple-element.12.mine_ref), channel_id=1, source_target_pairs={{0,1},{1,0},{2,3},{3,2},{4,5},{5,4},{6,7},{7,6},{8,9},{9,8},{10,11... | collective-permute-start | bytes 4128776 | tf_op jit(solution)/shard_map/ppermute | solution.py:325
  5.2 18.3 %collective-permute-start.1 = (bf16[21,64,128]{2,1,0:T(8,128)(2,1)S(1)}, bf16[21,64,128]{2,1,0:T(8,128)(2,1)S(1)}, u32[]{:S(2)}, u32[]{:S(2)}) collective-permute-start(bf16[21,64,128]{2,1,0:T(8,128)(2,1)S(1)} %get-tuple-element.13.sent_ref), channel_id=1, source_target_pairs={{0,2},{2,0},{4,6},{6,4},{8,10},{10,8},{12,14},{14,12},{1,3},{3,1},... | collective-permute-start | bytes 1032200 | tf_op jit(solution)/shard_map/ppermute | solution.py:326
  7.8 41.2 %collective-permute-start.3 = (bf16[22,64,128]{2,1,0:T(8,128)(2,1)S(1)}, bf16[22,64,128]{2,1,0:T(8,128)(2,1)S(1)}, u32[]{:S(2)}, u32[]{:S(2)}) collective-permute-start(bf16[22,64,128]{2,1,0:T(8,128)(2,1)S(1)} %get-tuple-element.18.sent_ref), channel_id=1, source_target_pairs={{2,4},{4,2},{6,8},{8,6},{10,12},{12,10},{3,5},{5,3},{7,9},{9,7},{1... | collective-permute-start | bytes 1081352 | tf_op jit(solution)/shard_map/ppermute | solution.py:328
  23.5 22.1 %collective-permute-start.2 = (bf16[21,64,128]{2,1,0:T(8,128)(2,1)S(1)}, bf16[21,64,128]{2,1,0:T(8,128)(2,1)S(1)}, u32[]{:S(2)}, u32[]{:S(2)}) collective-permute-start(bf16[21,64,128]{2,1,0:T(8,128)(2,1)S(1)} %collective-permute-done.1.mine_ref), channel_id=1, source_target_pairs={{0,1},{1,0},{2,3},{3,2},{4,5},{5,4},{6,7},{7,6},{8,9},{9,8},{10,11... | collective-permute-start | bytes 1032200 | tf_op jit(solution)/shard_map/ppermute | solution.py:345
  49.1 1.7 %collective-permute-start.4 = (bf16[22,64,128]{2,1,0:T(8,128)(2,1)S(1)}, bf16[22,64,128]{2,1,0:T(8,128)(2,1)S(1)}, u32[]{:S(2)}, u32[]{:S(2)}) collective-permute-start(bf16[22,64,128]{2,1,0:T(8,128)(2,1)S(1)} %collective-permute-done.3.mine_ref), channel_id=1, source_target_pairs={{0,1},{1,0},{2,3},{3,2},{4,5},{5,4},{6,7},{7,6},{8,9},{9,8},{10,11... | collective-permute-start | bytes 1081352 | tf_op jit(solution)/shard_map/ppermute | solution.py:366

commit v8 on v7

--- a/solution.py
+++ b/solution.py
@@ -14,8 +14,7 @@
 F32 = jnp.float32
 BF16 = jnp.bfloat16
 MIB = 1 << 20
-LINES = 64
-PAD = 1
+LINES = 16
 SMALL = pl.CostEstimate(flops=1, bytes_accessed=1, transcendentals=0)
 
 
@@ -63,12 +62,20 @@
             blocks = tail_blocks(rows, width) if parity == tail_parity else head_blocks(width)
             for n, (row, d) in enumerate(blocks):
                 out_ref[n] = x_ref[row, d]
-    for n in range(len(head_blocks(width)), out_ref.shape[0]):
-        out_ref[n] = jnp.zeros(out_ref.shape[1:], BF16)
+
+
+def pack_far_kernel(dims, x_ref, sum_ref, out_ref):
+    rows, width, half, size = dims
+    pack_halo(dims, 1, x_ref, out_ref)
+    rest = sum_ref[...]
+    for n in range(half // LINES):
+        term = rest.astype(BF16) if n < 3 else jnp.zeros((LINES, size), BF16)
+        out_ref[out_ref.shape[0] - 1, pl.ds(n * LINES, LINES)] = term
+        rest = rest - term.astype(F32)
 
 
 def start_kernel(
-    dims, reach_hbm, bounds_hbm, flag_hbm, h_hbm, x_ref, near_ref, far_ref, part_ref, h_ref, reach_ref, bounds_ref,
+    dims, reach_hbm, bounds_hbm, flag_hbm, h_hbm, x_ref, near_ref, part_ref, h_ref, reach_ref, bounds_ref,
     flag_ref, in_sems, small_sems,
 ):
     rows, width, half, size = dims
@@ -108,7 +115,6 @@
     part_ref[...] = part
 
     pack_halo(dims, 0, x_ref, near_ref)
-    pack_halo(dims, 1, x_ref, far_ref)
 
 def strips(rows, width):
     out = []
@@ -187,11 +193,10 @@
     return copies
 
 
-def finish(dims, reach_ref, flag_ref, square, from_row, from_col, copies, jobs, held, out_ref, sems):
+def finish(dims, reach_ref, sign, square, from_row, from_col, copies, jobs, held, out_ref, sems):
     rows, width, half, size = dims
     first_row = lax.axis_index("row") * rows
     total_rows = lax.axis_size("row") * rows
-    sign = jnp.where(flag_ref[0] == 1, 1.0, -1.0)
     backs = []
     for n, (row, d, count, at) in enumerate(jobs):
         copies[n].wait()
@@ -237,7 +242,8 @@
                 whole[block(k), block(j)] = jnp.zeros((size, size), BF16)
                 left[pl.ds(j * half, half), block(k)] = jnp.zeros((half, size), BF16)
     square = jnp.dot(left[...], whole[...], preferred_element_type=F32)
-    finish(dims, reach_ref, flag_ref, square, 0, 0, copies, jobs, held, out_ref, out_sems)
+    sign = jnp.where(lax.axis_index("row") == 0, 0.0, jnp.where(flag_ref[0] == 1, 1.0, -1.0))
+    finish(dims, reach_ref, sign, square, 0, 0, copies, jobs, held, out_ref, out_sems)
 
 
 def add_below(dims, reach_ref, flag_ref, mine_ref, other_ref, sent_ref, base_ref, out_ref, whole, left, held, in_sems, out_sems):
@@ -264,14 +270,18 @@
         if d:
             whole[block(k + d), block(k)] = whole[block(k), block(k + d)].T
     square = jnp.dot(left[...], whole[...], preferred_element_type=F32)
-    finish(dims, reach_ref, flag_ref, square, rows - width, rows, copies, jobs, held, out_ref, out_sems)
+    sign = jnp.where(flag_ref[0] == 1, 1.0, -1.0)
+    finish(dims, reach_ref, sign, square, rows - width, rows, copies, jobs, held, out_ref, out_sems)
 
 
 def halo_kernel(
-    dims, above_parity, reach_ref, flag_ref, mine_ref, other_ref, sent_ref, trace_ref, base_ref, out_ref, sum_ref,
+    dims, above_parity, reach_ref, flag_ref, mine_ref, other_ref, sent_ref, trace_ref, got_ref, base_ref, out_ref, sum_ref,
     whole, turned, left, held, sems,
 ):
-    total = jnp.sum(trace_ref[...])
+    total = jnp.sum(trace_ref[...] + got_ref[...])
+    if above_parity == 0:
+        last = mine_ref.shape[0] - 1
+        total = total + jnp.sum(mine_ref[last].astype(F32) + other_ref[last].astype(F32))
     sum_ref[0] = total / (lax.axis_size("row") * dims[0] * dims[3])
     parity = lax.axis_index("row") % 2
 
@@ -295,21 +305,20 @@
     halo = len(head_blocks(width))
     count = lax.axis_size("row")
     near_pairs = [(i, i ^ 1) for i in range(count)]
-    far_pairs = [(i, j) for i in range(count) for j in [((i + 1) ^ 1) - 1] if 0 <= j < count]
+    far_pairs = [(i, j) for i in range(count) for j in [(((i + 1) ^ 1) - 1) % count]]
     swap = [(0, 1), (1, 0)]
     whole = jax.ShapeDtypeStruct(hamiltonian.shape, F32)
     packed = jax.ShapeDtypeStruct((halo, half, size), BF16)
 
-    current, near, far, part = pl.pallas_call(
+    current, near, part = pl.pallas_call(
         functools.partial(start_kernel, dims),
         out_shape=(
             jax.ShapeDtypeStruct(hamiltonian.shape, BF16),
             packed,
-            jax.ShapeDtypeStruct((halo + PAD, half, size), BF16),
             jax.ShapeDtypeStruct((LINES, size), F32),
         ),
         in_specs=[HBM, HBM, HBM, HBM],
-        out_specs=(VMEM, VMEM, VMEM, VMEM),
+        out_specs=(VMEM, VMEM, VMEM),
         scratch_shapes=[
             pltpu.VMEM(hamiltonian.shape, F32),
             pltpu.SMEM(block_reach.shape, jnp.int32),
@@ -318,13 +327,26 @@
             pltpu.SemaphoreType.DMA((rows,)),
             pltpu.SemaphoreType.DMA((3,)),
         ],
-        compiler_params=pltpu.CompilerParams(vmem_limit_bytes=50 * MIB),
+        compiler_params=pltpu.CompilerParams(vmem_limit_bytes=51 * MIB),
         cost_estimate=SMALL,
         name="start",
     )(block_reach, bounds, branch_flags, hamiltonian)
     swapped = lax.ppermute(current, "col", swap)
     near_mine = lax.ppermute(near, "row", near_pairs)
-    parts = lax.all_gather(part, ("row", "col"), tiled=True)
+    steps = [1 << n for n in reversed(range(1, count.bit_length() - 1))]
+    trace = part
+    for step in steps:
+        trace = trace + lax.ppermute(trace, "row", [(i, i ^ step) for i in range(count)])
+    far = pl.pallas_call(
+        functools.partial(pack_far_kernel, dims),
+        out_shape=jax.ShapeDtypeStruct((halo + 1, half, size), BF16),
+        in_specs=[VMEM, VMEM],
+        out_specs=VMEM,
+        compiler_params=pltpu.CompilerParams(vmem_limit_bytes=8 * MIB),
+        cost_estimate=SMALL,
+        name="pack_far",
+    )(current, trace)
+    got = lax.ppermute(trace, "col", swap)
     far_mine = lax.ppermute(far, "row", far_pairs)
     base = pl.pallas_call(
         functools.partial(inner_kernel, dims),
@@ -344,14 +366,14 @@
     base, near_mine = lax.optimization_barrier((base, near_mine))
     near_other = lax.ppermute(near_mine, "col", swap)
 
-    def add_halo(above_parity, mine, other, sent, trace, base):
+    def add_halo(above_parity, mine, other, sent, trace, got, base):
         square = pltpu.VMEM((width * size, width * size), BF16)
         return pl.pallas_call(
             functools.partial(halo_kernel, dims, above_parity),
             out_shape=(whole, jax.ShapeDtypeStruct((1,), F32)),
-            in_specs=[SMEM, SMEM, VMEM, VMEM, VMEM, VMEM, ANY],
+            in_specs=[SMEM, SMEM, VMEM, VMEM, VMEM, VMEM, VMEM, ANY],
             out_specs=(ANY, SMEM),
-            input_output_aliases={6: 0},
+            input_output_aliases={7: 0},
             scratch_shapes=[
                 square, square, pltpu.VMEM((width * half, width * size), BF16), pltpu.VMEM((halo, half, size), F32),
                 pltpu.SemaphoreType.DMA((2, width)),
@@ -359,12 +381,12 @@
             compiler_params=pltpu.CompilerParams(vmem_limit_bytes=16 * MIB),
             cost_estimate=SMALL,
             name="halo",
-        )(block_reach, branch_flags, mine, other, sent, trace, base)
-
-    base, _ = add_halo(1, near_mine, near_other, near, part, base)
-    base, far_mine, parts = lax.optimization_barrier((base, far_mine, parts))
+        )(block_reach, branch_flags, mine, other, sent, trace, got, base)
+
+    base = add_halo(1, near_mine, near_other, near, trace, got, base)[0]
+    base, far_mine = lax.optimization_barrier((base, far_mine))
     far_other = lax.ppermute(far_mine, "col", swap)
-    return add_halo(0, far_mine, far_other, far, parts, base)
+    return add_halo(0, far_mine, far_other, far, trace, got, base)
 
 
 def solution(mesh):

time: 54.6 us -> 36.1 us (0.66)
  blocking collectives: 22.1 us -> 0 us
  starting transfers between devices: 4.2 us -> 11.7 us
  waiting for transfers between devices: 10.6 us -> 6.74 us
    all_gather x1 -> x0, blocking collectives: 22.1 us -> none  [per_device(): parts = lax.all_gather(part, ('row', 'col'), tiled=True)]
    ppermute x1, waiting for transfers between devices: 9.26 us -> 0.01 us  [per_device(): near_mine = lax.ppermute(near, 'row', near_pairs)]
    ppermute x0 -> x3, waiting for transfers between devices: none -> 5.19 us  [the longest x2 4.03 us: per_device(): lax.ppermute(trace, 'row', [(i, i ^ step) for i in range(count)])]
    ppermute x0 -> x3, starting transfers between devices: none -> 4.66 us  [the longest x2 4.17 us: per_device(): lax.ppermute(trace, 'row', [(i, i ^ step) for i in range(count)])]
    ppermute x1, starting transfers between devices: 0.67 us -> 3.6 us  [per_device(): far_mine = lax.ppermute(far, 'row', far_pairs)]
  transfers between devices with their start and end apart: 5 -> 8, of which waited for: 2 -> 4; matrix products, arithmetic and copies ran while one was open for 0% -> 0% of each run, Pallas kernels for 17% -> 26%
where the time goes in v8:
time: 36.1 us; the launch traced here: 35.9 us
  Pallas kernels  14.8 us (41%)
  starting transfers between devices  11.7 us (32%)
  waiting for transfers between devices  6.74 us (19%)
  between operations  1.35 us (4%)
  local copies, waits for them, and re-layouts  1.3 us (4%)
    pallas_call x2, Pallas kernels, add_halo(): pl.pallas_call(functools.partial(halo_kernel, dims, above_parity), out_sh...  6.98 us
    pallas_call x1, Pallas kernels, per_device(): pl.pallas_call(functools.partial(inner_kernel, dims), out_shape=whole, in...  5.69 us
    ppermute x2, starting transfers between devices, per_device(): lax.ppermute(trace, 'row', [(i, i ^ step) for i in range(count)])  4.17 us
    ppermute x2, waiting for transfers between devices, per_device(): lax.ppermute(trace, 'row', [(i, i ^ step) for i in range(count)])  4.03 us
    ppermute x1, starting transfers between devices, per_device(): far_mine = lax.ppermute(far, 'row', far_pairs)  3.6 us
    ppermute x1, starting transfers between devices, per_device(): near_mine = lax.ppermute(near, 'row', near_pairs)  2.6 us
    pallas_call x1, Pallas kernels, per_device(): pl.pallas_call(functools.partial(start_kernel, dims), out_shape=(jax.Shap...  2.11 us
    ppermute x1, waiting for transfers between devices, per_device(): far_other = lax.ppermute(far_mine, 'col', swap)  1.54 us
  transfers between devices with their start and end apart: 8, of which 4 were waited for; matrix products, arithmetic and copies ran while one was open for 0% of the time, Pallas kernels for 26%

profile of v8, /device:TPU:0, one launch (start us, length us, event | category | flops | bytes accessed | tf_op | source)
XLA Modules:
  0.0 35.9 jit_solution(4321968463671967383)
XLA Ops:
  1.3 0.0 copy-start
  1.3 0.6 %copy-done = s32[12]{0:T(128)S(1)} copy-done((s32[12]{0:T(128)S(1)}, s32[12]{0:T(128)}, u32[]{:S(2)}) %copy-start) | copy-done | bytes 72
  1.9 0.0 copy-start.1
  1.9 0.7 %copy-done.1 = f32[2]{0:T(128)S(1)} copy-done((f32[2]{0:T(128)S(1)}, f32[2]{0:T(128)}, u32[]{:S(2)}) %copy-start.1) | copy-done | bytes 32
  2.6 2.1 %start.1 = (bf16[12,7,64,128]{3,2,1,0:T(8,128)(2,1)S(1)}, bf16[21,64,128]{2,1,0:T(8,128)(2,1)S(1)}, f32[16,128]{1,0:T(8,128)S(1)}) custom-call(s32[12]{0:T(128)S(1)} %copy-done, f32[2]{0:T(128)S(1)} %copy-done.1, s32[1]{0:T(128)S(6)} %copy.10.flag_hbm.flag_ref, f32[12,7,64,128]{3,2,1,0:T(8,128)} %h_hbm.1), custom_call_target="tpu_custom_call" | custom-call | flops 1 | bytes 1 | tf_op jit(solution)/shard_map/start/pallas_call | solution.py:313
  4.7 0.5 %collective-permute-start = (bf16[12,7,64,128]{3,2,1,0:T(8,128)(2,1)S(1)}, bf16[12,7,64,128]{3,2,1,0:T(8,128)(2,1)S(1)}, u32[]{:S(2)}, u32[]{:S(2)}) collective-permute-start(bf16[12,7,64,128]{3,2,1,0:T(8,128)(2,1)S(1)} %get-tuple-element.10.mine_ref.x_ref), channel_id=1, source_target_pairs={{0,1},{1,0},{2,3},{3,2},{4,5},{5,4},{6,7},{7,6},{8,9},{9,8},{10,11... | collective-permute-start | bytes 4128776 | tf_op jit(solution)/shard_map/ppermute | solution.py:334
  5.2 2.6 %collective-permute-start.1 = (bf16[21,64,128]{2,1,0:T(8,128)(2,1)S(1)}, bf16[21,64,128]{2,1,0:T(8,128)(2,1)S(1)}, u32[]{:S(2)}, u32[]{:S(2)}) collective-permute-start(bf16[21,64,128]{2,1,0:T(8,128)(2,1)S(1)} %get-tuple-element.11.sent_ref), channel_id=1, source_target_pairs={{0,2},{2,0},{4,6},{6,4},{8,10},{10,8},{12,14},{14,12},{1,3},{3,1},... | collective-permute-start | bytes 1032200 | tf_op jit(solution)/shard_map/ppermute | solution.py:335
  7.8 2.6 %collective-permute-start.3 = (f32[16,128]{1,0:T(8,128)S(1)}, f32[16,128]{1,0:T(8,128)S(1)}, u32[]{:S(2)}, u32[]{:S(2)}) collective-permute-start(f32[16,128]{1,0:T(8,128)S(1)} %get-tuple-element.13), channel_id=1, source_target_pairs={{0,8},{2,10},{4,12},{6,14},{8,0},{10,2},{12,4},{14,6},{1,9},{3,11}... | collective-permute-start | bytes 24584 | tf_op jit(solution)/shard_map/ppermute | solution.py:339
  10.4 2.0 %collective-permute-done.3 = f32[16,128]{1,0:T(8,128)S(1)} collective-permute-done((f32[16,128]{1,0:T(8,128)S(1)}, f32[16,128]{1,0:T(8,128)S(1)}, u32[]{:S(2)}, u32[]{:S(2)}) %collective-permute-start.3) | collective-permute-done | bytes 8224 | tf_op jit(solution)/shard_map/ppermute | solution.py:339
  12.4 1.6 %collective-permute-start.4 = (f32[16,128]{1,0:T(8,128)S(1)}, f32[16,128]{1,0:T(8,128)S(1)}, u32[]{:S(2)}, u32[]{:S(2)}) collective-permute-start(f32[16,128]{1,0:T(8,128)S(1)} %add.6), channel_id=1, source_target_pairs={{0,4},{2,6},{4,0},{6,2},{8,12},{10,14},{12,8},{14,10},{1,5},{3,7},... | collective-permute-start | bytes 24584 | tf_op jit(solution)/shard_map/ppermute | solution.py:339
  14.0 2.1 %collective-permute-done.4 = f32[16,128]{1,0:T(8,128)S(1)} collective-permute-done((f32[16,128]{1,0:T(8,128)S(1)}, f32[16,128]{1,0:T(8,128)S(1)}, u32[]{:S(2)}, u32[]{:S(2)}) %collective-permute-start.4) | collective-permute-done | bytes 8224 | tf_op jit(solution)/shard_map/ppermute | solution.py:339
  16.1 3.6 %collective-permute-start.6 = (bf16[22,64,128]{2,1,0:T(8,128)(2,1)S(1)}, bf16[22,64,128]{2,1,0:T(8,128)(2,1)S(1)}, u32[]{:S(2)}, u32[]{:S(2)}) collective-permute-start(bf16[22,64,128]{2,1,0:T(8,128)(2,1)S(1)} %pack_far.1.sent_ref), channel_id=1, source_target_pairs={{0,14},{2,4},{4,2},{6,8},{8,6},{10,12},{12,10},{14,0},{1,15},{3,5}... | collective-permute-start | bytes 1081352 | tf_op jit(solution)/shard_map/ppermute | solution.py:350
  19.7 0.0 collective-permute-done.other_ref
  19.7 5.7 %inner.1.base_ref = f32[12,7,64,128]{3,2,1,0:T(8,128)} custom-call(s32[12]{0:T(128)S(1)} %copy-done, s32[1]{0:T(128)S(6)} %copy.10.flag_hbm.flag_ref, bf16[12,7,64,128]{3,2,1,0:T(8,128)(2,1)S(1)} %get-tuple-element.10.mine_ref.x_ref, bf16[12,7,64,128]{3,2,1,0:T(8,128)(2,1)S(1)} %collective-permute-done.other_ref), custom_call_target="tpu_custom_call" | custom-call | flops 1 | bytes 1 | tf_op jit(solution)/shard_map/inner/pallas_call | solution.py:351
  25.4 0.0 collective-permute-done.1.mine_ref
  25.4 0.1 collective-permute-start.2
  25.5 0.5 %collective-permute-start.5 = (f32[16,128]{1,0:T(8,128)S(1)}, f32[16,128]{1,0:T(8,128)S(1)}, u32[]{:S(2)}, u32[]{:S(2)}) collective-permute-start(f32[16,128]{1,0:T(8,128)S(1)} %add.7.trace_ref.sum_ref), channel_id=1, source_target_pairs={{0,1},{1,0},{2,3},{3,2},{4,5},{5,4},{6,7},{7,6},{8,9},{9,8},{10,11... | collective-permute-start | bytes 24584 | tf_op jit(solution)/shard_map/ppermute | solution.py:349
  26.0 1.2 %collective-permute-done.5.got_ref = f32[16,128]{1,0:T(8,128)S(1)} collective-permute-done((f32[16,128]{1,0:T(8,128)S(1)}, f32[16,128]{1,0:T(8,128)S(1)}, u32[]{:S(2)}, u32[]{:S(2)}) %collective-permute-start.5) | collective-permute-done | bytes 8224 | tf_op jit(solution)/shard_map/ppermute | solution.py:349
  27.1 0.0 collective-permute-done.2.other_ref
  27.1 3.5 %halo.2 = (f32[12,7,64,128]{3,2,1,0:T(8,128)}, f32[1]{0:T(128)}) custom-call(s32[12]{0:T(128)S(1)} %copy-done, s32[1]{0:T(128)S(6)} %copy.10.flag_hbm.flag_ref, bf16[21,64,128]{2,1,0:T(8,128)(2,1)S(1)} %collective-permute-done.1.mine_ref, bf16[21,64,128]{2,1,0:T(8,128)(2,1)S(1)} %collective-permute-done.2.other_ref, ...), custom_call_target="tpu_custom_call", output_to_operand_aliasing={{0}: (7, {})} | custom-call | flops 1 | bytes 1 | tf_op jit(solution)/shard_map/halo/pallas_call | solution.py:371
  30.6 0.0 collective-permute-done.6.mine_ref
  30.6 0.2 collective-permute-start.7
  30.8 1.5 %collective-permute-done.7.other_ref = bf16[22,64,128]{2,1,0:T(8,128)(2,1)S(1)} collective-permute-done((bf16[22,64,128]{2,1,0:T(8,128)(2,1)S(1)}, bf16[22,64,128]{2,1,0:T(8,128)(2,1)S(1)}, u32[]{:S(2)}, u32[]{:S(2)}) %collective-permute-start.7) | collective-permute-done | bytes 360480 | tf_op jit(solution)/shard_map/ppermute | solution.py:388
  32.4 3.5 %halo.3 = (f32[12,7,64,128]{3,2,1,0:T(8,128)}, f32[1]{0:T(128)}) custom-call(s32[12]{0:T(128)S(1)} %copy-done, s32[1]{0:T(128)S(6)} %copy.10.flag_hbm.flag_ref, bf16[22,64,128]{2,1,0:T(8,128)(2,1)S(1)} %collective-permute-done.6.mine_ref, bf16[22,64,128]{2,1,0:T(8,128)(2,1)S(1)} %collective-permute-done.7.other_ref, ...), custom_call_target="tpu_custom_call", output_to_operand_aliasing={{0}: (7, {})} | custom-call | flops 1 | bytes 1 | tf_op jit(solution)/shard_map/halo/pallas_call | solution.py:371
  (3 shorter events, 0.0 us)
Async XLA Ops:
  1.3 0.7 %copy-start = (s32[12]{0:T(128)S(1)}, s32[12]{0:T(128)}, u32[]{:S(2)}) copy-start(s32[12]{0:T(128)} %reach_ref.5) | copy-start | bytes 148
  1.9 0.7 %copy-start.1 = (f32[2]{0:T(128)S(1)}, f32[2]{0:T(128)}, u32[]{:S(2)}) copy-start(f32[2]{0:T(128)} %bounds_hbm.1) | copy-start | bytes 28
  4.7 15.0 %collective-permute-start = (bf16[12,7,64,128]{3,2,1,0:T(8,128)(2,1)S(1)}, bf16[12,7,64,128]{3,2,1,0:T(8,128)(2,1)S(1)}, u32[]{:S(2)}, u32[]{:S(2)}) collective-permute-start(bf16[12,7,64,128]{3,2,1,0:T(8,128)(2,1)S(1)} %get-tuple-element.10.mine_ref.x_ref), channel_id=1, source_target_pairs={{0,1},{1,0},{2,3},{3,2},{4,5},{5,4},{6,7},{7,6},{8,9},{9,8},{10,11... | collective-permute-start | bytes 4128776 | tf_op jit(solution)/shard_map/ppermute | solution.py:334
  5.2 20.2 %collective-permute-start.1 = (bf16[21,64,128]{2,1,0:T(8,128)(2,1)S(1)}, bf16[21,64,128]{2,1,0:T(8,128)(2,1)S(1)}, u32[]{:S(2)}, u32[]{:S(2)}) collective-permute-start(bf16[21,64,128]{2,1,0:T(8,128)(2,1)S(1)} %get-tuple-element.11.sent_ref), channel_id=1, source_target_pairs={{0,2},{2,0},{4,6},{6,4},{8,10},{10,8},{12,14},{14,12},{1,3},{3,1},... | collective-permute-start | bytes 1032200 | tf_op jit(solution)/shard_map/ppermute | solution.py:335
  7.8 4.5 %collective-permute-start.3 = (f32[16,128]{1,0:T(8,128)S(1)}, f32[16,128]{1,0:T(8,128)S(1)}, u32[]{:S(2)}, u32[]{:S(2)}) collective-permute-start(f32[16,128]{1,0:T(8,128)S(1)} %get-tuple-element.13), channel_id=1, source_target_pairs={{0,8},{2,10},{4,12},{6,14},{8,0},{10,2},{12,4},{14,6},{1,9},{3,11}... | collective-permute-start | bytes 24584 | tf_op jit(solution)/shard_map/ppermute | solution.py:339
  12.4 3.7 %collective-permute-start.4 = (f32[16,128]{1,0:T(8,128)S(1)}, f32[16,128]{1,0:T(8,128)S(1)}, u32[]{:S(2)}, u32[]{:S(2)}) collective-permute-start(f32[16,128]{1,0:T(8,128)S(1)} %add.6), channel_id=1, source_target_pairs={{0,4},{2,6},{4,0},{6,2},{8,12},{10,14},{12,8},{14,10},{1,5},{3,7},... | collective-permute-start | bytes 24584 | tf_op jit(solution)/shard_map/ppermute | solution.py:339
  16.1 14.6 %collective-permute-start.6 = (bf16[22,64,128]{2,1,0:T(8,128)(2,1)S(1)}, bf16[22,64,128]{2,1,0:T(8,128)(2,1)S(1)}, u32[]{:S(2)}, u32[]{:S(2)}) collective-permute-start(bf16[22,64,128]{2,1,0:T(8,128)(2,1)S(1)} %pack_far.1.sent_ref), channel_id=1, source_target_pairs={{0,14},{2,4},{4,2},{6,8},{8,6},{10,12},{12,10},{14,0},{1,15},{3,5}... | collective-permute-start | bytes 1081352 | tf_op jit(solution)/shard_map/ppermute | solution.py:350
  25.4 1.7 %collective-permute-start.2 = (bf16[21,64,128]{2,1,0:T(8,128)(2,1)S(1)}, bf16[21,64,128]{2,1,0:T(8,128)(2,1)S(1)}, u32[]{:S(2)}, u32[]{:S(2)}) collective-permute-start(bf16[21,64,128]{2,1,0:T(8,128)(2,1)S(1)} %collective-permute-done.1.mine_ref), channel_id=1, source_target_pairs={{0,1},{1,0},{2,3},{3,2},{4,5},{5,4},{6,7},{7,6},{8,9},{9,8},{10,11... | collective-permute-start | bytes 1032200 | tf_op jit(solution)/shard_map/ppermute | solution.py:367
  25.5 1.7 %collective-permute-start.5 = (f32[16,128]{1,0:T(8,128)S(1)}, f32[16,128]{1,0:T(8,128)S(1)}, u32[]{:S(2)}, u32[]{:S(2)}) collective-permute-start(f32[16,128]{1,0:T(8,128)S(1)} %add.7.trace_ref.sum_ref), channel_id=1, source_target_pairs={{0,1},{1,0},{2,3},{3,2},{4,5},{5,4},{6,7},{7,6},{8,9},{9,8},{10,11... | collective-permute-start | bytes 24584 | tf_op jit(solution)/shard_map/ppermute | solution.py:349
  30.6 1.7 %collective-permute-start.7 = (bf16[22,64,128]{2,1,0:T(8,128)(2,1)S(1)}, bf16[22,64,128]{2,1,0:T(8,128)(2,1)S(1)}, u32[]{:S(2)}, u32[]{:S(2)}) collective-permute-start(bf16[22,64,128]{2,1,0:T(8,128)(2,1)S(1)} %collective-permute-done.6.mine_ref), channel_id=1, source_target_pairs={{0,1},{1,0},{2,3},{3,2},{4,5},{5,4},{6,7},{7,6},{8,9},{9,8},{10,11... | collective-permute-start | bytes 1081352 | tf_op jit(solution)/shard_map/ppermute | solution.py:388

commit v9 on v8

--- a/solution.py
+++ b/solution.py
@@ -193,7 +193,7 @@
     return copies
 
 
-def finish(dims, reach_ref, sign, square, from_row, from_col, copies, jobs, held, out_ref, sems):
+def finish(dims, reach_ref, sign, squares, from_row, from_col, from_pair, copies, jobs, held, out_ref, sems):
     rows, width, half, size = dims
     first_row = lax.axis_index("row") * rows
     total_rows = lax.axis_size("row") * rows
@@ -203,7 +203,9 @@
         for e in range(count):
             i, j = row - from_row, row + d + e - from_col
             kept = is_kept(reach_ref, row, d + e, first_row, total_rows)
-            part = square[i * half : (i + 1) * half, j * size : (j + 1) * size]
+            pair = j - j % 2
+            i, j = i - pair * from_pair, j - pair
+            part = squares[pair][i * half : (i + 1) * half, j * size : (j + 1) * size]
             held[at + e] = held[at + e] + part * jnp.where(kept, sign, 0.0)
         copy = pltpu.make_async_copy(held.at[pl.ds(at, count)], out_ref.at[row, pl.ds(d, count)], sems.at[n])
         copy.start()
@@ -238,12 +240,19 @@
             if (k, j) in have:
                 turned[block(j), block(k)] = whole[block(k), block(j)].T
                 left[pl.ds(j * half, half), block(k)] = turned[pl.ds(j * size + mine, half), block(k)]
-            else:
+            elif k >= j - j % 2:
                 whole[block(k), block(j)] = jnp.zeros((size, size), BF16)
                 left[pl.ds(j * half, half), block(k)] = jnp.zeros((half, size), BF16)
-    square = jnp.dot(left[...], whole[...], preferred_element_type=F32)
+    squares = {}
+    for j in range(0, width, 2):
+        depth, cols = pl.ds(j * size, (width - j) * size), min(2, width - j)
+        squares[j] = jnp.dot(
+            left[pl.ds(0, (j + cols) * half), depth],
+            whole[depth, pl.ds(j * size, cols * size)],
+            preferred_element_type=F32,
+        )
     sign = jnp.where(lax.axis_index("row") == 0, 0.0, jnp.where(flag_ref[0] == 1, 1.0, -1.0))
-    finish(dims, reach_ref, sign, square, 0, 0, copies, jobs, held, out_ref, out_sems)
+    finish(dims, reach_ref, sign, squares, 0, 0, False, copies, jobs, held, out_ref, out_sems)
 
 
 def add_below(dims, reach_ref, flag_ref, mine_ref, other_ref, sent_ref, base_ref, out_ref, whole, left, held, in_sems, out_sems):
@@ -269,9 +278,16 @@
         whole[pl.ds(k * size + other, half), block(k + d)] = other_ref[n]
         if d:
             whole[block(k + d), block(k)] = whole[block(k), block(k + d)].T
-    square = jnp.dot(left[...], whole[...], preferred_element_type=F32)
+    squares = {}
+    for j in range(0, width, 2):
+        cols = min(2, width - j)
+        squares[j] = jnp.dot(
+            left[pl.ds(j * half, (width - j) * half), :],
+            whole[:, pl.ds(j * size, cols * size)],
+            preferred_element_type=F32,
+        )
     sign = jnp.where(flag_ref[0] == 1, 1.0, -1.0)
-    finish(dims, reach_ref, sign, square, rows - width, rows, copies, jobs, held, out_ref, out_sems)
+    finish(dims, reach_ref, sign, squares, rows - width, rows, True, copies, jobs, held, out_ref, out_sems)
 
 
 def halo_kernel(
@@ -348,6 +364,7 @@
     )(current, trace)
     got = lax.ppermute(trace, "col", swap)
     far_mine = lax.ppermute(far, "row", far_pairs)
+    swapped, near_mine = lax.optimization_barrier((swapped, near_mine))
     base = pl.pallas_call(
         functools.partial(inner_kernel, dims),
         out_shape=whole,
@@ -363,7 +380,6 @@
         cost_estimate=SMALL,
         name="inner",
     )(block_reach, branch_flags, current, swapped)
-    base, near_mine = lax.optimization_barrier((base, near_mine))
     near_other = lax.ppermute(near_mine, "col", swap)
 
     def add_halo(above_parity, mine, other, sent, trace, got, base):

time: 36.1 us -> 34.9 us (0.967)
  waiting for transfers between devices: 6.74 us -> 5.6 us
    ppermute x1, waiting for transfers between devices: 1.15 us -> 0.01 us  [per_device(): got = lax.ppermute(trace, 'col', swap)]
  transfers between devices with their start and end apart: 8 -> 8, of which waited for: 4 -> 3; matrix products, arithmetic and copies ran while one was open for 0% -> 0% of each run, Pallas kernels for 26% -> 27%
where the time goes in v9:
time: 34.9 us; the launch traced here: 34.7 us
  Pallas kernels  14.9 us (43%)
  starting transfers between devices  11.6 us (33%)
  waiting for transfers between devices  5.6 us (16%)
  between operations  1.35 us (4%)
  local copies, waits for them, and re-layouts  1.3 us (4%)
    pallas_call x2, Pallas kernels, add_halo(): pl.pallas_call(functools.partial(halo_kernel, dims, above_parity), out_sh...  7.03 us
    pallas_call x1, Pallas kernels, per_device(): pl.pallas_call(functools.partial(inner_kernel, dims), out_shape=whole, in...  5.69 us
    ppermute x2, starting transfers between devices, per_device(): lax.ppermute(trace, 'row', [(i, i ^ step) for i in range(count)])  4.17 us
    ppermute x2, waiting for transfers between devices, per_device(): lax.ppermute(trace, 'row', [(i, i ^ step) for i in range(count)])  4.03 us
    ppermute x1, starting transfers between devices, per_device(): far_mine = lax.ppermute(far, 'row', far_pairs)  3.6 us
    ppermute x1, starting transfers between devices, per_device(): near_mine = lax.ppermute(near, 'row', near_pairs)  2.6 us
    pallas_call x1, Pallas kernels, per_device(): pl.pallas_call(functools.partial(start_kernel, dims), out_shape=(jax.Shap...  2.11 us
    ppermute x1, waiting for transfers between devices, per_device(): far_other = lax.ppermute(far_mine, 'col', swap)  1.56 us
  transfers between devices with their start and end apart: 8, of which 3 were waited for; matrix products, arithmetic and copies ran while one was open for 0% of the time, Pallas kernels for 27%

profile of v9, /device:TPU:0, one launch (start us, length us, event | category | flops | bytes accessed | tf_op | source)
XLA Modules:
  0.0 34.7 jit_solution(2501917809526239959)
XLA Ops:
  1.3 0.0 copy-start
  1.3 0.6 %copy-done = s32[12]{0:T(128)S(1)} copy-done((s32[12]{0:T(128)S(1)}, s32[12]{0:T(128)}, u32[]{:S(2)}) %copy-start) | copy-done | bytes 72
  1.9 0.0 copy-start.1
  1.9 0.7 %copy-done.1 = f32[2]{0:T(128)S(1)} copy-done((f32[2]{0:T(128)S(1)}, f32[2]{0:T(128)}, u32[]{:S(2)}) %copy-start.1) | copy-done | bytes 32
  2.6 2.1 %start.1 = (bf16[12,7,64,128]{3,2,1,0:T(8,128)(2,1)S(1)}, bf16[21,64,128]{2,1,0:T(8,128)(2,1)S(1)}, f32[16,128]{1,0:T(8,128)S(1)}) custom-call(s32[12]{0:T(128)S(1)} %copy-done, f32[2]{0:T(128)S(1)} %copy-done.1, s32[1]{0:T(128)S(6)} %copy.10.flag_hbm.flag_ref, f32[12,7,64,128]{3,2,1,0:T(8,128)} %h_hbm.1), custom_call_target="tpu_custom_call" | custom-call | flops 1 | bytes 1 | tf_op jit(solution)/shard_map/start/pallas_call | solution.py:329
  4.7 0.5 %collective-permute-start = (bf16[12,7,64,128]{3,2,1,0:T(8,128)(2,1)S(1)}, bf16[12,7,64,128]{3,2,1,0:T(8,128)(2,1)S(1)}, u32[]{:S(2)}, u32[]{:S(2)}) collective-permute-start(bf16[12,7,64,128]{3,2,1,0:T(8,128)(2,1)S(1)} %get-tuple-element.10.mine_ref.x_ref), channel_id=1, source_target_pairs={{0,1},{1,0},{2,3},{3,2},{4,5},{5,4},{6,7},{7,6},{8,9},{9,8},{10,11... | collective-permute-start | bytes 4128776 | tf_op jit(solution)/shard_map/ppermute | solution.py:350
  5.2 2.6 %collective-permute-start.1 = (bf16[21,64,128]{2,1,0:T(8,128)(2,1)S(1)}, bf16[21,64,128]{2,1,0:T(8,128)(2,1)S(1)}, u32[]{:S(2)}, u32[]{:S(2)}) collective-permute-start(bf16[21,64,128]{2,1,0:T(8,128)(2,1)S(1)} %get-tuple-element.11.sent_ref), channel_id=1, source_target_pairs={{0,2},{2,0},{4,6},{6,4},{8,10},{10,8},{12,14},{14,12},{1,3},{3,1},... | collective-permute-start | bytes 1032200 | tf_op jit(solution)/shard_map/ppermute | solution.py:351
  7.8 2.6 %collective-permute-start.3 = (f32[16,128]{1,0:T(8,128)S(1)}, f32[16,128]{1,0:T(8,128)S(1)}, u32[]{:S(2)}, u32[]{:S(2)}) collective-permute-start(f32[16,128]{1,0:T(8,128)S(1)} %get-tuple-element.13), channel_id=1, source_target_pairs={{0,8},{2,10},{4,12},{6,14},{8,0},{10,2},{12,4},{14,6},{1,9},{3,11}... | collective-permute-start | bytes 24584 | tf_op jit(solution)/shard_map/ppermute | solution.py:355
  10.4 2.0 %collective-permute-done.3 = f32[16,128]{1,0:T(8,128)S(1)} collective-permute-done((f32[16,128]{1,0:T(8,128)S(1)}, f32[16,128]{1,0:T(8,128)S(1)}, u32[]{:S(2)}, u32[]{:S(2)}) %collective-permute-start.3) | collective-permute-done | bytes 8224 | tf_op jit(solution)/shard_map/ppermute | solution.py:355
  12.4 1.6 %collective-permute-start.4 = (f32[16,128]{1,0:T(8,128)S(1)}, f32[16,128]{1,0:T(8,128)S(1)}, u32[]{:S(2)}, u32[]{:S(2)}) collective-permute-start(f32[16,128]{1,0:T(8,128)S(1)} %add.6), channel_id=1, source_target_pairs={{0,4},{2,6},{4,0},{6,2},{8,12},{10,14},{12,8},{14,10},{1,5},{3,7},... | collective-permute-start | bytes 24584 | tf_op jit(solution)/shard_map/ppermute | solution.py:355
  14.0 2.1 %collective-permute-done.4 = f32[16,128]{1,0:T(8,128)S(1)} collective-permute-done((f32[16,128]{1,0:T(8,128)S(1)}, f32[16,128]{1,0:T(8,128)S(1)}, u32[]{:S(2)}, u32[]{:S(2)}) %collective-permute-start.4) | collective-permute-done | bytes 8224 | tf_op jit(solution)/shard_map/ppermute | solution.py:355
  16.1 3.6 %collective-permute-start.6 = (bf16[22,64,128]{2,1,0:T(8,128)(2,1)S(1)}, bf16[22,64,128]{2,1,0:T(8,128)(2,1)S(1)}, u32[]{:S(2)}, u32[]{:S(2)}) collective-permute-start(bf16[22,64,128]{2,1,0:T(8,128)(2,1)S(1)} %pack_far.1.sent_ref), channel_id=1, source_target_pairs={{0,14},{2,4},{4,2},{6,8},{8,6},{10,12},{12,10},{14,0},{1,15},{3,5}... | collective-permute-start | bytes 1081352 | tf_op jit(solution)/shard_map/ppermute | solution.py:366
  19.7 0.0 collective-permute-done.1.mine_ref
  19.7 0.0 collective-permute-done.other_ref
  19.7 0.0 collective-permute-start.2
  19.7 0.5 %collective-permute-start.5 = (f32[16,128]{1,0:T(8,128)S(1)}, f32[16,128]{1,0:T(8,128)S(1)}, u32[]{:S(2)}, u32[]{:S(2)}) collective-permute-start(f32[16,128]{1,0:T(8,128)S(1)} %add.7.trace_ref.sum_ref), channel_id=1, source_target_pairs={{0,1},{1,0},{2,3},{3,2},{4,5},{5,4},{6,7},{7,6},{8,9},{9,8},{10,11... | collective-permute-start | bytes 24584 | tf_op jit(solution)/shard_map/ppermute | solution.py:365
  20.2 5.7 %inner.1.base_ref = f32[12,7,64,128]{3,2,1,0:T(8,128)} custom-call(s32[12]{0:T(128)S(1)} %copy-done, s32[1]{0:T(128)S(6)} %copy.10.flag_hbm.flag_ref, bf16[12,7,64,128]{3,2,1,0:T(8,128)(2,1)S(1)} %get-tuple-element.10.mine_ref.x_ref, bf16[12,7,64,128]{3,2,1,0:T(8,128)(2,1)S(1)} %collective-permute-done.other_ref), custom_call_target="tpu_custom_call" | custom-call | flops 1 | bytes 1 | tf_op jit(solution)/shard_map/inner/pallas_call | solution.py:368
  25.9 0.0 collective-permute-done.5.got_ref
  25.9 0.0 collective-permute-done.2.other_ref
  25.9 3.6 %halo.2 = (f32[12,7,64,128]{3,2,1,0:T(8,128)}, f32[1]{0:T(128)}) custom-call(s32[12]{0:T(128)S(1)} %copy-done, s32[1]{0:T(128)S(6)} %copy.10.flag_hbm.flag_ref, bf16[21,64,128]{2,1,0:T(8,128)(2,1)S(1)} %collective-permute-done.1.mine_ref, bf16[21,64,128]{2,1,0:T(8,128)(2,1)S(1)} %collective-permute-done.2.other_ref, ...), custom_call_target="tpu_custom_call", output_to_operand_aliasing={{0}: (7, {})} | custom-call | flops 1 | bytes 1 | tf_op jit(solution)/shard_map/halo/pallas_call | solution.py:387
  29.5 0.0 collective-permute-done.6.mine_ref
  29.6 0.2 collective-permute-start.7
  29.7 1.6 %collective-permute-done.7.other_ref = bf16[22,64,128]{2,1,0:T(8,128)(2,1)S(1)} collective-permute-done((bf16[22,64,128]{2,1,0:T(8,128)(2,1)S(1)}, bf16[22,64,128]{2,1,0:T(8,128)(2,1)S(1)}, u32[]{:S(2)}, u32[]{:S(2)}) %collective-permute-start.7) | collective-permute-done | bytes 360480 | tf_op jit(solution)/shard_map/ppermute | solution.py:404
  31.3 3.4 %halo.3 = (f32[12,7,64,128]{3,2,1,0:T(8,128)}, f32[1]{0:T(128)}) custom-call(s32[12]{0:T(128)S(1)} %copy-done, s32[1]{0:T(128)S(6)} %copy.10.flag_hbm.flag_ref, bf16[22,64,128]{2,1,0:T(8,128)(2,1)S(1)} %collective-permute-done.6.mine_ref, bf16[22,64,128]{2,1,0:T(8,128)(2,1)S(1)} %collective-permute-done.7.other_ref, ...), custom_call_target="tpu_custom_call", output_to_operand_aliasing={{0}: (7, {})} | custom-call | flops 1 | bytes 1 | tf_op jit(solution)/shard_map/halo/pallas_call | solution.py:387
  (3 shorter events, 0.0 us)
Async XLA Ops:
  1.3 0.7 %copy-start = (s32[12]{0:T(128)S(1)}, s32[12]{0:T(128)}, u32[]{:S(2)}) copy-start(s32[12]{0:T(128)} %reach_ref.5) | copy-start | bytes 148
  1.9 0.7 %copy-start.1 = (f32[2]{0:T(128)S(1)}, f32[2]{0:T(128)}, u32[]{:S(2)}) copy-start(f32[2]{0:T(128)} %bounds_hbm.1) | copy-start | bytes 28
  4.7 15.0 %collective-permute-start = (bf16[12,7,64,128]{3,2,1,0:T(8,128)(2,1)S(1)}, bf16[12,7,64,128]{3,2,1,0:T(8,128)(2,1)S(1)}, u32[]{:S(2)}, u32[]{:S(2)}) collective-permute-start(bf16[12,7,64,128]{3,2,1,0:T(8,128)(2,1)S(1)} %get-tuple-element.10.mine_ref.x_ref), channel_id=1, source_target_pairs={{0,1},{1,0},{2,3},{3,2},{4,5},{5,4},{6,7},{7,6},{8,9},{9,8},{10,11... | collective-permute-start | bytes 4128776 | tf_op jit(solution)/shard_map/ppermute | solution.py:350
  5.2 14.4 %collective-permute-start.1 = (bf16[21,64,128]{2,1,0:T(8,128)(2,1)S(1)}, bf16[21,64,128]{2,1,0:T(8,128)(2,1)S(1)}, u32[]{:S(2)}, u32[]{:S(2)}) collective-permute-start(bf16[21,64,128]{2,1,0:T(8,128)(2,1)S(1)} %get-tuple-element.11.sent_ref), channel_id=1, source_target_pairs={{0,2},{2,0},{4,6},{6,4},{8,10},{10,8},{12,14},{14,12},{1,3},{3,1},... | collective-permute-start | bytes 1032200 | tf_op jit(solution)/shard_map/ppermute | solution.py:351
  7.8 4.5 %collective-permute-start.3 = (f32[16,128]{1,0:T(8,128)S(1)}, f32[16,128]{1,0:T(8,128)S(1)}, u32[]{:S(2)}, u32[]{:S(2)}) collective-permute-start(f32[16,128]{1,0:T(8,128)S(1)} %get-tuple-element.13), channel_id=1, source_target_pairs={{0,8},{2,10},{4,12},{6,14},{8,0},{10,2},{12,4},{14,6},{1,9},{3,11}... | collective-permute-start | bytes 24584 | tf_op jit(solution)/shard_map/ppermute | solution.py:355
  12.4 3.7 %collective-permute-start.4 = (f32[16,128]{1,0:T(8,128)S(1)}, f32[16,128]{1,0:T(8,128)S(1)}, u32[]{:S(2)}, u32[]{:S(2)}) collective-permute-start(f32[16,128]{1,0:T(8,128)S(1)} %add.6), channel_id=1, source_target_pairs={{0,4},{2,6},{4,0},{6,2},{8,12},{10,14},{12,8},{14,10},{1,5},{3,7},... | collective-permute-start | bytes 24584 | tf_op jit(solution)/shard_map/ppermute | solution.py:355
  16.1 13.5 %collective-permute-start.6 = (bf16[22,64,128]{2,1,0:T(8,128)(2,1)S(1)}, bf16[22,64,128]{2,1,0:T(8,128)(2,1)S(1)}, u32[]{:S(2)}, u32[]{:S(2)}) collective-permute-start(bf16[22,64,128]{2,1,0:T(8,128)(2,1)S(1)} %pack_far.1.sent_ref), channel_id=1, source_target_pairs={{0,14},{2,4},{4,2},{6,8},{8,6},{10,12},{12,10},{14,0},{1,15},{3,5}... | collective-permute-start | bytes 1081352 | tf_op jit(solution)/shard_map/ppermute | solution.py:366
  19.7 6.2 %collective-permute-start.2 = (bf16[21,64,128]{2,1,0:T(8,128)(2,1)S(1)}, bf16[21,64,128]{2,1,0:T(8,128)(2,1)S(1)}, u32[]{:S(2)}, u32[]{:S(2)}) collective-permute-start(bf16[21,64,128]{2,1,0:T(8,128)(2,1)S(1)} %collective-permute-done.1.mine_ref), channel_id=1, source_target_pairs={{0,1},{1,0},{2,3},{3,2},{4,5},{5,4},{6,7},{7,6},{8,9},{9,8},{10,11... | collective-permute-start | bytes 1032200 | tf_op jit(solution)/shard_map/ppermute | solution.py:383
  19.7 6.2 %collective-permute-start.5 = (f32[16,128]{1,0:T(8,128)S(1)}, f32[16,128]{1,0:T(8,128)S(1)}, u32[]{:S(2)}, u32[]{:S(2)}) collective-permute-start(f32[16,128]{1,0:T(8,128)S(1)} %add.7.trace_ref.sum_ref), channel_id=1, source_target_pairs={{0,1},{1,0},{2,3},{3,2},{4,5},{5,4},{6,7},{7,6},{8,9},{9,8},{10,11... | collective-permute-start | bytes 24584 | tf_op jit(solution)/shard_map/ppermute | solution.py:365
  29.6 1.7 %collective-permute-start.7 = (bf16[22,64,128]{2,1,0:T(8,128)(2,1)S(1)}, bf16[22,64,128]{2,1,0:T(8,128)(2,1)S(1)}, u32[]{:S(2)}, u32[]{:S(2)}) collective-permute-start(bf16[22,64,128]{2,1,0:T(8,128)(2,1)S(1)} %collective-permute-done.6.mine_ref), channel_id=1, source_target_pairs={{0,1},{1,0},{2,3},{3,2},{4,5},{5,4},{6,7},{7,6},{8,9},{9,8},{10,11... | collective-permute-start | bytes 1081352 | tf_op jit(solution)/shard_map/ppermute | solution.py:404
